TPU v7x, 32 devices: a whole 2x2x4 slice. The times are simulated.
32 devices in a mesh: batch: 16 (over z, x, core), seq: 2 (over y).
Axes of the slice: x: 2, y: 2, z: 4, core: 2. Of those that a mesh axis runs over, the one named last changes fastest.
Arguments:
- tokens: bfloat16 [16, 512, 768], P('batch', 'seq'), may hold values from -6 to 6
- segment_ids: int32 [16, 512], P('batch'), may hold values from 0 to 32, as said below
- w_query: bfloat16 [768, 768], replicated, may hold values from -0.21875 to 0.21875
- b_query: float32 [768], replicated, may hold values from -3 to 3
- w_key: bfloat16 [768, 768], replicated, may hold values from -0.21875 to 0.21875
- w_value: bfloat16 [768, 768], replicated, may hold values from -0.21875 to 0.21875
- b_value: float32 [768], replicated, may hold values from -3 to 3
- w_out: bfloat16 [768, 768], replicated, may hold values from -2 to 2
- b_out: float32 [768], replicated, may hold values from -3 to 3
- gain_attn: float32 [768], replicated, may hold values from 0.5 to 1.5
- shift_attn: float32 [768], replicated, may hold values from -2 to 2
- w_up: bfloat16 [768, 3072], replicated, may hold values from -0.21875 to 0.21875
- b_up: float32 [3072], replicated, may hold values from -3 to 3
- w_down: bfloat16 [3072, 768], replicated, may hold values from -0.109375 to 0.109375
- b_down: float32 [768], replicated, may hold values from -3 to 3
- gain_ffn: float32 [768], replicated, may hold values from 0.5 to 1.5
- shift_ffn: float32 [768], replicated, may hold values from -2 to 2
- w_head: bfloat16 [768], replicated, may hold values from -0.21875 to 0.21875
- cot_out: bfloat16 [16, 512, 768], P('batch', 'seq'), may hold values from -6 to 6
- cot_weight: float32 [16, 512], P('batch', 'seq'), may hold values from -6 to 6
Outputs:
- layer_out: bfloat16 [16, 512, 768], P('batch', 'seq')
- term_weight: float32 [16, 512], P('batch', 'seq')
- grad_tokens: float32 [16, 512, 768], P('batch', 'seq')
- grad_w_query: float32 [768, 768], replicated
- grad_b_query: float32 [768], replicated
- grad_w_key: float32 [768, 768], replicated
- grad_w_value: float32 [768, 768], replicated
- grad_b_value: float32 [768], replicated
- grad_w_out: float32 [768, 768], replicated
- grad_b_out: float32 [768], replicated
- grad_gain_attn: float32 [768], replicated
- grad_shift_attn: float32 [768], replicated
- grad_w_up: float32 [768, 3072], replicated
- grad_b_up: float32 [3072], replicated
- grad_w_down: float32 [3072, 768], replicated
- grad_b_down: float32 [768], replicated
- grad_gain_ffn: float32 [768], replicated
- grad_shift_ffn: float32 [768], replicated
- grad_w_head: float32 [768], replicated
Inputs may be any that keep to these rules, and one draw needn't show every extreme that they name: `segment_ids`: in each row the ids start at 0, never fall, and rise by at most one from a position to the next; no new id begins within 64 positions of the row's middle; some row reaches the largest id.
All inputs are finite; a program needn't handle non-finite values.
Results may differ from a plain program's by a relative error of at most 0.023.
Values may be sent and summed in bfloat16 or wider, within the bound.
No kernel may reach another device: no remote copies, remote signals or barrier semaphores. Data moves between devices by JAX's collectives and lax.ppermute only.
A program may use at most 384 MiB of HBM per device.

v0:
```python
from functools import partial

import jax
import jax.numpy as jnp
from jax import lax
from jax.sharding import PartitionSpec as P

HD = 64


masked = -1e30
eps_norm = 1e-06
highest = lax.Precision.HIGHEST


def layer_norm(values, gain, shift):
    centered = values - jnp.mean(values, -1, keepdims=True)
    inverse = lax.rsqrt(jnp.mean(centered * centered, -1, keepdims=True) + eps_norm)
    return centered * inverse * gain + shift


def exact_gelu(values):
    return jax.nn.gelu(values, approximate=False)


def attend_piece(state_in, pieces, offset, queries, query_ids, segment_ids):
    run_max, run_total, run_acc = state_in
    key_block, value_block = pieces
    row_count, key_len, model_width = key_block.shape
    allowed = (query_ids[:, :, None] == segment_ids[:, None, :])[:, None]
    scores = jnp.einsum(
        "rqhd,rkhd->rhqk",
        queries,
        key_block.reshape(row_count, key_len, -1, HD),
        preferred_element_type=jnp.float32,
    ) * HD ** (-0.5)
    scores = jnp.where(allowed, scores, masked)
    new_max = jnp.maximum(run_max, jnp.max(scores, -1))
    weights = jnp.where(allowed, jnp.exp(scores - new_max[..., None]), 0.0)
    run_total = jnp.sum(weights, -1)
    gathered = jnp.einsum(
        "rhqk,rkhd->rhqd",
        weights.astype(jnp.bfloat16),
        value_block.reshape(row_count, key_len, -1, HD),
        preferred_element_type=jnp.float32,
    )
    return (new_max, run_total, gathered)


def attend_back(
    state_in, pieces, offset, queries, query_ids, segment_ids, log_total, grad_mix, delta
):
    key_block, value_block = pieces
    row_count, key_len, model_width = key_block.shape
    key_heads = key_block.reshape(row_count, key_len, -1, HD)
    value_heads = value_block.reshape(row_count, key_len, -1, HD)
    allowed = (query_ids[:, :, None] == segment_ids[:, None, :])[:, None]
    scores = jnp.einsum(
        "rqhd,rkhd->rhqk", queries, key_heads, preferred_element_type=jnp.float32
    ) * HD ** (-0.5)
    scores = jnp.where(allowed, scores, masked)
    attn_probs = jnp.where(allowed, jnp.exp(scores - log_total[..., None]), 0.0)
    grad_probs = jnp.einsum(
        "rqhd,rkhd->rhqk", grad_mix, value_heads, preferred_element_type=jnp.float32
    )
    grad_scores = (attn_probs * (grad_probs - delta[..., None])).astype(jnp.bfloat16)
    grad_query = jnp.einsum(
        "rhqk,rkhd->rqhd", grad_scores, key_heads, preferred_element_type=jnp.float32
    ) * HD ** (-0.5)
    key_part = (
        jnp.einsum("rhqk,rqhd->rkhd", grad_scores, queries, preferred_element_type=jnp.float32)
        * HD ** (-0.5)
    ).reshape(row_count, key_len, model_width)
    value_part = jnp.einsum(
        "rhqk,rqhd->rkhd",
        attn_probs.astype(jnp.bfloat16),
        grad_mix,
        preferred_element_type=jnp.float32,
    ).reshape(row_count, key_len, model_width)
    return (grad_query, key_part, value_part)


def reduce_all(flat_grads):
    device_total = lax.axis_size("batch") * lax.axis_size("seq")
    block_len = device_total * 128
    total_len = flat_grads.shape[0]
    padded_len = -(-total_len // block_len) * block_len
    padded = jnp.pad(flat_grads, (0, padded_len - total_len))
    spread_out = padded.reshape(padded_len // device_total, device_total).T
    shard_sum = lax.psum_scatter(spread_out, ("batch", "seq"), scatter_dimension=0, tiled=True)
    whole = lax.all_gather(
        shard_sum.astype(jnp.bfloat16), ("batch", "seq"), axis=0, tiled=True
    ).astype(shard_sum.dtype)
    return whole.T.reshape(-1)[:total_len]


def body(
    tokens,
    segment_ids,
    w_query,
    b_query,
    w_key,
    w_value,
    b_value,
    w_out,
    b_out,
    gain_attn,
    shift_attn,
    w_up,
    b_up,
    w_down,
    b_down,
    gain_ffn,
    shift_ffn,
    w_head,
    cot_out,
    cot_weight,
):
    row_count, local_len, model_width = tokens.shape
    head_count = model_width // HD
    full_len = segment_ids.shape[1]
    query_ids = lax.dynamic_slice_in_dim(
        segment_ids, lax.axis_index("seq") * local_len, local_len, 1
    )
    token_rows = tokens.reshape(-1, model_width)
    queries = (
        (jnp.dot(token_rows, w_query, preferred_element_type=jnp.float32) + b_query)
        .astype(jnp.bfloat16)
        .reshape(row_count, local_len, head_count, HD)
    )
    keys_low = (
        jnp.dot(token_rows, w_key, preferred_element_type=jnp.float32)
        .astype(jnp.bfloat16)
        .reshape(row_count, local_len, model_width)
    )
    values_low = (
        (jnp.dot(token_rows, w_value, preferred_element_type=jnp.float32) + b_value)
        .astype(jnp.bfloat16)
        .reshape(row_count, local_len, model_width)
    )
    start_state = (
        jnp.full((row_count, head_count, local_len), masked, jnp.float32),
        jnp.zeros((row_count, head_count, local_len), jnp.float32),
        jnp.zeros((row_count, head_count, local_len, HD), jnp.float32),
    )
    forward_step = partial(
        attend_piece, queries=queries, query_ids=query_ids, segment_ids=segment_ids
    )
    run_max, run_total, run_acc = forward_step(
        start_state,
        (
            lax.all_gather(keys_low, "seq", axis=1, tiled=True),
            lax.all_gather(values_low, "seq", axis=1, tiled=True),
        ),
        jnp.int32(0),
    )
    attended = jnp.transpose(run_acc / run_total[..., None], (0, 2, 1, 3)).reshape(-1, model_width)
    log_total = run_max + jnp.log(run_total)
    attended_low = attended.astype(jnp.bfloat16)
    attn_out = jnp.dot(attended_low, w_out, preferred_element_type=jnp.float32) + b_out
    first_norm, first_pull = jax.vjp(
        layer_norm, token_rows.astype(jnp.float32) + attn_out, gain_attn, shift_attn
    )
    first_low = first_norm.astype(jnp.bfloat16)
    upper_pre = jnp.dot(first_low, w_up, preferred_element_type=jnp.float32) + b_up
    activated, gelu_pull = jax.vjp(exact_gelu, upper_pre)
    active_low = activated.astype(jnp.bfloat16)
    down_out = jnp.dot(active_low, w_down, preferred_element_type=jnp.float32) + b_down
    second_norm, second_pull = jax.vjp(layer_norm, first_norm + down_out, gain_ffn, shift_ffn)
    head_vector = w_head.astype(jnp.float32)
    logits = jnp.dot(second_norm, head_vector, precision=highest)
    term_weight = jax.nn.softplus(logits)
    grad_logits = cot_weight.reshape(-1) * jax.nn.sigmoid(logits)
    grad_head = jnp.dot(grad_logits, second_norm, precision=highest)
    grad_second = (
        cot_out.reshape(-1, model_width).astype(jnp.float32) + grad_logits[:, None] * head_vector
    )
    grad_sum2, grad_gain2, grad_shift2 = second_pull(grad_second)
    grad_down = grad_sum2.astype(jnp.bfloat16)
    grad_w_down = jnp.einsum("tf,td->fd", active_low, grad_down, preferred_element_type=jnp.float32)
    grad_b_down = jnp.sum(grad_down.astype(jnp.float32), 0)
    grad_active = jnp.einsum("td,fd->tf", grad_down, w_down, preferred_element_type=jnp.float32)
    grad_upper = gelu_pull(grad_active)[0].astype(jnp.bfloat16)
    grad_w_up = jnp.einsum("td,tf->df", first_low, grad_upper, preferred_element_type=jnp.float32)
    grad_b_up = jnp.sum(grad_upper.astype(jnp.float32), 0)
    grad_first = grad_sum2 + jnp.einsum(
        "tf,df->td", grad_upper, w_up, preferred_element_type=jnp.float32
    )
    grad_sum1, grad_gain1, grad_shift1 = first_pull(grad_first)
    grad_attn = grad_sum1.astype(jnp.bfloat16)
    grad_w_out = jnp.einsum(
        "td,te->de", attended_low, grad_attn, preferred_element_type=jnp.float32
    )
    grad_b_out = jnp.sum(grad_attn.astype(jnp.float32), 0)
    grad_mix = jnp.einsum("te,de->td", grad_attn, w_out, preferred_element_type=jnp.float32).astype(
        jnp.bfloat16
    )
    delta = jnp.transpose(
        jnp.sum(
            (grad_mix.astype(jnp.float32) * attended).reshape(row_count, local_len, head_count, HD),
            -1,
        ),
        (0, 2, 1),
    )
    grad_mix = grad_mix.reshape(row_count, local_len, head_count, HD)
    back_state = (
        jnp.zeros((row_count, local_len, head_count, HD), jnp.float32),
        jnp.zeros((row_count, full_len, model_width), jnp.float32),
        jnp.zeros((row_count, full_len, model_width), jnp.float32),
    )
    back_step = partial(
        attend_back,
        queries=queries,
        query_ids=query_ids,
        segment_ids=segment_ids,
        log_total=log_total,
        grad_mix=grad_mix,
        delta=delta,
    )
    grad_query, key_terms, value_terms = back_step(
        back_state,
        (
            lax.all_gather(keys_low, "seq", axis=1, tiled=True),
            lax.all_gather(values_low, "seq", axis=1, tiled=True),
        ),
        jnp.int32(0),
    )
    grad_key, grad_value = (
        lax.psum_scatter(
            key_terms.astype(jnp.bfloat16), "seq", scatter_dimension=1, tiled=True
        ).astype(jnp.float32),
        lax.psum_scatter(
            value_terms.astype(jnp.bfloat16), "seq", scatter_dimension=1, tiled=True
        ).astype(jnp.float32),
    )
    grad_query = grad_query.reshape(-1, model_width).astype(jnp.bfloat16)
    grad_key = grad_key.reshape(-1, model_width).astype(jnp.bfloat16)
    grad_value = grad_value.reshape(-1, model_width).astype(jnp.bfloat16)
    grad_tokens = (
        grad_sum1
        + jnp.einsum("te,de->td", grad_query, w_query, preferred_element_type=jnp.float32)
        + jnp.einsum("te,de->td", grad_key, w_key, preferred_element_type=jnp.float32)
        + jnp.einsum("te,de->td", grad_value, w_value, preferred_element_type=jnp.float32)
    )
    grad_w_query = jnp.einsum(
        "td,te->de", token_rows, grad_query, preferred_element_type=jnp.float32
    )
    grad_b_query = jnp.sum(grad_query.astype(jnp.float32), 0)
    grad_w_key = jnp.einsum("td,te->de", token_rows, grad_key, preferred_element_type=jnp.float32)
    grad_w_value = jnp.einsum(
        "td,te->de", token_rows, grad_value, preferred_element_type=jnp.float32
    )
    grad_b_value = jnp.sum(grad_value.astype(jnp.float32), 0)
    gradients = (
        grad_w_query,
        grad_b_query,
        grad_w_key,
        grad_w_value,
        grad_b_value,
        grad_w_out,
        grad_b_out,
        grad_gain1,
        grad_shift1,
        grad_w_up,
        grad_b_up,
        grad_w_down,
        grad_b_down,
        grad_gain2,
        grad_shift2,
        grad_head,
    )
    summed = reduce_all(jnp.concatenate([grad_item.reshape(-1) for grad_item in gradients]))
    results = []
    cursor = 0
    for grad_item in gradients:
        item_size = grad_item.size
        results.append(summed[cursor : cursor + item_size].reshape(grad_item.shape))
        cursor = cursor + item_size
    return (
        second_norm.reshape(row_count, local_len, model_width).astype(jnp.bfloat16),
        term_weight.reshape(row_count, local_len),
        grad_tokens.reshape(row_count, local_len, model_width),
    ) + tuple(results)


def solution(mesh):
    in_specs = (
        P("batch", "seq", None),
        P("batch", None),
        P(),
        P(),
        P(),
        P(),
        P(),
        P(),
        P(),
        P(),
        P(),
        P(),
        P(),
        P(),
        P(),
        P(),
        P(),
        P(),
        P("batch", "seq", None),
        P("batch", "seq"),
    )
    out_specs = (
        P("batch", "seq", None),
        P("batch", "seq"),
        P("batch", "seq", None),
        P(),
        P(),
        P(),
        P(),
        P(),
        P(),
        P(),
        P(),
        P(),
        P(),
        P(),
        P(),
        P(),
        P(),
        P(),
        P(),
    )
    return jax.shard_map(body, mesh=mesh, in_specs=in_specs, out_specs=out_specs, check_vma=False)
```

profile of v0, /device:TPU:0, one launch (start us, length us, event | category | flops | bytes accessed | tf_op | source)
XLA Modules:
  0.0 2699.4 jit_solution(6134204606907488328)
XLA Ops:
  11.8 13.0 all-gather.1
  29.5 11.1 all-gather
  50.1 10.3 multiply_convert_fusion.1
  86.7 5.7 fusion.17
  116.5 5.9 copy.101
  122.5 5.2 fusion.74
  127.7 10.7 reshape.397
  158.9 20.2 dynamic-update-slice.2
  179.1 21.3 dynamic-update-slice.3
  201.9 20.2 dynamic-update-slice.5
  226.0 80.6 %dynamic-update-slice.9 = f32[7087872]{0:T(1024)} dynamic-update-slice(f32[7087872]{0:T(1024)} %constant_dynamic-update-slice_fusion.5, f32[2359296]{0:T(1024)} %bitcast.128, s32[]{} %constant.120) | dynamic-update-slice | bytes 18874372
  307.9 80.4 %dynamic-update-slice.11 = f32[7087872]{0:T(1024)} dynamic-update-slice(f32[7087872]{0:T(1024)} %constant_dynamic-update-slice_fusion.4, f32[2359296]{0:T(1024)} %reshape.397, s32[]{} %constant.122) | dynamic-update-slice | bytes 18874372
  392.8 21.6 pad.4
  414.4 66.7 %reshape.398 = f32[221568,32]{1,0:T(8,128)} reshape(f32[7090176]{0:T(1024)} %pad.4) | data formatting | bytes 56721408 | tf_op jit(solution)/shard_map/reshape | solution.py:89
  481.2 1785.1 %all-reduce.3 = bf16[32,221568]{0,1:T(8,128)(2,1)} all-reduce(f32[32,221568]{0,1:T(8,128)} %bitcast.39), channel_id=6, replica_groups=mesh['batch'=16,'seq'=2] {'batch','seq'}, use_global_device_ids=true, to_apply=%region_22.23.clone | all-reduce | flops 7090176 | bytes 42541056
  2266.2 42.6 %fusion = bf16[221568]{0:T(1024)(128)(2,1)S(1)} fusion(bf16[32,221568]{0,1:T(8,128)(2,1)} %all-reduce.3, u32[]{:T(128)S(6)} %add.152), kind=kLoop, calls=%fused_computation.1 | loop fusion | bytes 886276 | tf_op jit(solution)/shard_map/convert_element_type | solution.py:92
  2308.9 5.8 reshape.410
  2318.6 166.0 %all-gather.5.cloned.1.call-done = bf16[32,1,221568]{2,1,0:T(2,128)(2,1)} async-done(((bf16[1,1,221568]{2,1,0:T(2,128)(2,1)}), bf16[32,1,221568]{2,1,0:T(2,128)(2,1)}) %all-gather.5.cloned.1.call-update) | async-done | bytes 14180368 | tf_op jit(solution)/shard_map/all_gather | solution.py:91
  2484.6 25.7 copy.103
  2510.3 8.6 fusion.71
  2520.5 13.2 fusion.70
  2534.5 6.7 copy.82
  2541.2 7.4 reshape.399
  2549.4 6.7 copy.84
  2556.1 7.4 reshape.400
  2563.5 6.7 copy.85
  2570.2 7.4 reshape.401
  2583.4 7.4 reshape.402
  2593.0 21.0 copy.91
  2614.0 27.7 %reshape.403 = f32[768,3072]{1,0:T(8,128)} reshape(f32[73728,32]{1,0:T(8,128)} %copy.91) | data formatting | bytes 18874368 | tf_op jit(solution)/shard_map/reshape | solution.py:277
  2642.5 21.0 copy.93
  2663.5 25.9 reshape.404
  (250 shorter events, 119.0 us)
Async XLA Ops:
  7.2 42.0 %copy-start = (bf16[768,768]{1,0:T(8,128)(2,1)S(1)}, bf16[768,768]{1,0:T(8,128)(2,1)}, u32[]{:S(2)}) copy-start(bf16[768,768]{1,0:T(8,128)(2,1)} %param.27) | copy-start | bytes 3538948
  7.2 19.8 copy-start.4
  7.2 19.8 copy-start.66
  7.2 133.2 %reduce-scatter.4.cloned.1.call-start = ((), (), s32[]{:S(2)}) async-start(), calls=%async_computation.2 | async-start | bytes 1179648 | tf_op jit(solution)/shard_map/reduce_scatter | solution.py:229
  11.8 17.2 copy-start.13
  28.8 13.2 copy-start.60
  29.0 14.5 copy-start.18
  48.0 12.5 copy-start.7
  49.2 11.3 slice-start
  49.8 21.9 copy-start.45
  50.1 21.6 copy-start.54
  86.7 62.9 %reduce-scatter.6.cloned.1.call-start = ((), (), s32[]{:S(2)}) async-start(), calls=%async_computation.3 | async-start | bytes 1179648 | tf_op jit(solution)/shard_map/reduce_scatter | solution.py:232
  92.4 2392.2 %all-gather.5.cloned.1.call-start = ((), (), s32[]{:S(2)}) async-start(), calls=%async_computation.4 | async-start | bytes 29246976 | tf_op jit(solution)/shard_map/all_gather | solution.py:91
  127.7 12.0 copy-start.40
  127.7 12.0 copy-start.44
  127.7 12.0 copy-start.48
  179.1 21.3 copy-start.15
  179.1 22.8 copy-start.5
  200.4 21.7 copy-start.52
  200.4 23.0 copy-start.63
  200.4 24.3 copy-start.62
  226.0 80.6 %copy-start.57 = (f32[3072]{0:T(1024)S(1)}, f32[3072]{0:T(1024)}, u32[]{:S(2)}) copy-start(f32[3072]{0:T(1024)} %get-tuple-element.27) | copy-start | bytes 36868
  307.9 80.4 %copy-start.51 = (f32[768]{0:T(1024)S(1)}, f32[768]{0:T(1024)}, u32[]{:S(2)}) copy-start(f32[768]{0:T(1024)} %get-tuple-element.25) | copy-start | bytes 9220
  307.9 81.7 %copy-start.50 = (f32[768]{0:T(1024)S(1)}, f32[768]{0:T(1024)}, u32[]{:S(2)}) copy-start(f32[768]{0:T(1024)} %get-tuple-element.21) | copy-start | bytes 9220
  307.9 83.0 %copy-start.49 = (f32[768]{0:T(1024)S(1)}, f32[768]{0:T(1024)}, u32[]{:S(2)}) copy-start(f32[768]{0:T(1024)} %get-tuple-element.24) | copy-start | bytes 9220
  2266.2 48.5 %copy-start.10 = (f32[256,768]{1,0:T(8,128)S(1)}, f32[256,768]{1,0:T(8,128)}, u32[]{:S(2)}) copy-start(f32[256,768]{1,0:T(8,128)} %copy-done.9) | copy-start | bytes 2359300
  2266.2 48.5 %copy-start.17 = (bf16[12,64,256]{2,1,0:T(8,128)(2,1)S(1)}, bf16[12,64,256]{2,1,0:T(8,128)(2,1)}, u32[]{:S(2)}) copy-start(bf16[12,64,256]{2,1,0:T(8,128)(2,1)} %copy-done.16) | copy-start | bytes 1179652
  2266.2 48.5 %copy-start.59 = (f32[256]{0:T(256)S(1)}, f32[256]{0:T(256)}, u32[]{:S(2)}) copy-start(f32[256]{0:T(256)} %copy-done.58) | copy-start | bytes 3076
  2663.5 26.0 copy-start.37
  2663.5 26.7 copy-start.36
  2663.5 27.4 %copy-start.35 = (f32[24,32]{0,1:T(8,128)S(1)}, f32[24,32]{0,1:T(8,128)}, u32[]{:S(2)}) copy-start(f32[24,32]{0,1:T(8,128)} %get-tuple-element.38) | copy-start | bytes 9220
  2663.5 28.9 %copy-start.1 = (bf16[768,768]{1,0:T(8,128)(2,1)S(1)}, bf16[768,768]{1,0:T(8,128)(2,1)}, u32[]{:S(2)}) copy-start(bf16[768,768]{1,0:T(8,128)(2,1)} %param.27) | copy-start | bytes 3538948
  (43 other events, 163.6 us)
Sparse Core Ops, SparseCore 0:
  86.8 18.5 reduce-scatter.3
  107.8 17.4 reduce-scatter.5
  2314.8 169.6 all-gather.4
where the time goes:
time: 2730 us; the launch traced here: 2700 us
  blocking collectives  1810 us (66%)
  local copies, waits for them, and re-layouts  634 us (23%)
  waiting for transfers between devices  166 us (6%)
  matrix products  64.7 us (2%)
    unnamed x1, blocking collectives  1790 us
    unnamed x163, local copies, waits for them, and re-layouts  279 us
    all_gather x1, waiting for transfers between devices, reduce_all(): lax.all_gather(shard_sum.astype(jnp.bfloat16), ('batch', 'seq'), axis=0,...  166 us
    slice x30, local copies, waits for them, and re-layouts, body(): results.append(summed[cursor:cursor + item_size].reshape(grad_item.shape))  98.8 us
    reshape x6, local copies, waits for them, and re-layouts, body(): results.append(summed[cursor:cursor + item_size].reshape(grad_item.shape))  83.3 us
    reshape x1, local copies, waits for them, and re-layouts, reduce_all(): spread_out = padded.reshape(padded_len // device_total, device_total).T  66.7 us
  transfers between devices with their start and end apart: 3, of which 1 were waited for; matrix products, arithmetic and copies ran while one was open for 2% of the time, Pallas kernels for 0%

commit v1 on v0

v1 whole, which is shorter than its diff:
```python
from functools import partial

import jax
import jax.numpy as jnp
from jax import lax
from jax.experimental import pallas as pl
from jax.experimental.pallas import tpu as pltpu
from jax.sharding import PartitionSpec as P

HD = 64
EPS = 1e-06
MASKED = -1e30
bf16 = jnp.bfloat16
f32 = jnp.float32
AXES = ("batch", "seq")
PAIR = 2 * HD
VMEM = pl.BlockSpec(memory_space=pltpu.VMEM)
SMEM = pl.BlockSpec(memory_space=pltpu.SMEM)
HBM = pl.BlockSpec(memory_space=pl.ANY)


def dot(left, right, left_dim=1, right_dim=0):
    dims = (((left_dim,), (right_dim,)), ((), ()))
    return lax.dot_general(left, right, dims, preferred_element_type=f32)


def fetch(source, target, sem):
    copy = pltpu.make_async_copy(source, target, sem)
    copy.start()
    return copy


def column(row):
    return jnp.transpose(jnp.broadcast_to(row, (128, row.shape[1])))[:, :1]


def row_of(col):
    return jnp.transpose(jnp.broadcast_to(col, (col.shape[0], 128)))[:1]


def half_masks():
    lane = lax.broadcasted_iota(jnp.int32, (1, PAIR), 1)
    low = (lane < HD).astype(f32)
    return low.astype(bf16), (1.0 - low).astype(bf16)


def store_blocks(out, at, group, values, flip, rows):
    per = values.shape[0] // rows
    for i in range(per):
        place = (group * per + i) ^ flip
        start = pl.multiple_of(place * rows, 16)
        out[at, pl.ds(start, rows), :] = values[i * rows : (i + 1) * rows]


def project_kernel(x, wq, bq, wk, wv, bv, q, k, v):
    t = x[...]
    q[...] = (dot(t, wq[...]) + bq[...]).astype(bf16) * bf16(HD**-0.5)
    k[...] = dot(t, wk[...]).astype(bf16)
    v[...] = (dot(t, wv[...]) + bv[...]).astype(bf16)


def norm_forward(values):
    centered = values - jnp.mean(values, -1, keepdims=True)
    inverse = lax.rsqrt(jnp.mean(centered * centered, -1, keepdims=True) + EPS)
    return centered * inverse, inverse


def norm_backward(grad, gain, normed, inverse):
    g = grad * gain
    return inverse * (
        g - jnp.mean(g, -1, keepdims=True) - normed * jnp.mean(g * normed, -1, keepdims=True)
    )


def forward_kernel(
    scal, x_own, x_oth, q, k_own, v_own, seg, bv, b_out, gain1, shift1, b_up, b_down,
    gain2, shift2, w_head, cot, cot_weight, wk_h, wv_h, w_out_h, w_up_h, w_down_h,
    layer_out, term, probs_h, k_all, v_all, att_t, normed1, inv1, first_low, slope,
    grad_sum2, grad_down, vecs, send_h, keep_h,
    wk, wv, w_out, w_up, w_down, v_t, probs, active, packed, w_sems, p_sems, o_sems,
):
    loads = [
        fetch(a, b, w_sems.at[n])
        for n, (a, b) in enumerate(
            ((wk_h, wk), (wv_h, wv), (w_out_h, w_out), (w_up_h, w_up), (w_down_h, w_down))
        )
    ]
    here, width = x_own.shape
    half, core, flip_keep, flip_send = scal[0], scal[1], scal[2], scal[3]
    heads = width // HD
    loads[0].wait()
    loads[1].wait()
    other = x_oth[...]
    k_all[:here] = k_own[...]
    v_all[:here] = v_own[...]
    k_all[here:] = dot(other, wk[...]).astype(bf16)
    v_all[here:] = (dot(other, wv[...]) + bv[...]).astype(bf16)
    v_t[...] = jnp.transpose(v_all[...])

    own_ids = seg[:, pl.ds(pl.multiple_of(half * here, 128), here)].astype(f32)
    oth_ids = seg[:, pl.ds(pl.multiple_of((1 - half) * here, 128), here)].astype(f32)
    key_ids = jnp.concatenate([own_ids, oth_ids], 1)
    bias = jnp.where(column(key_ids) == own_ids, 0.0, MASKED)
    masks = half_masks()
    stores = []
    for p in range(heads // 2):
        lanes = slice(p * PAIR, (p + 1) * PAIR)
        q_pair, k_pair = q[:, lanes], k_all[:, lanes]
        for e in range(2):
            h = 2 * p + e
            scores = dot(k_pair, q_pair * masks[e], 1, 1) + bias
            weights = jnp.exp(scores - jnp.max(scores, 0, keepdims=True))
            weights = weights * (1.0 / jnp.sum(weights, 0, keepdims=True))
            low = weights.astype(bf16)
            probs[h] = low
            att_t[h * HD : (h + 1) * HD] = dot(v_t[h * HD : (h + 1) * HD], low).astype(bf16)
        stores.append(fetch(probs.at[pl.ds(2 * p, 2)], probs_h.at[pl.ds(2 * p, 2)], p_sems.at[p]))

    loads[2].wait()
    attn_out = dot(att_t[...], w_out[...], 0, 0) + b_out[...]
    n1, i1 = norm_forward(x_own[...].astype(f32) + attn_out)
    normed1[...] = n1
    inv1[...] = jnp.broadcast_to(i1, inv1.shape)
    first = n1 * gain1[...] + shift1[...]
    f_low = first.astype(bf16)
    first_low[...] = f_low

    loads[3].wait()
    loads[4].wait()
    down = first + b_down[...]
    chunk = 512
    for j in range(w_up.shape[1] // chunk):
        cols = slice(j * chunk, (j + 1) * chunk)
        u = dot(f_low, w_up[:, cols]) + b_up[:, cols]
        cdf = 0.5 + 0.5 * lax.erf(u * (2.0**-0.5))
        pdf = jnp.exp(-0.5 * u * u) * 0.3989422804014327
        slope[:, cols] = (cdf + u * pdf).astype(bf16)
        act = (u * cdf).astype(bf16)
        active[:, cols] = act
        down = down + dot(act, w_down[cols, :])

    n2, i2 = norm_forward(down)
    second = n2 * gain2[...] + shift2[...]
    layer_out[...] = second.astype(bf16)
    head = w_head[...].astype(f32)
    logits = jnp.sum(second * head, -1, keepdims=True)
    softplus = jnp.maximum(logits, 0.0) + jnp.log1p(jnp.exp(-jnp.abs(logits)))
    term[...] = row_of(softplus)
    grad_logits = column(cot_weight[...]) * lax.logistic(logits)
    vecs[0:1] = jnp.sum(grad_logits * second, 0, keepdims=True)
    grad_second = cot[...].astype(f32) + grad_logits * head
    vecs[1:2] = jnp.sum(grad_second * n2, 0, keepdims=True)
    vecs[2:3] = jnp.sum(grad_second, 0, keepdims=True)
    g_sum2 = norm_backward(grad_second, gain2[...], n2, i2)
    grad_sum2[...] = g_sum2
    g_down = g_sum2.astype(bf16)
    grad_down[...] = g_down
    vecs[3:4] = jnp.sum(g_down.astype(f32), 0, keepdims=True)
    vecs[4:8] = jnp.zeros((4, width), f32)

    rows = packed.shape[1] // 16
    outs = []
    for e, (which, flip, out) in enumerate(
        ((1 - core, flip_send, send_h), (core, flip_keep, keep_h))
    ):
        for j in range(2):
            start = pl.multiple_of((which * 2 + j) * width, 128)
            grad = dot(active[:, pl.ds(start, width)], g_down, 0, 0).astype(bf16)
            store_blocks(packed, e, j, grad, flip, rows)
        outs.append(fetch(packed.at[e], out, o_sems.at[e]))
    for copy in stores + outs:
        copy.wait()


def upper_kernel(
    scal, first_low, slope, grad_down, w_down_h, grad_upper, vecs, send_h, keep_h,
    w_down, packed, w_sems, o_sems,
):
    here, width = first_low.shape
    core, flip_keep, flip_send = scal[1], scal[4], scal[5]
    order = [(e, w, j) for e, w in enumerate((1 - core, core)) for j in range(2)]
    loads = []
    for n, (e, which, j) in enumerate(order):
        part = pl.ds(pl.multiple_of((which * 2 + j) * width, 16), width)
        loads.append(fetch(w_down_h.at[part, :], w_down.at[n], w_sems.at[n]))
    first_t = jnp.transpose(first_low[...])
    g_down = grad_down[...]
    rows = packed.shape[1] // 16
    outs = []
    for n, (e, which, j) in enumerate(order):
        start = pl.multiple_of((which * 2 + j) * width, 128)
        loads[n].wait()
        g_active = dot(g_down, w_down[n], 1, 1)
        g_upper = (g_active * slope[:, pl.ds(start, width)].astype(f32)).astype(bf16)
        grad_upper[:, pl.ds(start, width)] = g_upper
        vecs[pl.ds(which * 2 + j, 1), :] = jnp.sum(g_upper.astype(f32), 0, keepdims=True)
        grad = dot(first_t, g_upper).astype(bf16)
        store_blocks(packed, e, j, grad, (flip_send, flip_keep)[e], rows)
        if j == 1:
            outs.append(fetch(packed.at[e], (send_h, keep_h)[e], o_sems.at[e]))
    vecs[4:8] = jnp.zeros((4, width), f32)
    for copy in outs:
        copy.wait()


def first_back_kernel(
    grad_sum2, grad_upper, normed1, inv1, gain1, w_up_h, w_out_h,
    grad_sum1, grad_attn, grad_mix, vecs, w_up, w_out, sems,
):
    load_up = fetch(w_up_h, w_up, sems.at[0])
    load_out = fetch(w_out_h, w_out, sems.at[1])
    n1 = normed1[...]
    load_up.wait()
    grad_first = grad_sum2[...] + dot(grad_upper[...], w_up[...], 1, 1)
    vecs[0:1] = jnp.sum(grad_first * n1, 0, keepdims=True)
    vecs[1:2] = jnp.sum(grad_first, 0, keepdims=True)
    g_sum1 = norm_backward(grad_first, gain1[...], n1, inv1[:, :1])
    grad_sum1[...] = g_sum1
    g_attn = g_sum1.astype(bf16)
    grad_attn[...] = g_attn
    vecs[2:3] = jnp.sum(g_attn.astype(f32), 0, keepdims=True)
    vecs[3:8] = jnp.zeros((5, vecs.shape[1]), f32)
    load_out.wait()
    grad_mix[...] = dot(g_attn, w_out[...], 1, 1).astype(bf16)


def attention_back_kernel(
    scal, x_own, x_oth, q, k_all, v_all, probs_h, att_t, grad_attn, grad_mix, vec_a, vec_b, vec_c,
    grad_query, grad_key, grad_value, extra, send_h, keep_h,
    probs, k_t, x_t, gq_t, vec_all, packed, p_sems, o_sems,
):
    here, width = x_own.shape
    heads = width // HD
    core, flip_keep, flip_send = scal[1], scal[2], scal[3]
    loads = [
        fetch(probs_h.at[pl.ds(2 * p, 2)], probs.at[pl.ds(2 * p, 2)], p_sems.at[p])
        for p in range(heads // 2)
    ]
    k_t[...] = jnp.transpose(k_all[...])
    masks = half_masks()
    for p in range(heads // 2):
        lanes = slice(p * PAIR, (p + 1) * PAIR)
        mix_pair, q_pair, v_pair = grad_mix[:, lanes], q[:, lanes], v_all[:, lanes]
        mixes = [mix_pair * m for m in masks]
        queries = [q_pair * m for m in masks]
        loads[p].wait()
        grads = []
        for e in range(2):
            h = 2 * p + e
            weights = probs[h].astype(f32)
            product = weights * dot(v_pair, mixes[e], 1, 1)
            delta = jnp.sum(product, 0, keepdims=True)
            grad_scores = (product - weights * delta).astype(bf16)
            grads.append(grad_scores)
            gq_t[h * HD : (h + 1) * HD] = (
                dot(k_t[h * HD : (h + 1) * HD], grad_scores) * (HD**-0.5)
            ).astype(bf16)
        both = jnp.concatenate([probs[2 * p], probs[2 * p + 1]], 1)
        grad_value[:, lanes] = dot(both, jnp.concatenate(mixes, 0)).astype(bf16)
        grad_key[:, lanes] = dot(
            jnp.concatenate(grads, 1), jnp.concatenate(queries, 0)
        ).astype(bf16)
    g_query = jnp.transpose(gq_t[...])
    grad_query[...] = g_query
    x_t[:, :here] = jnp.transpose(x_own[...])
    x_t[:, here:] = jnp.transpose(x_oth[...])

    vec_all[0:8] = vec_a[...]
    vec_all[4:8] = vec_b[0:4]
    vec_all[8:16] = vec_c[...]
    vec_all[11:12] = jnp.sum(g_query.astype(f32), 0, keepdims=True)
    vec_all[12:13] = jnp.sum(grad_value[...].astype(f32), 0, keepdims=True)
    extra_low = vec_all[...].astype(bf16)
    extra[...] = extra_low

    total = packed.shape[1] - 16
    rows = total // 16
    packed[0, total:] = extra_low
    packed[1, total:] = extra_low
    for n in range(4):
        if n == 0:
            grad = dot(x_t[:, :here], gq_t[...], 1, 1)
        elif n == 1:
            grad = dot(att_t[...], grad_attn[...])
        elif n == 2:
            grad = dot(x_t[...], grad_key[...])
        else:
            grad = dot(x_t[...], grad_value[...])
        keeps = (core == n // 2).astype(jnp.int32)
        flip = jnp.where(core == n // 2, flip_keep, flip_send)
        store_blocks(packed, keeps, n % 2, grad.astype(bf16), flip, rows)
    outs = [
        fetch(packed.at[0], send_h, o_sems.at[0]),
        fetch(packed.at[1, pl.ds(0, total)], keep_h, o_sems.at[1]),
    ]
    for copy in outs:
        copy.wait()


def tokens_kernel(grad_sum1, grad_query, grad_key, grad_value, wq, wk, wv, own, other):
    here = grad_sum1.shape[0]
    w_key, w_value = wk[...], wv[...]
    other[...] = (
        dot(grad_key[here:], w_key, 1, 1) + dot(grad_value[here:], w_value, 1, 1)
    ).astype(bf16)
    own[...] = (
        grad_sum1[...]
        + dot(grad_query[...], wq[...], 1, 1)
        + dot(grad_key[:here], w_key, 1, 1)
        + dot(grad_value[:here], w_value, 1, 1)
    )


def unpack_kernel(kind, flips, scal, own, received, *refs):
    outs, (scratch, sems) = refs[:-2], refs[-2:]
    core = scal[1]
    width = own.shape[1]
    rows = own.shape[0] // 16
    per = width // rows
    for e, source in enumerate((own, received)):
        which = core if e == 0 else 1 - core
        flip = scal[flips[e]]
        for j in range(2):
            for i in range(per):
                place = pl.multiple_of(((j * per + i) ^ flip) * rows, 16)
                scratch[2 * e + j, i * rows : (i + 1) * rows, :] = source[
                    pl.ds(place, rows), :
                ].astype(f32)
            part = scratch.at[2 * e + j]
            sem = sems.at[2 * e + j]
            start = pl.multiple_of((which * 2 + j) * width, 128)
            if kind == "rows":
                fetch(part, outs[0].at[pl.ds(start, width), :], sem)
            elif kind == "columns":
                fetch(part, outs[0].at[:, pl.ds(start, width)], sem)
            else:
                for group in range(2):
                    @pl.when(which == group)
                    def _():
                        fetch(part, outs[2 * group + j], sem)
    for n in range(4):
        part = scratch.at[n]
        pltpu.make_async_copy(part, part, sems.at[n]).wait()


def call(kernel, in_specs, out_shapes, out_specs, scratch, flops, moved, exps=0):
    return pl.pallas_call(
        kernel,
        in_specs=in_specs,
        out_shape=out_shapes,
        out_specs=out_specs,
        scratch_shapes=scratch,
        compiler_params=pltpu.CompilerParams(vmem_limit_bytes=56 * 2**20),
        cost_estimate=pl.CostEstimate(
            flops=int(flops), bytes_accessed=int(moved), transcendentals=int(exps)
        ),
    )


CORE, NEAR, SEQ = 1, 2, 0


def orders(bits, first):
    rest = list(range(3, bits))
    if first == "plane":
        pairs = [(NEAR, SEQ), (SEQ, NEAR), (rest[0], rest[0]), (rest[1], rest[1])]
    else:
        pairs = [(rest[0], rest[0]), (NEAR, SEQ), (SEQ, NEAR), (rest[1], rest[1])]
    return pairs, [(b, b) for b in rest[2:]]


def flip_of(index, pairs, core):
    bits = [(index >> pair[core]) & 1 for pair in pairs]
    return sum(b << (len(pairs) - 1 - n) for n, b in enumerate(bits))


def swap(values, pair, count):
    perm = [(i, i ^ (1 << pair[(i >> CORE) & 1])) for i in range(count)]
    return lax.ppermute(values, AXES, perm)


def scatter_sum(keep, send, pairs, more, count, extra=None):
    for pair in [(CORE, CORE)] + pairs:
        size = keep.shape[0]
        got = swap(send, pair, count)
        if extra is not None:
            extra = extra + got[size:]
        if size > keep.shape[0] // 2 and pair is not pairs[-1]:
            half = size // 2
            total_keep = keep[:half] + got[:half]
            send = keep[half:] + got[half:size]
            keep = total_keep
            if extra is not None:
                send = jnp.concatenate([send, extra], 0)
        else:
            keep = keep + got[:size]
    if more:
        if extra is not None:
            keep = jnp.concatenate([keep, extra], 0)
        for pair in more:
            keep = keep + swap(keep, pair, count)
        if extra is not None:
            keep, extra = keep[:-16], keep[-16:]
    return keep, extra


def gather_all(part, pairs, count):
    for pair in reversed(pairs):
        part = jnp.concatenate([part, swap(part, pair, count)], 0)
    return part, swap(part, (CORE, CORE), count)


def body(
    count, tokens, segment_ids, w_query, b_query, w_key, w_value, b_value, w_out, b_out,
    gain_attn, shift_attn, w_up, b_up, w_down, b_down, gain_ffn, shift_ffn, w_head, cot_out,
    cot_weight,
):
    row_count, here, width = tokens.shape
    hidden = w_up.shape[1]
    heads = width // HD
    keys = segment_ids.shape[1]
    bits = count.bit_length() - 1
    share = hidden // 2
    rows = share // 16

    seq = lax.axis_index("seq")
    index = lax.axis_index("batch") * 2 + seq
    core = (index >> CORE) & 1
    plane, more = orders(bits, "plane")
    line, _ = orders(bits, "line")
    scal = [seq, core]
    for pairs in (plane, line):
        flips = [flip_of(index, pairs, c) for c in (0, 1)]
        scal.append(jnp.where(core == 0, flips[0], flips[1]))
        scal.append(jnp.where(core == 0, flips[1], flips[0]))
    scal = jnp.stack([jnp.asarray(v, jnp.int32) for v in scal])

    x_own = tokens.reshape(here, width)
    x_oth = lax.ppermute(x_own, "seq", [(0, 1), (1, 0)])
    line_of = lambda v: v.reshape(1, -1)
    sds = jax.ShapeDtypeStruct
    dma = pltpu.SemaphoreType.DMA

    q, k_own, v_own = call(
        project_kernel,
        [VMEM] * 6,
        [sds((here, width), bf16)] * 3,
        [VMEM] * 3,
        [],
        6 * here * width * width,
        3.6e6 + 1.6e6,
    )(x_own, w_query, line_of(b_query), w_key, w_value, line_of(b_value))

    packed_shape = [sds((share, width), bf16)] * 2
    (
        layer_out, term, probs, k_all, v_all, att_t, normed1, inv1, first_low, slope,
        grad_sum2, grad_down, vec_a, send_d, keep_d,
    ) = call(
        forward_kernel,
        [SMEM] + [VMEM] * 17 + [HBM] * 5,
        [
            sds((here, width), bf16),
            sds((1, here), f32),
            sds((heads, keys, here), bf16),
            sds((keys, width), bf16),
            sds((keys, width), bf16),
            sds((width, here), bf16),
            sds((here, width), f32),
            sds((here, 128), f32),
            sds((here, width), bf16),
            sds((here, hidden), bf16),
            sds((here, width), f32),
            sds((here, width), bf16),
            sds((8, width), f32),
        ]
        + packed_shape,
        [VMEM, VMEM, HBM] + [VMEM] * 10 + [HBM, HBM],
        [
            pltpu.VMEM((width, width), bf16),
            pltpu.VMEM((width, width), bf16),
            pltpu.VMEM((width, width), bf16),
            pltpu.VMEM((width, hidden), bf16),
            pltpu.VMEM((hidden, width), bf16),
            pltpu.VMEM((width, keys), bf16),
            pltpu.VMEM((heads, keys, here), bf16),
            pltpu.VMEM((here, hidden), bf16),
            pltpu.VMEM((2, share, width), bf16),
            dma((5,)),
            dma((heads // 2,)),
            dma((2,)),
        ],
        2 * here * width * (3 * width + 3 * hidden) + 4 * heads * keys * here * 128,
        30e6,
        heads * keys * here + 2 * here * hidden,
    )(
        scal, x_own, x_oth, q, k_own, v_own, segment_ids, line_of(b_value), line_of(b_out),
        line_of(gain_attn), line_of(shift_attn), line_of(b_up), line_of(b_down),
        line_of(gain_ffn), line_of(shift_ffn), line_of(w_head), cot_out.reshape(here, width),
        cot_weight, w_key, w_value, w_out, w_up, w_down,
    )
    part_d, _ = scatter_sum(keep_d, send_d, plane, more, count)

    grad_upper, vec_b, send_u, keep_u = call(
        upper_kernel,
        [SMEM] + [VMEM] * 3 + [HBM],
        [sds((here, hidden), bf16), sds((8, width), f32)] + packed_shape,
        [VMEM, VMEM, HBM, HBM],
        [
            pltpu.VMEM((4, width, width), bf16),
            pltpu.VMEM((2, share, width), bf16),
            dma((4,)),
            dma((2,)),
        ],
        4 * here * width * hidden,
        15e6,
    )(scal, first_low, slope, grad_down, w_down)
    part_u, _ = scatter_sum(keep_u, send_u, line, more, count)

    grad_sum1, grad_attn, grad_mix, vec_c = call(
        first_back_kernel,
        [VMEM] * 5 + [HBM] * 2,
        [
            sds((here, width), f32),
            sds((here, width), bf16),
            sds((here, width), bf16),
            sds((8, width), f32),
        ],
        [VMEM] * 4,
        [pltpu.VMEM((width, hidden), bf16), pltpu.VMEM((width, width), bf16), dma((2,))],
        2 * here * width * (hidden + width),
        12e6,
    )(grad_sum2, grad_upper, normed1, inv1, line_of(gain_attn), w_up, w_out)

    grad_query, grad_key, grad_value, extra, send_q, keep_q = call(
        attention_back_kernel,
        [SMEM] + [VMEM] * 5 + [HBM] + [VMEM] * 6,
        [
            sds((here, width), bf16),
            sds((keys, width), bf16),
            sds((keys, width), bf16),
            sds((16, width), bf16),
            sds((share + 16, width), bf16),
            sds((share, width), bf16),
        ],
        [VMEM] * 4 + [HBM] * 2,
        [
            pltpu.VMEM((heads, keys, here), bf16),
            pltpu.VMEM((width, keys), bf16),
            pltpu.VMEM((width, keys), bf16),
            pltpu.VMEM((width, here), bf16),
            pltpu.VMEM((16, width), f32),
            pltpu.VMEM((2, share + 16, width), bf16),
            dma((heads // 2,)),
            dma((2,)),
        ],
        12 * here * width * width + 8 * heads * keys * here * 128,
        15e6,
    )(
        scal, x_own, x_oth, q, k_all, v_all, probs, att_t, grad_attn, grad_mix,
        vec_a, vec_b, vec_c,
    )
    part_q, extra = scatter_sum(keep_q, send_q, plane, more, count, extra)

    own, other = call(
        tokens_kernel,
        [VMEM] * 7,
        [sds((here, width), f32), sds((here, width), bf16)],
        [VMEM] * 2,
        [],
        10 * here * width * width,
        7e6,
    )(grad_sum1, grad_query, grad_key, grad_value, w_query, w_key, w_value)
    grad_tokens = own + lax.ppermute(other, "seq", [(0, 1), (1, 0)]).astype(f32)

    def unpack(kind, flips, part, pairs, shapes):
        own_half, other_half = gather_all(part, pairs, count)
        return call(
            partial(unpack_kernel, kind, flips),
            [SMEM, VMEM, VMEM],
            [sds(s, f32) for s in shapes],
            [HBM] * len(shapes),
            [pltpu.VMEM((4, width, width), f32), dma((4,))],
            0,
            14e6,
        )(scal, own_half, other_half)

    (grad_w_down,) = unpack("rows", (2, 3), part_d, plane, [(hidden, width)])
    (grad_w_up,) = unpack("columns", (4, 5), part_u, line, [(width, hidden)])
    grad_w_query, grad_w_out, grad_w_key, grad_w_value = unpack(
        "groups", (2, 3), part_q, plane, [(width, width)] * 4
    )
    vec = extra.astype(f32)
    return (
        layer_out.reshape(row_count, here, width),
        term.reshape(row_count, here),
        grad_tokens.reshape(row_count, here, width),
        grad_w_query,
        vec[11],
        grad_w_key,
        grad_w_value,
        vec[12],
        grad_w_out,
        vec[10],
        vec[8],
        vec[9],
        grad_w_up,
        vec[4:8].reshape(-1),
        grad_w_down,
        vec[3],
        vec[1],
        vec[2],
        vec[0],
    )


def solution(mesh):
    rows, places = P("batch", "seq", None), P("batch", "seq")
    in_specs = (rows, P("batch", None)) + (P(),) * 16 + (rows, places)
    out_specs = (rows, places, rows) + (P(),) * 16
    count = mesh.shape["batch"] * mesh.shape["seq"]
    return jax.shard_map(
        partial(body, count), mesh=mesh, in_specs=in_specs, out_specs=out_specs, check_vma=False
    )
```

time: 2730 us -> 261 us (0.10); the launches traced: 2700 us -> 261 us
  blocking collectives: 1810 us -> 0 us
  local copies, waits for them, and re-layouts: 634 us -> 21.4 us
  Pallas kernels: 0 us -> 83.1 us
  matrix products: 64.7 us -> 0 us
  waiting for transfers between devices: 166 us -> 114 us
  starting transfers between devices: 0.53 us -> 35.3 us
    unnamed x1 -> x0, blocking collectives: 1790 us -> none
    unnamed x163 -> x21, local copies, waits for them, and re-layouts: 279 us -> 5.81 us
    all_gather x1 -> x0, waiting for transfers between devices: 166 us -> none  [reduce_all(): lax.all_gather(shard_sum.astype(jnp.bfloat16), ('batch', 'seq'), axis=0,...]
    reshape x13 -> x10, local copies, waits for them, and re-layouts: 175 us -> 12 us  [the longest x9 11.4 us: body(): line_of = lambda v: v.reshape(1, -1)]
    ppermute x0 -> x32, waiting for transfers between devices: none -> 114 us  [the longest x30 103 us: swap(): return lax.ppermute(values, AXES, perm)]
    slice x30 -> x2, local copies, waits for them, and re-layouts: 98.8 us -> 0.67 us  [the longest x1 0.66 us: body(): vec[0]]
    pallas_call x0 -> x9, Pallas kernels: none -> 83.1 us  [the longest x1 21.7 us: body(): call(forward_kernel, [SMEM] + [VMEM] * 17 + [HBM] * 5, [sds((here, width)...]
    dot_general x26 -> x0, matrix products: 64.7 us -> none  [the longest x1 10.3 us: body(): jnp.dot(first_low, w_up, preferred_element_type=jnp.float32) + b_up]
  transfers between devices with their start and end apart: 3 -> 32, of which waited for: 1 -> 19; matrix products, arithmetic and copies ran while one was open for 2% -> 10% of each run, Pallas kernels for 0% -> 21%
where the time goes in v1:
time: 261 us
  waiting for transfers between devices  114 us (44%)
  Pallas kernels  83.1 us (32%)
  starting transfers between devices  35.3 us (14%)
  local copies, waits for them, and re-layouts  21.4 us (8%)
  other arithmetic  5.66 us (2%)
    ppermute x30, waiting for transfers between devices, swap(): return lax.ppermute(values, AXES, perm)  103 us
    ppermute x30, starting transfers between devices, swap(): return lax.ppermute(values, AXES, perm)  31.7 us
    pallas_call x1, Pallas kernels, body(): call(forward_kernel, [SMEM] + [VMEM] * 17 + [HBM] * 5, [sds((here, width)...  21.7 us
    pallas_call x3, Pallas kernels, unpack(): call(partial(unpack_kernel, kind, flips), [SMEM, VMEM, VMEM], [sds(s, f32...  18.7 us
    pallas_call x1, Pallas kernels, body(): call(attention_back_kernel, [SMEM] + [VMEM] * 5 + [HBM] + [VMEM] * 6, [sd...  16.2 us
    ppermute x1, waiting for transfers between devices, body(): grad_tokens = own + lax.ppermute(other, 'seq', [(0, 1), (1, 0)]).astype(f32)  11.5 us
    reshape x9, local copies, waits for them, and re-layouts, body(): line_of = lambda v: v.reshape(1, -1)  11.4 us
    pallas_call x1, Pallas kernels, body(): call(upper_kernel, [SMEM] + [VMEM] * 3 + [HBM], [sds((here, hidden), bf16...  9.28 us
  transfers between devices with their start and end apart: 32, of which 19 were waited for; matrix products, arithmetic and copies ran while one was open for 10% of the time, Pallas kernels for 21%

profile of v1, /device:TPU:0, one launch (start us, length us, event | category | flops | bytes accessed | tf_op | source)
XLA Modules:
  0.0 260.8 jit_solution(11592556835488005654)
XLA Ops:
  0.7 3.0 %collective-permute-start = (bf16[256,768]{1,0:T(8,128)(2,1)}, bf16[256,768]{1,0:T(8,128)(2,1)S(1)}, u32[]{:S(2)}, u32[]{:S(2)}) collective-permute-start(bf16[256,768]{1,0:T(8,128)(2,1)} %bitcast.12), channel_id=1, source_target_pairs={{0,1},{1,0},{2,3},{3,2},{4,5},{5,4},{6,7},{7,6},{8,9},{9,8},{10,11... | collective-permute-start | bytes 1179656 | tf_op jit(solution)/shard_map/ppermute | solution.py:439
  15.7 4.0 %shard_map.339 = (bf16[256,768]{1,0:T(8,128)(2,1)}, bf16[256,768]{1,0:T(8,128)(2,1)}, bf16[256,768]{1,0:T(8,128)(2,1)}) custom-call(bf16[256,768]{1,0:T(8,128)(2,1)} %bitcast.13, bf16[768,768]{1,0:T(8,128)(2,1)} %wq.3, f32[1,768]{1,0:T(1,128)} %reshape.86.bq, bf16[768,768]{1,0:T(8,128)(2,1)} %wk.3, bf16[768,768]{1,0:T(8,128)(2,1)} %wv.3, f32[1,768]{1,0:T(1,128)} %reshape.87.bv), custom_call_target="tpu_custom_call" | custom-call | flops 905969664 | bytes 5200000 | tf_op jit(solution)/shard_map/pallas_call | solution.py:444
  20.4 21.7 %shard_map.340 = (bf16[256,768]{1,0:T(8,128)(2,1)}, f32[1,256]{1,0:T(1,128)}, bf16[12,512,256]{2,1,0:T(8,128)(2,1)}, bf16[512,768]{1,0:T(8,128)(2,1)}, bf16[512,...) custom-call(s32[6]{0:T(128)} %stack.27.scal, ...), custom_call_target="tpu_custom_call" | custom-call | flops 5335154688 | bytes 30000000 | tf_op jit(solution)/shard_map/pallas_call | solution.py:458
  42.2 9.3 %shard_map.341 = (bf16[256,3072]{1,0:T(8,128)(2,1)}, f32[8,768]{1,0:T(8,128)}, bf16[1536,768]{1,0:T(8,128)(2,1)}, bf16[1536,768]{1,0:T(8,128)(2,1)}) custom-call(s32[6]{0:T(128)} %stack.27.scal, bf16[256,768]{1,0:T(8,128)(2,1)} %get-tuple-element.63.first_low, bf16[256,3072]{1,0:T(8,128)(2,1)} %get-tuple-element.64.slope, ...), custom_call_target="tpu_custom_call" | custom-call | flops 2415919104 | bytes 15000000 | tf_op jit(solution)/shard_map/pallas_call | solution.py:503
  52.0 7.8 %shard_map.342 = (f32[256,768]{1,0:T(8,128)}, bf16[256,768]{1,0:T(8,128)(2,1)}, bf16[256,768]{1,0:T(8,128)(2,1)}, f32[8,768]{1,0:T(8,128)}) custom-call(f32[256,768]{1,0:T(8,128)} %get-tuple-element.62.grad_sum2, bf16[256,3072]{1,0:T(8,128)(2,1)} %get-tuple-element.66.grad_upper, f32[256,768]{1,0:T(8,128)} %get-tuple-element.67.normed1, ...), custom_call_target="tpu_custom_call" | custom-call | flops 1509949440 | bytes 12000000 | tf_op jit(solution)/shard_map/pallas_call | solution.py:519
  59.8 16.2 %shard_map.343 = (bf16[256,768]{1,0:T(8,128)(2,1)}, bf16[512,768]{1,0:T(8,128)(2,1)}, bf16[512,768]{1,0:T(8,128)(2,1)}, bf16[16,768]{1,0:T(8,128)(2,1)}, bf16[15...) custom-call(s32[6]{0:T(128)} %stack.27.scal, bf16[256,768]{1,0:T(8,128)(2,1)} %bitcast.15, bf16[256,768]{1,0:T(8,128)(2,1)} %copy-done.5, ...), custom_call_target="tpu_custom_call" | custom-call | flops 3422552064 | bytes 15000000 | tf_op jit(solution)/shard_map/pallas_call | solution.py:534
  78.2 1.6 collective-permute-start.13
  83.3 9.4 %collective-permute-done.23 = bf16[768,768]{1,0:T(8,128)(2,1)S(1)} collective-permute-done((bf16[768,768]{1,0:T(8,128)(2,1)S(1)}, bf16[768,768]{1,0:T(8,128)(2,1)S(1)}, u32[]{:S(2)}, u32[]{:S(2)}) %collective-permute-start.23) | collective-permute-done | bytes 1179680 | tf_op jit(solution)/shard_map/ppermute | solution.py:379
  92.9 13.6 %collective-permute-done.13 = bf16[768,768]{1,0:T(8,128)(2,1)S(1)} collective-permute-done((bf16[768,768]{1,0:T(8,128)(2,1)S(1)}, bf16[768,768]{1,0:T(8,128)(2,1)S(1)}, u32[]{:S(2)}, u32[]{:S(2)}) %collective-permute-start.13) | collective-permute-done | bytes 1179680 | tf_op jit(solution)/shard_map/ppermute | solution.py:379
  108.2 3.7 %collective-permute-done.3 = bf16[784,768]{1,0:T(8,128)(2,1)S(1)} collective-permute-done((bf16[784,768]{1,0:T(8,128)(2,1)S(1)}, bf16[784,768]{1,0:T(8,128)(2,1)S(1)}, u32[]{:S(2)}, u32[]{:S(2)}) %collective-permute-start.3) | collective-permute-done | bytes 1204256 | tf_op jit(solution)/shard_map/ppermute | solution.py:379
  112.3 2.1 collective-permute-start.25
  114.4 7.6 %collective-permute-done.14 = bf16[384,768]{1,0:T(8,128)(2,1)S(1)} collective-permute-done((bf16[384,768]{1,0:T(8,128)(2,1)S(1)}, bf16[384,768]{1,0:T(8,128)(2,1)S(1)}, u32[]{:S(2)}, u32[]{:S(2)}) %collective-permute-start.14) | collective-permute-done | bytes 589856 | tf_op jit(solution)/shard_map/ppermute | solution.py:379
  122.1 2.1 collective-permute-done.4
  124.4 1.6 collective-permute-start.5
  126.1 2.6 %collective-permute-start.26 = (bf16[96,768]{1,0:T(8,128)(2,1)S(1)}, bf16[96,768]{1,0:T(8,128)(2,1)S(1)}, u32[]{:S(2)}, u32[]{:S(2)}) collective-permute-start(bf16[96,768]{1,0:T(8,128)(2,1)S(1)} %slice_add_fusion.18), channel_id=1, source_target_pairs={{0,16},{1,17},{2,18},{3,19},{4,20},{5,21},{6,22},{7,23},{8,24},{9,... | collective-permute-start | bytes 442376 | tf_op jit(solution)/shard_map/ppermute | solution.py:379
  128.9 2.6 %collective-permute-start.16 = (bf16[96,768]{1,0:T(8,128)(2,1)S(1)}, bf16[96,768]{1,0:T(8,128)(2,1)S(1)}, u32[]{:S(2)}, u32[]{:S(2)}) collective-permute-start(bf16[96,768]{1,0:T(8,128)(2,1)S(1)} %slice_add_fusion.20), channel_id=1, source_target_pairs={{0,16},{1,17},{2,18},{3,19},{4,20},{5,21},{6,22},{7,23},{8,24},{9,... | collective-permute-start | bytes 442376 | tf_op jit(solution)/shard_map/ppermute | solution.py:379
  131.5 9.1 %collective-permute-done.5 = bf16[208,768]{1,0:T(8,128)(2,1)S(1)} collective-permute-done((bf16[208,768]{1,0:T(8,128)(2,1)S(1)}, bf16[208,768]{1,0:T(8,128)(2,1)S(1)}, u32[]{:S(2)}, u32[]{:S(2)}) %collective-permute-start.5) | collective-permute-done | bytes 319520 | tf_op jit(solution)/shard_map/ppermute | solution.py:379
  142.2 2.1 collective-permute-start.27
  145.9 14.9 %collective-permute-done.27 = bf16[96,768]{1,0:T(8,128)(2,1)S(1)} collective-permute-done((bf16[96,768]{1,0:T(8,128)(2,1)S(1)}, bf16[96,768]{1,0:T(8,128)(2,1)S(1)}, u32[]{:S(2)}, u32[]{:S(2)}) %collective-permute-start.27) | collective-permute-done | bytes 147488 | tf_op jit(solution)/shard_map/ppermute | solution.py:379
  160.9 2.2 collective-permute-start.7
  164.3 6.2 %collective-permute-done.7 = bf16[96,768]{1,0:T(8,128)(2,1)S(1)} collective-permute-done((bf16[96,768]{1,0:T(8,128)(2,1)S(1)}, bf16[96,768]{1,0:T(8,128)(2,1)S(1)}, u32[]{:S(2)}, u32[]{:S(2)}) %collective-permute-start.7) | collective-permute-done | bytes 147488 | tf_op jit(solution)/shard_map/ppermute | solution.py:379
  170.4 2.9 %collective-permute-start.8 = (bf16[192,768]{1,0:T(8,128)(2,1)S(1)}, bf16[192,768]{1,0:T(8,128)(2,1)S(1)}, u32[]{:S(2)}, u32[]{:S(2)}) collective-permute-start(bf16[192,768]{1,0:T(8,128)(2,1)S(1)} %pad_maximum_fusion.9), channel_id=1, source_target_pairs={{0,8},{1,9},{2,10},{3,11},{4,12},{5,13},{6,14},{7,15},{8,0},{9,1},... | collective-permute-start | bytes 884744 | tf_op jit(solution)/shard_map/ppermute | solution.py:379
  175.6 4.3 %collective-permute-done.8 = bf16[192,768]{1,0:T(8,128)(2,1)S(1)} collective-permute-done((bf16[192,768]{1,0:T(8,128)(2,1)S(1)}, bf16[192,768]{1,0:T(8,128)(2,1)S(1)}, u32[]{:S(2)}, u32[]{:S(2)}) %collective-permute-start.8) | collective-permute-done | bytes 294944 | tf_op jit(solution)/shard_map/ppermute | solution.py:379
  181.2 8.5 %collective-permute-done.29 = bf16[384,768]{1,0:T(8,128)(2,1)S(1)} collective-permute-done((bf16[384,768]{1,0:T(8,128)(2,1)S(1)}, bf16[384,768]{1,0:T(8,128)(2,1)S(1)}, u32[]{:S(2)}, u32[]{:S(2)}) %collective-permute-start.29) | collective-permute-done | bytes 589856 | tf_op jit(solution)/shard_map/ppermute | solution.py:379
  190.5 11.8 %collective-permute-done.9 = bf16[384,768]{1,0:T(8,128)(2,1)S(1)} collective-permute-done((bf16[384,768]{1,0:T(8,128)(2,1)S(1)}, bf16[384,768]{1,0:T(8,128)(2,1)S(1)}, u32[]{:S(2)}, u32[]{:S(2)}) %collective-permute-start.9) | collective-permute-done | bytes 589856 | tf_op jit(solution)/shard_map/ppermute | solution.py:379
  209.6 7.7 %collective-permute-done.20 = bf16[768,768]{1,0:T(8,128)(2,1)S(1)} collective-permute-done((bf16[768,768]{1,0:T(8,128)(2,1)S(1)}, bf16[768,768]{1,0:T(8,128)(2,1)S(1)}, u32[]{:S(2)}, u32[]{:S(2)}) %collective-permute-start.20) | collective-permute-done | bytes 1179680 | tf_op jit(solution)/shard_map/ppermute | solution.py:379
  221.0 5.5 %shard_map.344 = (f32[256,768]{1,0:T(8,128)}, bf16[256,768]{1,0:T(8,128)(2,1)}) custom-call(f32[256,768]{1,0:T(8,128)} %get-tuple-element.69.grad_sum1, bf16[256,768]{1,0:T(8,128)(2,1)} %get-tuple-element.79.grad_query, bf16[512,768]{1,0:T(8,128)(2,1)} %get-tuple-element.80.grad_key, bf16[512,768]{1,0:T(8,128)(2,1)} %get-tuple-element.81.grad_value, ...), custom_call_target="tpu_custom_call" | custom-call | flops 1509949440 | bytes 7000000 | tf_op jit(solution)/shard_map/pallas_call | solution.py:564
  227.0 11.5 %collective-permute-done.1 = bf16[256,768]{1,0:T(8,128)(2,1)S(1)} collective-permute-done((bf16[256,768]{1,0:T(8,128)(2,1)}, bf16[256,768]{1,0:T(8,128)(2,1)S(1)}, u32[]{:S(2)}, u32[]{:S(2)}) %collective-permute-start.1) | collective-permute-done | bytes 393248 | tf_op jit(solution)/shard_map/ppermute | solution.py:573
  238.5 2.1 add_bitcast_fusion
  241.8 6.2 %shard_map.347 = f32[3072,768]{1,0:T(8,128)} custom-call(s32[6]{0:T(128)} %stack.27.scal, bf16[1536,768]{1,0:T(8,128)(2,1)} %constant_dynamic-update-slice_fusion.10.own, bf16[1536,768]{1,0:T(8,128)(2,1)} %collective-permute-done.31.received), custom_call_target="tpu_custom_call" | custom-call | bytes 14000000 | tf_op jit(solution)/shard_map/pallas_call | solution.py:577
  248.1 6.2 %shard_map.346 = f32[768,3072]{1,0:T(8,128)} custom-call(s32[6]{0:T(128)} %stack.27.scal, bf16[1536,768]{1,0:T(8,128)(2,1)} %constant_dynamic-update-slice_fusion.5.own, bf16[1536,768]{1,0:T(8,128)(2,1)} %collective-permute-done.21.received), custom_call_target="tpu_custom_call" | custom-call | bytes 14000000 | tf_op jit(solution)/shard_map/pallas_call | solution.py:577
  254.4 6.2 %shard_map.345 = (f32[768,768]{1,0:T(8,128)}, f32[768,768]{1,0:T(8,128)}, f32[768,768]{1,0:T(8,128)}, f32[768,768]{1,0:T(8,128)}) custom-call(s32[6]{0:T(128)} %stack.27.scal, bf16[1536,768]{1,0:T(8,128)(2,1)} %copy-done, bf16[1536,768]{1,0:T(8,128)(2,1)} %collective-permute-done.11.received), custom_call_target="tpu_custom_call" | custom-call | bytes 14000000 | tf_op jit(solution)/shard_map/pallas_call | solution.py:577
  (112 shorter events, 43.2 us)
Async XLA Ops:
  0.7 19.0 %collective-permute-start = (bf16[256,768]{1,0:T(8,128)(2,1)}, bf16[256,768]{1,0:T(8,128)(2,1)S(1)}, u32[]{:S(2)}, u32[]{:S(2)}) collective-permute-start(bf16[256,768]{1,0:T(8,128)(2,1)} %bitcast.12), channel_id=1, source_target_pairs={{0,1},{1,0},{2,3},{3,2},{4,5},{5,4},{6,7},{7,6},{8,9},{9,8},{10,11... | collective-permute-start | bytes 1179656 | tf_op jit(solution)/shard_map/ppermute | solution.py:439
  42.1 34.0 %collective-permute-start.22 = (bf16[1536,768]{1,0:T(8,128)(2,1)}, bf16[1536,768]{1,0:T(8,128)(2,1)S(1)}, u32[]{:S(2)}, u32[]{:S(2)}) collective-permute-start(bf16[1536,768]{1,0:T(8,128)(2,1)} %get-tuple-element.94), channel_id=1, source_target_pairs={{0,2},{1,3},{2,0},{3,1},{4,6},{5,7},{6,4},{7,5},{8,10},{9,11},{10,... | collective-permute-start | bytes 7077896 | tf_op jit(solution)/shard_map/ppermute | solution.py:379
  51.5 26.4 %collective-permute-start.12 = (bf16[1536,768]{1,0:T(8,128)(2,1)}, bf16[1536,768]{1,0:T(8,128)(2,1)S(1)}, u32[]{:S(2)}, u32[]{:S(2)}) collective-permute-start(bf16[1536,768]{1,0:T(8,128)(2,1)} %get-tuple-element.92), channel_id=1, source_target_pairs={{0,2},{1,3},{2,0},{3,1},{4,6},{5,7},{6,4},{7,5},{8,10},{9,11},{10,... | collective-permute-start | bytes 7077896 | tf_op jit(solution)/shard_map/ppermute | solution.py:379
  76.0 4.8 %collective-permute-start.2 = (bf16[1552,768]{1,0:T(8,128)(2,1)}, bf16[1552,768]{1,0:T(8,128)(2,1)S(1)}, u32[]{:S(2)}, u32[]{:S(2)}) collective-permute-start(bf16[1552,768]{1,0:T(8,128)(2,1)} %get-tuple-element.85), channel_id=1, source_target_pairs={{0,2},{1,3},{2,0},{3,1},{4,6},{5,7},{6,4},{7,5},{8,10},{9,11},{10,... | collective-permute-start | bytes 7151624 | tf_op jit(solution)/shard_map/ppermute | solution.py:379
  76.4 16.3 %collective-permute-start.23 = (bf16[768,768]{1,0:T(8,128)(2,1)S(1)}, bf16[768,768]{1,0:T(8,128)(2,1)S(1)}, u32[]{:S(2)}, u32[]{:S(2)}) collective-permute-start(bf16[768,768]{1,0:T(8,128)(2,1)S(1)} %get-tuple-element.113), channel_id=1, source_target_pairs={{0,4},{1,5},{2,3},{3,2},{4,0},{5,1},{6,7},{7,6},{8,12},{9,13},{10,... | collective-permute-start | bytes 3538952 | tf_op jit(solution)/shard_map/ppermute | solution.py:379
  78.2 28.3 %collective-permute-start.13 = (bf16[768,768]{1,0:T(8,128)(2,1)S(1)}, bf16[768,768]{1,0:T(8,128)(2,1)S(1)}, u32[]{:S(2)}, u32[]{:S(2)}) collective-permute-start(bf16[768,768]{1,0:T(8,128)(2,1)S(1)} %get-tuple-element.115), channel_id=1, source_target_pairs={{0,8},{1,9},{2,10},{3,11},{4,12},{5,13},{6,14},{7,15},{8,0},{9,1},... | collective-permute-start | bytes 3538952 | tf_op jit(solution)/shard_map/ppermute | solution.py:379
  81.7 30.2 %collective-permute-start.3 = (bf16[784,768]{1,0:T(8,128)(2,1)S(1)}, bf16[784,768]{1,0:T(8,128)(2,1)S(1)}, u32[]{:S(2)}, u32[]{:S(2)}) collective-permute-start(bf16[784,768]{1,0:T(8,128)(2,1)S(1)} %pad_maximum_fusion), channel_id=1, source_target_pairs={{0,4},{1,5},{2,3},{3,2},{4,0},{5,1},{6,7},{7,6},{8,12},{9,13},{10,... | collective-permute-start | bytes 3612680 | tf_op jit(solution)/shard_map/ppermute | solution.py:379
  92.8 19.4 %collective-permute-start.24 = (bf16[384,768]{1,0:T(8,128)(2,1)S(1)}, bf16[384,768]{1,0:T(8,128)(2,1)S(1)}, u32[]{:S(2)}, u32[]{:S(2)}) collective-permute-start(bf16[384,768]{1,0:T(8,128)(2,1)S(1)} %get-tuple-element.119), channel_id=1, source_target_pairs={{0,1},{1,0},{2,6},{3,7},{4,5},{5,4},{6,2},{7,3},{8,9},{9,8},{10,14... | collective-permute-start | bytes 1769480 | tf_op jit(solution)/shard_map/ppermute | solution.py:379
  106.6 15.4 %collective-permute-start.14 = (bf16[384,768]{1,0:T(8,128)(2,1)S(1)}, bf16[384,768]{1,0:T(8,128)(2,1)S(1)}, u32[]{:S(2)}, u32[]{:S(2)}) collective-permute-start(bf16[384,768]{1,0:T(8,128)(2,1)S(1)} %get-tuple-element.121), channel_id=1, source_target_pairs={{0,4},{1,5},{2,3},{3,2},{4,0},{5,1},{6,7},{7,6},{8,12},{9,13},{10,... | collective-permute-start | bytes 1769480 | tf_op jit(solution)/shard_map/ppermute | solution.py:379
  112.1 12.2 %collective-permute-start.4 = (bf16[400,768]{1,0:T(8,128)(2,1)S(1)}, bf16[400,768]{1,0:T(8,128)(2,1)S(1)}, u32[]{:S(2)}, u32[]{:S(2)}) collective-permute-start(bf16[400,768]{1,0:T(8,128)(2,1)S(1)} %pad_maximum_fusion.4), channel_id=1, source_target_pairs={{0,1},{1,0},{2,6},{3,7},{4,5},{5,4},{6,2},{7,3},{8,9},{9,8},{10,14... | collective-permute-start | bytes 1843208 | tf_op jit(solution)/shard_map/ppermute | solution.py:379
  112.3 13.8 %collective-permute-start.25 = (bf16[192,768]{1,0:T(8,128)(2,1)S(1)}, bf16[192,768]{1,0:T(8,128)(2,1)S(1)}, u32[]{:S(2)}, u32[]{:S(2)}) collective-permute-start(bf16[192,768]{1,0:T(8,128)(2,1)S(1)} %get-tuple-element.125), channel_id=1, source_target_pairs={{0,8},{1,9},{2,10},{3,11},{4,12},{5,13},{6,14},{7,15},{8,0},{9,1},... | collective-permute-start | bytes 884744 | tf_op jit(solution)/shard_map/ppermute | solution.py:379
  122.0 6.8 %collective-permute-start.15 = (bf16[192,768]{1,0:T(8,128)(2,1)S(1)}, bf16[192,768]{1,0:T(8,128)(2,1)S(1)}, u32[]{:S(2)}, u32[]{:S(2)}) collective-permute-start(bf16[192,768]{1,0:T(8,128)(2,1)S(1)} %get-tuple-element.127), channel_id=1, source_target_pairs={{0,1},{1,0},{2,6},{3,7},{4,5},{5,4},{6,2},{7,3},{8,9},{9,8},{10,14... | collective-permute-start | bytes 884744 | tf_op jit(solution)/shard_map/ppermute | solution.py:379
  124.4 16.1 %collective-permute-start.5 = (bf16[208,768]{1,0:T(8,128)(2,1)S(1)}, bf16[208,768]{1,0:T(8,128)(2,1)S(1)}, u32[]{:S(2)}, u32[]{:S(2)}) collective-permute-start(bf16[208,768]{1,0:T(8,128)(2,1)S(1)} %pad_maximum_fusion.8), channel_id=1, source_target_pairs={{0,8},{1,9},{2,10},{3,11},{4,12},{5,13},{6,14},{7,15},{8,0},{9,1},... | collective-permute-start | bytes 958472 | tf_op jit(solution)/shard_map/ppermute | solution.py:379
  126.1 15.4 %collective-permute-start.26 = (bf16[96,768]{1,0:T(8,128)(2,1)S(1)}, bf16[96,768]{1,0:T(8,128)(2,1)S(1)}, u32[]{:S(2)}, u32[]{:S(2)}) collective-permute-start(bf16[96,768]{1,0:T(8,128)(2,1)S(1)} %slice_add_fusion.18), channel_id=1, source_target_pairs={{0,16},{1,17},{2,18},{3,19},{4,20},{5,21},{6,22},{7,23},{8,24},{9,... | collective-permute-start | bytes 442376 | tf_op jit(solution)/shard_map/ppermute | solution.py:379
  128.9 15.5 %collective-permute-start.16 = (bf16[96,768]{1,0:T(8,128)(2,1)S(1)}, bf16[96,768]{1,0:T(8,128)(2,1)S(1)}, u32[]{:S(2)}, u32[]{:S(2)}) collective-permute-start(bf16[96,768]{1,0:T(8,128)(2,1)S(1)} %slice_add_fusion.20), channel_id=1, source_target_pairs={{0,16},{1,17},{2,18},{3,19},{4,20},{5,21},{6,22},{7,23},{8,24},{9,... | collective-permute-start | bytes 442376 | tf_op jit(solution)/shard_map/ppermute | solution.py:379
  140.6 20.2 %collective-permute-start.6 = (bf16[112,768]{1,0:T(8,128)(2,1)S(1)}, bf16[112,768]{1,0:T(8,128)(2,1)S(1)}, u32[]{:S(2)}, u32[]{:S(2)}) collective-permute-start(bf16[112,768]{1,0:T(8,128)(2,1)S(1)} %pad_maximum_fusion.12), channel_id=1, source_target_pairs={{0,16},{1,17},{2,18},{3,19},{4,20},{5,21},{6,22},{7,23},{8,24},{9,... | collective-permute-start | bytes 516104 | tf_op jit(solution)/shard_map/ppermute | solution.py:379
  142.2 18.5 %collective-permute-start.27 = (bf16[96,768]{1,0:T(8,128)(2,1)S(1)}, bf16[96,768]{1,0:T(8,128)(2,1)S(1)}, u32[]{:S(2)}, u32[]{:S(2)}) collective-permute-start(bf16[96,768]{1,0:T(8,128)(2,1)S(1)} %get-tuple-element.105), channel_id=1, source_target_pairs={{0,16},{1,17},{2,18},{3,19},{4,20},{5,21},{6,22},{7,23},{8,24},{9,... | collective-permute-start | bytes 442376 | tf_op jit(solution)/shard_map/ppermute | solution.py:379
  145.1 18.7 %collective-permute-start.17 = (bf16[96,768]{1,0:T(8,128)(2,1)S(1)}, bf16[96,768]{1,0:T(8,128)(2,1)S(1)}, u32[]{:S(2)}, u32[]{:S(2)}) collective-permute-start(bf16[96,768]{1,0:T(8,128)(2,1)S(1)} %get-tuple-element.107), channel_id=1, source_target_pairs={{0,16},{1,17},{2,18},{3,19},{4,20},{5,21},{6,22},{7,23},{8,24},{9,... | collective-permute-start | bytes 442376 | tf_op jit(solution)/shard_map/ppermute | solution.py:379
  160.8 12.6 %collective-permute-start.28 = (bf16[192,768]{1,0:T(8,128)(2,1)S(1)}, bf16[192,768]{1,0:T(8,128)(2,1)S(1)}, u32[]{:S(2)}, u32[]{:S(2)}) collective-permute-start(bf16[192,768]{1,0:T(8,128)(2,1)S(1)} %pad_maximum_fusion.11), channel_id=1, source_target_pairs={{0,8},{1,9},{2,10},{3,11},{4,12},{5,13},{6,14},{7,15},{8,0},{9,1},... | collective-permute-start | bytes 884744 | tf_op jit(solution)/shard_map/ppermute | solution.py:379
  160.9 9.5 %collective-permute-start.7 = (bf16[96,768]{1,0:T(8,128)(2,1)S(1)}, bf16[96,768]{1,0:T(8,128)(2,1)S(1)}, u32[]{:S(2)}, u32[]{:S(2)}) collective-permute-start(bf16[96,768]{1,0:T(8,128)(2,1)S(1)} %get-tuple-element.109), channel_id=1, source_target_pairs={{0,16},{1,17},{2,18},{3,19},{4,20},{5,21},{6,22},{7,23},{8,24},{9,... | collective-permute-start | bytes 442376 | tf_op jit(solution)/shard_map/ppermute | solution.py:379
  163.8 10.2 %collective-permute-start.18 = (bf16[192,768]{1,0:T(8,128)(2,1)S(1)}, bf16[192,768]{1,0:T(8,128)(2,1)S(1)}, u32[]{:S(2)}, u32[]{:S(2)}) collective-permute-start(bf16[192,768]{1,0:T(8,128)(2,1)S(1)} %pad_maximum_fusion.10), channel_id=1, source_target_pairs={{0,1},{1,0},{2,6},{3,7},{4,5},{5,4},{6,2},{7,3},{8,9},{9,8},{10,14... | collective-permute-start | bytes 884744 | tf_op jit(solution)/shard_map/ppermute | solution.py:379
  170.4 9.5 %collective-permute-start.8 = (bf16[192,768]{1,0:T(8,128)(2,1)S(1)}, bf16[192,768]{1,0:T(8,128)(2,1)S(1)}, u32[]{:S(2)}, u32[]{:S(2)}) collective-permute-start(bf16[192,768]{1,0:T(8,128)(2,1)S(1)} %pad_maximum_fusion.9), channel_id=1, source_target_pairs={{0,8},{1,9},{2,10},{3,11},{4,12},{5,13},{6,14},{7,15},{8,0},{9,1},... | collective-permute-start | bytes 884744 | tf_op jit(solution)/shard_map/ppermute | solution.py:379
  173.4 16.3 %collective-permute-start.29 = (bf16[384,768]{1,0:T(8,128)(2,1)S(1)}, bf16[384,768]{1,0:T(8,128)(2,1)S(1)}, u32[]{:S(2)}, u32[]{:S(2)}) collective-permute-start(bf16[384,768]{1,0:T(8,128)(2,1)S(1)} %pad_maximum_fusion.7), channel_id=1, source_target_pairs={{0,1},{1,0},{2,6},{3,7},{4,5},{5,4},{6,2},{7,3},{8,9},{9,8},{10,14... | collective-permute-start | bytes 1769480 | tf_op jit(solution)/shard_map/ppermute | solution.py:379
  174.0 16.3 %collective-permute-start.19 = (bf16[384,768]{1,0:T(8,128)(2,1)S(1)}, bf16[384,768]{1,0:T(8,128)(2,1)S(1)}, u32[]{:S(2)}, u32[]{:S(2)}) collective-permute-start(bf16[384,768]{1,0:T(8,128)(2,1)S(1)} %pad_maximum_fusion.6), channel_id=1, source_target_pairs={{0,4},{1,5},{2,3},{3,2},{4,0},{5,1},{6,7},{7,6},{8,12},{9,13},{10,... | collective-permute-start | bytes 1769480 | tf_op jit(solution)/shard_map/ppermute | solution.py:379
  180.0 22.4 %collective-permute-start.9 = (bf16[384,768]{1,0:T(8,128)(2,1)S(1)}, bf16[384,768]{1,0:T(8,128)(2,1)S(1)}, u32[]{:S(2)}, u32[]{:S(2)}) collective-permute-start(bf16[384,768]{1,0:T(8,128)(2,1)S(1)} %pad_maximum_fusion.5), channel_id=1, source_target_pairs={{0,1},{1,0},{2,6},{3,7},{4,5},{5,4},{6,2},{7,3},{8,9},{9,8},{10,14... | collective-permute-start | bytes 1769480 | tf_op jit(solution)/shard_map/ppermute | solution.py:379
  189.8 17.3 %collective-permute-start.30 = (bf16[768,768]{1,0:T(8,128)(2,1)S(1)}, bf16[768,768]{1,0:T(8,128)(2,1)S(1)}, u32[]{:S(2)}, u32[]{:S(2)}) collective-permute-start(bf16[768,768]{1,0:T(8,128)(2,1)S(1)} %pad_maximum_fusion.3), channel_id=1, source_target_pairs={{0,4},{1,5},{2,3},{3,2},{4,0},{5,1},{6,7},{7,6},{8,12},{9,13},{10,... | collective-permute-start | bytes 3538952 | tf_op jit(solution)/shard_map/ppermute | solution.py:379
  190.4 26.9 %collective-permute-start.20 = (bf16[768,768]{1,0:T(8,128)(2,1)S(1)}, bf16[768,768]{1,0:T(8,128)(2,1)S(1)}, u32[]{:S(2)}, u32[]{:S(2)}) collective-permute-start(bf16[768,768]{1,0:T(8,128)(2,1)S(1)} %pad_maximum_fusion.2), channel_id=1, source_target_pairs={{0,8},{1,9},{2,10},{3,11},{4,12},{5,13},{6,14},{7,15},{8,0},{9,1},... | collective-permute-start | bytes 3538952 | tf_op jit(solution)/shard_map/ppermute | solution.py:379
  202.4 17.3 %collective-permute-start.10 = (bf16[768,768]{1,0:T(8,128)(2,1)S(1)}, bf16[768,768]{1,0:T(8,128)(2,1)S(1)}, u32[]{:S(2)}, u32[]{:S(2)}) collective-permute-start(bf16[768,768]{1,0:T(8,128)(2,1)S(1)} %pad_maximum_fusion.1), channel_id=1, source_target_pairs={{0,4},{1,5},{2,3},{3,2},{4,0},{5,1},{6,7},{7,6},{8,12},{9,13},{10,... | collective-permute-start | bytes 3538952 | tf_op jit(solution)/shard_map/ppermute | solution.py:379
  208.1 33.7 %collective-permute-start.31 = (bf16[1536,768]{1,0:T(8,128)(2,1)}, bf16[1536,768]{1,0:T(8,128)(2,1)}, u32[]{:S(2)}, u32[]{:S(2)}) collective-permute-start(bf16[1536,768]{1,0:T(8,128)(2,1)} %constant_dynamic-update-slice_fusion.10.own), channel_id=1, source_target_pairs={{0,2},{1,3},{2,0},{3,1},{4,6},{5,7},{6,4},{7,5},{8,10},{9,11},{10,... | collective-permute-start | bytes 7077896 | tf_op jit(solution)/shard_map/ppermute | solution.py:379
  218.4 29.7 %collective-permute-start.21 = (bf16[1536,768]{1,0:T(8,128)(2,1)}, bf16[1536,768]{1,0:T(8,128)(2,1)}, u32[]{:S(2)}, u32[]{:S(2)}) collective-permute-start(bf16[1536,768]{1,0:T(8,128)(2,1)} %constant_dynamic-update-slice_fusion.5.own), channel_id=1, source_target_pairs={{0,2},{1,3},{2,0},{3,1},{4,6},{5,7},{6,4},{7,5},{8,10},{9,11},{10,... | collective-permute-start | bytes 7077896 | tf_op jit(solution)/shard_map/ppermute | solution.py:379
  219.8 34.6 %collective-permute-start.11 = (bf16[1536,768]{1,0:T(8,128)(2,1)S(1)}, bf16[1536,768]{1,0:T(8,128)(2,1)}, u32[]{:S(2)}, u32[]{:S(2)}) collective-permute-start(bf16[1536,768]{1,0:T(8,128)(2,1)S(1)} %constant_dynamic-update-slice_fusion.own), channel_id=1, source_target_pairs={{0,2},{1,3},{2,0},{3,1},{4,6},{5,7},{6,4},{7,5},{8,10},{9,11},{10,... | collective-permute-start | bytes 7077896 | tf_op jit(solution)/shard_map/ppermute | solution.py:379
  226.4 12.0 %collective-permute-start.1 = (bf16[256,768]{1,0:T(8,128)(2,1)}, bf16[256,768]{1,0:T(8,128)(2,1)S(1)}, u32[]{:S(2)}, u32[]{:S(2)}) collective-permute-start(bf16[256,768]{1,0:T(8,128)(2,1)} %get-tuple-element.83), channel_id=1, source_target_pairs={{0,1},{1,0},{2,3},{3,2},{4,5},{5,4},{6,7},{7,6},{8,9},{9,8},{10,11... | collective-permute-start | bytes 1179656 | tf_op jit(solution)/shard_map/ppermute | solution.py:573
  (6 other events, 29.2 us)

commit v2 on v1

--- a/solution.py
+++ b/solution.py
@@ -38,6 +38,10 @@
     return jnp.transpose(jnp.broadcast_to(col, (col.shape[0], 128)))[:1]
 
 
+def line(ref, part=slice(None)):
+    return ref[part].reshape(1, -1)
+
+
 def half_masks():
     lane = lax.broadcasted_iota(jnp.int32, (1, PAIR), 1)
     low = (lane < HD).astype(f32)
@@ -54,9 +58,9 @@
 
 def project_kernel(x, wq, bq, wk, wv, bv, q, k, v):
     t = x[...]
-    q[...] = (dot(t, wq[...]) + bq[...]).astype(bf16) * bf16(HD**-0.5)
+    q[...] = (dot(t, wq[...]) + line(bq)).astype(bf16) * bf16(HD**-0.5)
     k[...] = dot(t, wk[...]).astype(bf16)
-    v[...] = (dot(t, wv[...]) + bv[...]).astype(bf16)
+    v[...] = (dot(t, wv[...]) + line(bv)).astype(bf16)
 
 
 def norm_forward(values):
@@ -94,7 +98,7 @@
     k_all[:here] = k_own[...]
     v_all[:here] = v_own[...]
     k_all[here:] = dot(other, wk[...]).astype(bf16)
-    v_all[here:] = (dot(other, wv[...]) + bv[...]).astype(bf16)
+    v_all[here:] = (dot(other, wv[...]) + line(bv)).astype(bf16)
     v_t[...] = jnp.transpose(v_all[...])
 
     own_ids = seg[:, pl.ds(pl.multiple_of(half * here, 128), here)].astype(f32)
@@ -117,21 +121,21 @@
         stores.append(fetch(probs.at[pl.ds(2 * p, 2)], probs_h.at[pl.ds(2 * p, 2)], p_sems.at[p]))
 
     loads[2].wait()
-    attn_out = dot(att_t[...], w_out[...], 0, 0) + b_out[...]
+    attn_out = dot(att_t[...], w_out[...], 0, 0) + line(b_out)
     n1, i1 = norm_forward(x_own[...].astype(f32) + attn_out)
     normed1[...] = n1
     inv1[...] = jnp.broadcast_to(i1, inv1.shape)
-    first = n1 * gain1[...] + shift1[...]
+    first = n1 * line(gain1) + line(shift1)
     f_low = first.astype(bf16)
     first_low[...] = f_low
 
     loads[3].wait()
     loads[4].wait()
-    down = first + b_down[...]
+    down = first + line(b_down)
     chunk = 512
     for j in range(w_up.shape[1] // chunk):
         cols = slice(j * chunk, (j + 1) * chunk)
-        u = dot(f_low, w_up[:, cols]) + b_up[:, cols]
+        u = dot(f_low, w_up[:, cols]) + line(b_up, cols)
         cdf = 0.5 + 0.5 * lax.erf(u * (2.0**-0.5))
         pdf = jnp.exp(-0.5 * u * u) * 0.3989422804014327
         slope[:, cols] = (cdf + u * pdf).astype(bf16)
@@ -140,9 +144,9 @@
         down = down + dot(act, w_down[cols, :])
 
     n2, i2 = norm_forward(down)
-    second = n2 * gain2[...] + shift2[...]
+    second = n2 * line(gain2) + line(shift2)
     layer_out[...] = second.astype(bf16)
-    head = w_head[...].astype(f32)
+    head = line(w_head).astype(f32)
     logits = jnp.sum(second * head, -1, keepdims=True)
     softplus = jnp.maximum(logits, 0.0) + jnp.log1p(jnp.exp(-jnp.abs(logits)))
     term[...] = row_of(softplus)
@@ -151,14 +155,14 @@
     grad_second = cot[...].astype(f32) + grad_logits * head
     vecs[1:2] = jnp.sum(grad_second * n2, 0, keepdims=True)
     vecs[2:3] = jnp.sum(grad_second, 0, keepdims=True)
-    g_sum2 = norm_backward(grad_second, gain2[...], n2, i2)
+    g_sum2 = norm_backward(grad_second, line(gain2), n2, i2)
     grad_sum2[...] = g_sum2
     g_down = g_sum2.astype(bf16)
     grad_down[...] = g_down
     vecs[3:4] = jnp.sum(g_down.astype(f32), 0, keepdims=True)
     vecs[4:8] = jnp.zeros((4, width), f32)
 
-    rows = packed.shape[1] // 16
+    rows = packed.shape[1] // BLOCKS
     outs = []
     for e, (which, flip, out) in enumerate(
         ((1 - core, flip_send, send_h), (core, flip_keep, keep_h))
@@ -173,7 +177,7 @@
 
 
 def upper_kernel(
-    scal, first_low, slope, grad_down, w_down_h, grad_upper, vecs, send_h, keep_h,
+    scal, first_low, slope, grad_down, w_down_h, after, grad_upper, vecs, send_h, keep_h,
     w_down, packed, w_sems, o_sems,
 ):
     here, width = first_low.shape
@@ -185,7 +189,7 @@
         loads.append(fetch(w_down_h.at[part, :], w_down.at[n], w_sems.at[n]))
     first_t = jnp.transpose(first_low[...])
     g_down = grad_down[...]
-    rows = packed.shape[1] // 16
+    rows = packed.shape[1] // BLOCKS
     outs = []
     for n, (e, which, j) in enumerate(order):
         start = pl.multiple_of((which * 2 + j) * width, 128)
@@ -204,7 +208,7 @@
 
 
 def first_back_kernel(
-    grad_sum2, grad_upper, normed1, inv1, gain1, w_up_h, w_out_h,
+    grad_sum2, grad_upper, normed1, inv1, gain1, w_up_h, w_out_h, after,
     grad_sum1, grad_attn, grad_mix, vecs, w_up, w_out, sems,
 ):
     load_up = fetch(w_up_h, w_up, sems.at[0])
@@ -214,7 +218,7 @@
     grad_first = grad_sum2[...] + dot(grad_upper[...], w_up[...], 1, 1)
     vecs[0:1] = jnp.sum(grad_first * n1, 0, keepdims=True)
     vecs[1:2] = jnp.sum(grad_first, 0, keepdims=True)
-    g_sum1 = norm_backward(grad_first, gain1[...], n1, inv1[:, :1])
+    g_sum1 = norm_backward(grad_first, line(gain1), n1, inv1[:, :1])
     grad_sum1[...] = g_sum1
     g_attn = g_sum1.astype(bf16)
     grad_attn[...] = g_attn
@@ -225,13 +229,12 @@
 
 
 def attention_back_kernel(
-    scal, x_own, x_oth, q, k_all, v_all, probs_h, att_t, grad_attn, grad_mix, vec_a, vec_b, vec_c,
-    grad_query, grad_key, grad_value, extra, send_h, keep_h,
-    probs, k_t, x_t, gq_t, vec_all, packed, p_sems, o_sems,
+    q, k_all, v_all, probs_h, grad_mix, after,
+    grad_query, query_t, grad_key, grad_value,
+    probs, k_t, p_sems,
 ):
-    here, width = x_own.shape
+    width = q.shape[1]
     heads = width // HD
-    core, flip_keep, flip_send = scal[1], scal[2], scal[3]
     loads = [
         fetch(probs_h.at[pl.ds(2 * p, 2)], probs.at[pl.ds(2 * p, 2)], p_sems.at[p])
         for p in range(heads // 2)
@@ -252,7 +255,7 @@
             delta = jnp.sum(product, 0, keepdims=True)
             grad_scores = (product - weights * delta).astype(bf16)
             grads.append(grad_scores)
-            gq_t[h * HD : (h + 1) * HD] = (
+            query_t[h * HD : (h + 1) * HD] = (
                 dot(k_t[h * HD : (h + 1) * HD], grad_scores) * (HD**-0.5)
             ).astype(bf16)
         both = jnp.concatenate([probs[2 * p], probs[2 * p + 1]], 1)
@@ -260,26 +263,35 @@
         grad_key[:, lanes] = dot(
             jnp.concatenate(grads, 1), jnp.concatenate(queries, 0)
         ).astype(bf16)
-    g_query = jnp.transpose(gq_t[...])
-    grad_query[...] = g_query
+    grad_query[...] = jnp.transpose(query_t[...])
+
+
+def attention_weights_kernel(
+    scal, x_own, x_oth, grad_query, query_t, grad_key, grad_value, att_t, grad_attn,
+    vec_a, vec_b, vec_c, after,
+    extra, send_h, keep_h,
+    x_t, vec_all, packed, o_sems,
+):
+    here, width = x_own.shape
+    core, flip_keep, flip_send = scal[1], scal[6], scal[7]
     x_t[:, :here] = jnp.transpose(x_own[...])
     x_t[:, here:] = jnp.transpose(x_oth[...])
 
     vec_all[0:8] = vec_a[...]
     vec_all[4:8] = vec_b[0:4]
     vec_all[8:16] = vec_c[...]
-    vec_all[11:12] = jnp.sum(g_query.astype(f32), 0, keepdims=True)
+    vec_all[11:12] = jnp.sum(grad_query[...].astype(f32), 0, keepdims=True)
     vec_all[12:13] = jnp.sum(grad_value[...].astype(f32), 0, keepdims=True)
     extra_low = vec_all[...].astype(bf16)
     extra[...] = extra_low
 
     total = packed.shape[1] - 16
-    rows = total // 16
+    rows = total // BLOCKS
     packed[0, total:] = extra_low
     packed[1, total:] = extra_low
     for n in range(4):
         if n == 0:
-            grad = dot(x_t[:, :here], gq_t[...], 1, 1)
+            grad = dot(x_t[:, :here], query_t[...], 1, 1)
         elif n == 1:
             grad = dot(att_t[...], grad_attn[...])
         elif n == 2:
@@ -297,7 +309,7 @@
         copy.wait()
 
 
-def tokens_kernel(grad_sum1, grad_query, grad_key, grad_value, wq, wk, wv, own, other):
+def tokens_kernel(grad_sum1, grad_query, grad_key, grad_value, wq, wk, wv, after, own, other):
     here = grad_sum1.shape[0]
     w_key, w_value = wk[...], wv[...]
     other[...] = (
@@ -311,11 +323,11 @@
     )
 
 
-def unpack_kernel(kind, flips, scal, own, received, *refs):
-    outs, (scratch, sems) = refs[:-2], refs[-2:]
+def unpack_kernel(kind, flips, outs_n, scal, own, received, *refs):
+    outs, (scratch, sems) = refs[-2 - outs_n : -2], refs[-2:]
     core = scal[1]
     width = own.shape[1]
-    rows = own.shape[0] // 16
+    rows = own.shape[0] // BLOCKS
     per = width // rows
     for e, source in enumerate((own, received)):
         which = core if e == 0 else 1 - core
@@ -343,30 +355,36 @@
         pltpu.make_async_copy(part, part, sems.at[n]).wait()
 
 
-def call(kernel, in_specs, out_shapes, out_specs, scratch, flops, moved, exps=0):
+def call(kernel, in_specs, out_shapes, out_specs, scratch, vmem):
     return pl.pallas_call(
         kernel,
         in_specs=in_specs,
         out_shape=out_shapes,
         out_specs=out_specs,
         scratch_shapes=scratch,
-        compiler_params=pltpu.CompilerParams(vmem_limit_bytes=56 * 2**20),
-        cost_estimate=pl.CostEstimate(
-            flops=int(flops), bytes_accessed=int(moved), transcendentals=int(exps)
-        ),
+        compiler_params=pltpu.CompilerParams(vmem_limit_bytes=vmem * 2**20),
+        cost_estimate=pl.CostEstimate(flops=0, bytes_accessed=0, transcendentals=0),
     )
 
 
-CORE, NEAR, SEQ = 1, 2, 0
-
-
-def orders(bits, first):
-    rest = list(range(3, bits))
-    if first == "plane":
-        pairs = [(NEAR, SEQ), (SEQ, NEAR), (rest[0], rest[0]), (rest[1], rest[1])]
-    else:
-        pairs = [(rest[0], rest[0]), (NEAR, SEQ), (SEQ, NEAR), (rest[1], rest[1])]
-    return pairs, [(b, b) for b in rest[2:]]
+SEQ, CORE, NEAR, LINE, FAR = range(5)
+
+STEPS = (
+    ((NEAR, SEQ), (LINE, NEAR), (SEQ, LINE)),
+    ((SEQ, LINE), (NEAR, SEQ), (LINE, NEAR)),
+    ((LINE, NEAR), (SEQ, LINE), (NEAR, SEQ)),
+)
+BLOCKS = 8
+UPPER, FIRST, ATTENTION, WEIGHTS, LAUNCH, TOKENS, EXCHANGED = range(3, 10)
+CHAINED = 10
+ORDER = (
+    (UPPER, CHAINED + 0, FIRST, CHAINED + 1, ATTENTION, CHAINED + 0, WEIGHTS, CHAINED + 1, CHAINED + 0)
+    + (LAUNCH, TOKENS, CHAINED + 2, CHAINED + 1, CHAINED + 0)
+    + (CHAINED + 2, CHAINED + 1, CHAINED + 0) * 2
+    + (EXCHANGED,)
+    + (CHAINED + 2, CHAINED + 1, CHAINED + 0) * 3
+    + (CHAINED + 2, CHAINED + 1, CHAINED + 2, CHAINED + 2)
+)
 
 
 def flip_of(index, pairs, core):
@@ -379,35 +397,51 @@
     return lax.ppermute(values, AXES, perm)
 
 
-def scatter_sum(keep, send, pairs, more, count, extra=None):
-    for pair in [(CORE, CORE)] + pairs:
-        size = keep.shape[0]
+def order_after(values, after):
+    return lax.optimization_barrier((values, after))[0] if after else values
+
+
+def halve(keep, got, extra, more_halves, after):
+    size = keep.shape[0]
+    keep, got = order_after((keep, got), after)
+    if extra is not None:
+        extra = extra + got[size:]
+    if not more_halves:
+        return keep + got[:size], None, extra
+    half = size // 2
+    send = keep[half:] + got[half:size]
+    if extra is not None:
+        send = jnp.concatenate([send, extra], 0)
+    return keep[:half] + got[:half], send, extra
+
+
+def join(part, got, after):
+    part, got = order_after((part, got), after)
+    return jnp.concatenate([part, got], 0)
+
+
+def sum_stream(keep, send, pairs, more, count, finish, extra=None):
+    steps = ((CORE, CORE),) + pairs
+    for n, pair in enumerate(steps):
         got = swap(send, pair, count)
-        if extra is not None:
-            extra = extra + got[size:]
-        if size > keep.shape[0] // 2 and pair is not pairs[-1]:
-            half = size // 2
-            total_keep = keep[:half] + got[:half]
-            send = keep[half:] + got[half:size]
-            keep = total_keep
-            if extra is not None:
-                send = jnp.concatenate([send, extra], 0)
-        else:
-            keep = keep + got[:size]
-    if more:
-        if extra is not None:
-            keep = jnp.concatenate([keep, extra], 0)
-        for pair in more:
-            keep = keep + swap(keep, pair, count)
-        if extra is not None:
-            keep, extra = keep[:-16], keep[-16:]
-    return keep, extra
-
-
-def gather_all(part, pairs, count):
+        after = yield keep
+        keep, send, extra = halve(keep, got, extra, n < len(steps) - 1, after)
+    size = keep.shape[0]
+    for n, pair in enumerate(more):
+        both = keep if extra is None else jnp.concatenate([keep, extra], 0)
+        got = swap(both, pair, count)
+        if n == 0:
+            after = yield keep
+            both, got = order_after((both, got), after)
+        both = both + got
+        keep, extra = both[:size], None if extra is None else both[size:]
     for pair in reversed(pairs):
-        part = jnp.concatenate([part, swap(part, pair, count)], 0)
-    return part, swap(part, (CORE, CORE), count)
+        got = swap(keep, pair, count)
+        after = yield keep
+        keep = join(keep, got, after)
+    got = swap(keep, (CORE, CORE), count)
+    after = yield keep
+    yield finish(keep, got, extra, after)
 
 
 def body(
@@ -421,15 +455,13 @@
     keys = segment_ids.shape[1]
     bits = count.bit_length() - 1
     share = hidden // 2
-    rows = share // 16
 
     seq = lax.axis_index("seq")
     index = lax.axis_index("batch") * 2 + seq
     core = (index >> CORE) & 1
-    plane, more = orders(bits, "plane")
-    line, _ = orders(bits, "line")
+    more = [(b, b) for b in range(FAR, bits)]
     scal = [seq, core]
-    for pairs in (plane, line):
+    for pairs in STEPS:
         flips = [flip_of(index, pairs, c) for c in (0, 1)]
         scal.append(jnp.where(core == 0, flips[0], flips[1]))
         scal.append(jnp.where(core == 0, flips[1], flips[0]))
@@ -437,7 +469,6 @@
 
     x_own = tokens.reshape(here, width)
     x_oth = lax.ppermute(x_own, "seq", [(0, 1), (1, 0)])
-    line_of = lambda v: v.reshape(1, -1)
     sds = jax.ShapeDtypeStruct
     dma = pltpu.SemaphoreType.DMA
 
@@ -447,9 +478,8 @@
         [sds((here, width), bf16)] * 3,
         [VMEM] * 3,
         [],
-        6 * here * width * width,
-        3.6e6 + 1.6e6,
-    )(x_own, w_query, line_of(b_query), w_key, w_value, line_of(b_value))
+        56,
+    )(x_own, w_query, b_query, w_key, w_value, b_value)
 
     packed_shape = [sds((share, width), bf16)] * 2
     (
@@ -489,107 +519,138 @@
             dma((heads // 2,)),
             dma((2,)),
         ],
-        2 * here * width * (3 * width + 3 * hidden) + 4 * heads * keys * here * 128,
-        30e6,
-        heads * keys * here + 2 * here * hidden,
+        56,
     )(
-        scal, x_own, x_oth, q, k_own, v_own, segment_ids, line_of(b_value), line_of(b_out),
-        line_of(gain_attn), line_of(shift_attn), line_of(b_up), line_of(b_down),
-        line_of(gain_ffn), line_of(shift_ffn), line_of(w_head), cot_out.reshape(here, width),
+        scal, x_own, x_oth, q, k_own, v_own, segment_ids, b_value, b_out,
+        gain_attn, shift_attn, b_up, b_down,
+        gain_ffn, shift_ffn, w_head, cot_out.reshape(here, width),
         cot_weight, w_key, w_value, w_out, w_up, w_down,
     )
-    part_d, _ = scatter_sum(keep_d, send_d, plane, more, count)
-
-    grad_upper, vec_b, send_u, keep_u = call(
-        upper_kernel,
-        [SMEM] + [VMEM] * 3 + [HBM],
-        [sds((here, hidden), bf16), sds((8, width), f32)] + packed_shape,
-        [VMEM, VMEM, HBM, HBM],
-        [
-            pltpu.VMEM((4, width, width), bf16),
-            pltpu.VMEM((2, share, width), bf16),
-            dma((4,)),
-            dma((2,)),
-        ],
-        4 * here * width * hidden,
-        15e6,
-    )(scal, first_low, slope, grad_down, w_down)
-    part_u, _ = scatter_sum(keep_u, send_u, line, more, count)
-
-    grad_sum1, grad_attn, grad_mix, vec_c = call(
-        first_back_kernel,
-        [VMEM] * 5 + [HBM] * 2,
-        [
-            sds((here, width), f32),
-            sds((here, width), bf16),
-            sds((here, width), bf16),
-            sds((8, width), f32),
-        ],
-        [VMEM] * 4,
-        [pltpu.VMEM((width, hidden), bf16), pltpu.VMEM((width, width), bf16), dma((2,))],
-        2 * here * width * (hidden + width),
-        12e6,
-    )(grad_sum2, grad_upper, normed1, inv1, line_of(gain_attn), w_up, w_out)
-
-    grad_query, grad_key, grad_value, extra, send_q, keep_q = call(
-        attention_back_kernel,
-        [SMEM] + [VMEM] * 5 + [HBM] + [VMEM] * 6,
-        [
-            sds((here, width), bf16),
-            sds((keys, width), bf16),
-            sds((keys, width), bf16),
-            sds((16, width), bf16),
-            sds((share + 16, width), bf16),
-            sds((share, width), bf16),
-        ],
-        [VMEM] * 4 + [HBM] * 2,
-        [
-            pltpu.VMEM((heads, keys, here), bf16),
-            pltpu.VMEM((width, keys), bf16),
-            pltpu.VMEM((width, keys), bf16),
-            pltpu.VMEM((width, here), bf16),
-            pltpu.VMEM((16, width), f32),
-            pltpu.VMEM((2, share + 16, width), bf16),
-            dma((heads // 2,)),
-            dma((2,)),
-        ],
-        12 * here * width * width + 8 * heads * keys * here * 128,
-        15e6,
-    )(
-        scal, x_own, x_oth, q, k_all, v_all, probs, att_t, grad_attn, grad_mix,
-        vec_a, vec_b, vec_c,
-    )
-    part_q, extra = scatter_sum(keep_q, send_q, plane, more, count, extra)
-
-    own, other = call(
-        tokens_kernel,
-        [VMEM] * 7,
-        [sds((here, width), f32), sds((here, width), bf16)],
-        [VMEM] * 2,
-        [],
-        10 * here * width * width,
-        7e6,
-    )(grad_sum1, grad_query, grad_key, grad_value, w_query, w_key, w_value)
-    grad_tokens = own + lax.ppermute(other, "seq", [(0, 1), (1, 0)]).astype(f32)
-
-    def unpack(kind, flips, part, pairs, shapes):
-        own_half, other_half = gather_all(part, pairs, count)
-        return call(
-            partial(unpack_kernel, kind, flips),
-            [SMEM, VMEM, VMEM],
-            [sds(s, f32) for s in shapes],
-            [HBM] * len(shapes),
-            [pltpu.VMEM((4, width, width), f32), dma((4,))],
-            0,
-            14e6,
-        )(scal, own_half, other_half)
-
-    (grad_w_down,) = unpack("rows", (2, 3), part_d, plane, [(hidden, width)])
-    (grad_w_up,) = unpack("columns", (4, 5), part_u, line, [(width, hidden)])
-    grad_w_query, grad_w_out, grad_w_key, grad_w_value = unpack(
-        "groups", (2, 3), part_q, plane, [(width, width)] * 4
-    )
-    vec = extra.astype(f32)
+
+    def unpack(kind, flips, shapes):
+        def finish(own_half, other_half, extra, after):
+            outs = call(
+                partial(unpack_kernel, kind, flips, len(shapes)),
+                [SMEM, VMEM, VMEM] + [HBM] * len(after),
+                [sds(s, f32) for s in shapes],
+                [HBM] * len(shapes),
+                [pltpu.VMEM((4, width, width), f32), dma((4,))],
+                20,
+            )(scal, own_half, other_half, *after)
+            return outs, extra
+
+        return finish
+
+    streams = {}
+
+    def launch(n, keep, send, kind, shapes, extra=None):
+        flips = (2 + 2 * n, 3 + 2 * n)
+        streams[n] = sum_stream(
+            keep, send, STEPS[n], more, count, unpack(kind, flips, shapes), extra
+        )
+        next(streams[n])
+
+    launch(0, keep_d, send_d, "rows", [(hidden, width)])
+    done, ended = keep_d, {}
+    for event in ORDER:
+        if event == UPPER:
+            grad_upper, vec_b, send_u, keep_u = call(
+                upper_kernel,
+                [SMEM] + [VMEM] * 3 + [HBM] * 2,
+                [sds((here, hidden), bf16), sds((8, width), f32)] + packed_shape,
+                [VMEM, VMEM, HBM, HBM],
+                [
+                    pltpu.VMEM((4, width, width), bf16),
+                    pltpu.VMEM((2, share, width), bf16),
+                    dma((4,)),
+                    dma((2,)),
+                ],
+                24,
+            )(scal, first_low, slope, grad_down, w_down, done)
+            launch(1, keep_u, send_u, "columns", [(width, hidden)])
+            done = grad_upper
+        elif event == FIRST:
+            grad_sum1, grad_attn, grad_mix, vec_c = call(
+                first_back_kernel,
+                [VMEM] * 5 + [HBM] * 3,
+                [
+                    sds((here, width), f32),
+                    sds((here, width), bf16),
+                    sds((here, width), bf16),
+                    sds((8, width), f32),
+                ],
+                [VMEM] * 4,
+                [pltpu.VMEM((width, hidden), bf16), pltpu.VMEM((width, width), bf16), dma((2,))],
+                20,
+            )(grad_sum2, grad_upper, normed1, inv1, gain_attn, w_up, w_out, done)
+            done = grad_mix
+        elif event == ATTENTION:
+            grad_query, query_t, grad_key, grad_value = call(
+                attention_back_kernel,
+                [VMEM] * 3 + [HBM, VMEM, HBM],
+                [
+                    sds((here, width), bf16),
+                    sds((width, here), bf16),
+                    sds((keys, width), bf16),
+                    sds((keys, width), bf16),
+                ],
+                [VMEM] * 4,
+                [
+                    pltpu.VMEM((heads, keys, here), bf16),
+                    pltpu.VMEM((width, keys), bf16),
+                    dma((heads // 2,)),
+                ],
+                20,
+            )(q, k_all, v_all, probs, grad_mix, done)
+            done = grad_query
+        elif event == WEIGHTS:
+            extra, send_q, keep_q = call(
+                attention_weights_kernel,
+                [SMEM] + [VMEM] * 11 + [HBM],
+                [
+                    sds((16, width), bf16),
+                    sds((share + 16, width), bf16),
+                    sds((share, width), bf16),
+                ],
+                [VMEM, HBM, HBM],
+                [
+                    pltpu.VMEM((width, keys), bf16),
+                    pltpu.VMEM((16, width), f32),
+                    pltpu.VMEM((2, share + 16, width), bf16),
+                    dma((2,)),
+                ],
+                20,
+            )(
+                scal, x_own, x_oth, grad_query, query_t, grad_key, grad_value, att_t, grad_attn,
+                vec_a, vec_b, vec_c, done,
+            )
+            done = extra
+        elif event == LAUNCH:
+            send_q = order_after(send_q, [done])
+            launch(2, keep_q, send_q, "groups", [(width, width)] * 4, extra)
+        elif event == TOKENS:
+            own, other = call(
+                tokens_kernel,
+                [VMEM] * 7 + [HBM],
+                [sds((here, width), f32), sds((here, width), bf16)],
+                [VMEM] * 2,
+                [],
+                16,
+            )(grad_sum1, grad_query, grad_key, grad_value, w_query, w_key, w_value, done)
+
+            received = lax.ppermute(other, "seq", [(0, 1), (1, 0)])
+            done = other
+        elif event == EXCHANGED:
+            grad_tokens = done = own + received.astype(f32)
+        else:
+            n = event % CHAINED
+            done = streams[n].send([done] if event >= CHAINED else [])
+            if isinstance(done, tuple):
+                ended[n], done = done, done[0][0]
+
+    (grad_w_down,), (grad_w_up,) = ended[0][0], ended[1][0]
+    grad_w_query, grad_w_out, grad_w_key, grad_w_value = ended[2][0]
+    vec = ended[2][1].astype(f32)
     return (
         layer_out.reshape(row_count, here, width),
         term.reshape(row_count, here),

time: 261 us -> 228 us (0.87)
  Pallas kernels: 83.1 us -> 63 us
  local copies, waits for them, and re-layouts: 21.4 us -> 12 us
  starting transfers between devices: 35.3 us -> 30.7 us
  waiting for transfers between devices: 114 us -> 118 us
  other arithmetic: 5.66 us -> 2.9 us
    pallas_call x7 -> x8, Pallas kernels: 57.4 us -> 36.8 us  [the longest x3 14.3 us: finish(): call(partial(unpack_kernel, kind, flips, len(shapes)), [SMEM, VMEM, VMEM]...]
    ppermute x1, waiting for transfers between devices: 11.5 us -> 0.01 us  [body(): received = lax.ppermute(other, 'seq', [(0, 1), (1, 0)])]
    reshape x9 -> x0, local copies, waits for them, and re-layouts: 11.4 us -> none  [body(): line_of = lambda v: v.reshape(1, -1)]
    ppermute x30 -> x27, waiting for transfers between devices: 103 us -> 113 us  [swap(): return lax.ppermute(values, AXES, perm)]
    ppermute x1, waiting for transfers between devices: 0.01 us -> 4.76 us  [body(): x_oth = lax.ppermute(x_own, 'seq', [(0, 1), (1, 0)])]
    ppermute x30 -> x27, starting transfers between devices: 31.7 us -> 27.2 us  [swap(): return lax.ppermute(values, AXES, perm)]
    unnamed x21 -> x59, local copies, waits for them, and re-layouts: 5.81 us -> 9.71 us
  transfers between devices with their start and end apart: 32 -> 29, of which waited for: 19 -> 17; matrix products, arithmetic and copies ran while one was open for 10% -> 2% of each run, Pallas kernels for 21% -> 15%
where the time goes in v2:
time: 228 us
  waiting for transfers between devices  118 us (52%)
  Pallas kernels  63 us (28%)
  starting transfers between devices  30.7 us (13%)
  local copies, waits for them, and re-layouts  12 us (5%)
  other arithmetic  2.9 us (1%)
    ppermute x27, waiting for transfers between devices, swap(): return lax.ppermute(values, AXES, perm)  113 us
    ppermute x27, starting transfers between devices, swap(): return lax.ppermute(values, AXES, perm)  27.2 us
    pallas_call x1, Pallas kernels, body(): call(forward_kernel, [SMEM] + [VMEM] * 17 + [HBM] * 5, [sds((here, width)...  22.2 us
    pallas_call x3, Pallas kernels, finish(): call(partial(unpack_kernel, kind, flips, len(shapes)), [SMEM, VMEM, VMEM]...  14.3 us
    unnamed x59, local copies, waits for them, and re-layouts  9.71 us
    pallas_call x1, Pallas kernels, body(): call(attention_back_kernel, [VMEM] * 3 + [HBM, VMEM, HBM], [sds((here, wi...  7.84 us
    pallas_call x1, Pallas kernels, body(): call(upper_kernel, [SMEM] + [VMEM] * 3 + [HBM] * 2, [sds((here, hidden),...  5.84 us
    ppermute x1, waiting for transfers between devices, body(): x_oth = lax.ppermute(x_own, 'seq', [(0, 1), (1, 0)])  4.76 us
  transfers between devices with their start and end apart: 29, of which 17 were waited for; matrix products, arithmetic and copies ran while one was open for 2% of the time, Pallas kernels for 15%

profile of v2, /device:TPU:0, one launch (start us, length us, event | category | flops | bytes accessed | tf_op | source)
XLA Modules:
  0.0 227.7 jit_solution(3404354286036452470)
XLA Ops:
  0.7 3.0 %collective-permute-start = (bf16[256,768]{1,0:T(8,128)(2,1)}, bf16[256,768]{1,0:T(8,128)(2,1)S(1)}, u32[]{:S(2)}, u32[]{:S(2)}) collective-permute-start(bf16[256,768]{1,0:T(8,128)(2,1)} %bitcast.14), channel_id=1, source_target_pairs={{0,1},{1,0},{2,3},{3,2},{4,5},{5,4},{6,7},{7,6},{8,9},{9,8},{10,11... | collective-permute-start | bytes 1179656 | tf_op jit(solution)/shard_map/ppermute | solution.py:471
  3.7 4.0 %shard_map.339 = (bf16[256,768]{1,0:T(8,128)(2,1)}, bf16[256,768]{1,0:T(8,128)(2,1)}, bf16[256,768]{1,0:T(8,128)(2,1)}) custom-call(bf16[256,768]{1,0:T(8,128)(2,1)} %bitcast.15, bf16[768,768]{1,0:T(8,128)(2,1)} %wq.3, f32[768]{0:T(1024)} %bq.1, bf16[768,768]{1,0:T(8,128)(2,1)} %wk.3, bf16[768,768]{1,0:T(8,128)(2,1)} %wv.3, f32[768]{0:T(1024)} %bv.3), custom_call_target="tpu_custom_call" | custom-call | tf_op jit(solution)/shard_map/pallas_call | solution.py:475
  8.3 4.8 %collective-permute-done.x_oth = bf16[256,768]{1,0:T(8,128)(2,1)S(1)} collective-permute-done((bf16[256,768]{1,0:T(8,128)(2,1)}, bf16[256,768]{1,0:T(8,128)(2,1)S(1)}, u32[]{:S(2)}, u32[]{:S(2)}) %collective-permute-start) | collective-permute-done | bytes 393248 | tf_op jit(solution)/shard_map/ppermute | solution.py:471
  13.8 22.2 %shard_map.340 = (bf16[256,768]{1,0:T(8,128)(2,1)}, f32[1,256]{1,0:T(1,128)}, bf16[12,512,256]{2,1,0:T(8,128)(2,1)}, bf16[512,768]{1,0:T(8,128)(2,1)}, bf16[512,...) custom-call(s32[8]{0:T(128)} %stack.35.scal, ...), custom_call_target="tpu_custom_call" | custom-call | tf_op jit(solution)/shard_map/pallas_call | solution.py:488
  41.2 5.8 %shard_map.341 = (bf16[256,3072]{1,0:T(8,128)(2,1)S(1)}, f32[8,768]{1,0:T(8,128)S(1)}, bf16[1536,768]{1,0:T(8,128)(2,1)S(1)}, bf16[1536,768]{1,0:T(8,128)(2,1)S(1)}) custom-call(s32[8]{0:T(128)S(1)} %copy-done.20, bf16[256,768]{1,0:T(8,128)(2,1)S(1)} %copy-done.16, bf16[256,3072]{1,0:T(8,128)(2,1)S(1)} %copy-done.8, bf16[256,768]{1,0:T(8,128)(2,1)S(1)} %copy-done.17, ...), custom_call_target="tpu_custom_call" | custom-call | tf_op jit(solution)/shard_map/pallas_call | solution.py:557
  47.8 1.8 collective-permute-start.3
  49.7 2.3 %copy-done = bf16[768,3072]{1,0:T(8,128)(2,1)S(1)} copy-done((bf16[768,3072]{1,0:T(8,128)(2,1)S(1)}, bf16[768,3072]{1,0:T(8,128)(2,1)}, u32[]{:S(2)}) %copy-start) | copy-done | bytes 4718616
  52.0 3.4 %shard_map.342 = (f32[256,768]{1,0:T(8,128)S(1)}, bf16[256,768]{1,0:T(8,128)(2,1)S(1)}, bf16[256,768]{1,0:T(8,128)(2,1)S(1)}, f32[8,768]{1,0:T(8,128)S(1)}) custom-call(f32[256,768]{1,0:T(8,128)S(1)} %copy-done.15, bf16[256,3072]{1,0:T(8,128)(2,1)S(1)} %get-tuple-element.117.grad_upper, f32[256,768]{1,0:T(8,128)S(1)} %copy-done.14, ...), custom_call_target="tpu_custom_call" | custom-call | tf_op jit(solution)/shard_map/pallas_call | solution.py:573
  57.9 7.8 %shard_map.343 = (bf16[256,768]{1,0:T(8,128)(2,1)S(1)}, bf16[768,256]{1,0:T(8,128)(2,1)S(1)}, bf16[512,768]{1,0:T(8,128)(2,1)S(1)}, bf16[512,768]{1,0:T(8,128)(2,1)S(1)}) custom-call(bf16[256,768]{1,0:T(8,128)(2,1)S(1)} %copy-done.11, bf16[512,768]{1,0:T(8,128)(2,1)S(1)} %copy-done.12, bf16[512,768]{1,0:T(8,128)(2,1)S(1)} %copy-done.13, ...), custom_call_target="tpu_custom_call" | custom-call | tf_op jit(solution)/shard_map/pallas_call | solution.py:588
  67.6 3.5 %shard_map.344 = (bf16[16,768]{1,0:T(8,128)(2,1)S(1)}, bf16[1552,768]{1,0:T(8,128)(2,1)S(1)}, bf16[1536,768]{1,0:T(8,128)(2,1)S(1)}) custom-call(s32[8]{0:T(128)S(1)} %copy-done.20, bf16[256,768]{1,0:T(8,128)(2,1)S(1)} %bitcast.17, bf16[256,768]{1,0:T(8,128)(2,1)S(1)} %copy-done.10, bf16[256,768]{1,0:T(8,128)(2,1)S(1)} %get-tuple-element.132.grad_query, ...), custom_call_target="tpu_custom_call" | custom-call | tf_op jit(solution)/shard_map/pallas_call | solution.py:607
  71.1 4.7 %collective-permute-done.5 = bf16[768,768]{1,0:T(8,128)(2,1)S(1)} collective-permute-done((bf16[768,768]{1,0:T(8,128)(2,1)S(1)}, bf16[768,768]{1,0:T(8,128)(2,1)S(1)}, u32[]{:S(2)}, u32[]{:S(2)}) %collective-permute-start.5) | collective-permute-done | bytes 1179680 | tf_op jit(solution)/shard_map/ppermute | solution.py:397
  77.8 1.8 shard_map.345
  79.6 2.2 collective-permute-done.7
  82.2 1.8 collective-permute-start.8
  87.0 13.3 %collective-permute-done.10 = bf16[384,768]{1,0:T(8,128)(2,1)S(1)} collective-permute-done((bf16[384,768]{1,0:T(8,128)(2,1)S(1)}, bf16[384,768]{1,0:T(8,128)(2,1)S(1)}, u32[]{:S(2)}, u32[]{:S(2)}) %collective-permute-start.10) | collective-permute-done | bytes 589856 | tf_op jit(solution)/shard_map/ppermute | solution.py:397
  102.1 1.7 collective-permute-start.11
  105.4 2.6 %collective-permute-start.12 = (bf16[192,768]{1,0:T(8,128)(2,1)S(1)}, bf16[192,768]{1,0:T(8,128)(2,1)S(1)}, u32[]{:S(2)}, u32[]{:S(2)}) collective-permute-start(bf16[192,768]{1,0:T(8,128)(2,1)S(1)} %add.136), channel_id=1, source_target_pairs={{0,16},{1,17},{2,18},{3,19},{4,20},{5,21},{6,22},{7,23},{8,24},{9,... | collective-permute-start | bytes 884744 | tf_op jit(solution)/shard_map/ppermute | solution.py:397
  108.5 14.1 %collective-permute-done.13 = bf16[192,768]{1,0:T(8,128)(2,1)S(1)} collective-permute-done((bf16[192,768]{1,0:T(8,128)(2,1)S(1)}, bf16[192,768]{1,0:T(8,128)(2,1)S(1)}, u32[]{:S(2)}, u32[]{:S(2)}) %collective-permute-start.13) | collective-permute-done | bytes 294944 | tf_op jit(solution)/shard_map/ppermute | solution.py:397
  123.8 11.3 %collective-permute-done.17 = bf16[192,768]{1,0:T(8,128)(2,1)S(1)} collective-permute-done((bf16[192,768]{1,0:T(8,128)(2,1)S(1)}, bf16[192,768]{1,0:T(8,128)(2,1)S(1)}, u32[]{:S(2)}, u32[]{:S(2)}) %collective-permute-start.17) | collective-permute-done | bytes 294944 | tf_op jit(solution)/shard_map/ppermute | solution.py:397
  136.6 2.1 collective-permute-start.18
  139.7 6.3 %collective-permute-done.14 = bf16[208,768]{1,0:T(8,128)(2,1)S(1)} collective-permute-done((bf16[208,768]{1,0:T(8,128)(2,1)S(1)}, bf16[208,768]{1,0:T(8,128)(2,1)S(1)}, u32[]{:S(2)}, u32[]{:S(2)}) %collective-permute-start.14) | collective-permute-done | bytes 319520 | tf_op jit(solution)/shard_map/ppermute | solution.py:397
  146.0 2.3 %collective-permute-done.18 = bf16[384,768]{1,0:T(8,128)(2,1)S(1)} collective-permute-done((bf16[384,768]{1,0:T(8,128)(2,1)S(1)}, bf16[384,768]{1,0:T(8,128)(2,1)S(1)}, u32[]{:S(2)}, u32[]{:S(2)}) %collective-permute-start.18) | collective-permute-done | bytes 589856 | tf_op jit(solution)/shard_map/ppermute | solution.py:397
  151.9 14.6 %collective-permute-done.15 = bf16[208,768]{1,0:T(8,128)(2,1)S(1)} collective-permute-done((bf16[208,768]{1,0:T(8,128)(2,1)S(1)}, bf16[208,768]{1,0:T(8,128)(2,1)S(1)}, u32[]{:S(2)}, u32[]{:S(2)}) %collective-permute-start.15) | collective-permute-done | bytes 319520 | tf_op jit(solution)/shard_map/ppermute | solution.py:397
  166.6 4.5 %collective-permute-done.22 = bf16[384,768]{1,0:T(8,128)(2,1)S(1)} collective-permute-done((bf16[384,768]{1,0:T(8,128)(2,1)S(1)}, bf16[384,768]{1,0:T(8,128)(2,1)S(1)}, u32[]{:S(2)}, u32[]{:S(2)}) %collective-permute-start.22) | collective-permute-done | bytes 589856 | tf_op jit(solution)/shard_map/ppermute | solution.py:397
  173.5 5.2 %collective-permute-done.20 = bf16[192,768]{1,0:T(8,128)(2,1)S(1)} collective-permute-done((bf16[192,768]{1,0:T(8,128)(2,1)S(1)}, bf16[192,768]{1,0:T(8,128)(2,1)S(1)}, u32[]{:S(2)}, u32[]{:S(2)}) %collective-permute-start.20) | collective-permute-done | bytes 294944 | tf_op jit(solution)/shard_map/ppermute | solution.py:397
  178.8 11.8 %collective-permute-done.25 = bf16[768,768]{1,0:T(8,128)(2,1)S(1)} collective-permute-done((bf16[768,768]{1,0:T(8,128)(2,1)S(1)}, bf16[768,768]{1,0:T(8,128)(2,1)S(1)}, u32[]{:S(2)}, u32[]{:S(2)}) %collective-permute-start.25) | collective-permute-done | bytes 1179680 | tf_op jit(solution)/shard_map/ppermute | solution.py:397
  191.4 4.4 %shard_map.346 = f32[3072,768]{1,0:T(8,128)} custom-call(s32[8]{0:T(128)S(1)} %copy-done.20, bf16[1536,768]{1,0:T(8,128)(2,1)S(1)} %constant_dynamic-update-slice_fusion.8.own, bf16[1536,768]{1,0:T(8,128)(2,1)S(1)} %collective-permute-done.24.received, bf16[1536,768]{1,0:T(8,128)(2,1)S(1)} %constant_dynamic-update-slice_fusion.12.refs_0_.own), custom_call_target="tpu_custom_call" | custom-call | tf_op jit(solution)/shard_map/pallas_call | solution.py:532
  195.8 5.0 %collective-permute-done.23 = bf16[384,768]{1,0:T(8,128)(2,1)S(1)} collective-permute-done((bf16[384,768]{1,0:T(8,128)(2,1)S(1)}, bf16[384,768]{1,0:T(8,128)(2,1)S(1)}, u32[]{:S(2)}, u32[]{:S(2)}) %collective-permute-start.23) | collective-permute-done | bytes 589856 | tf_op jit(solution)/shard_map/ppermute | solution.py:397
  201.1 4.4 %shard_map.347 = f32[768,3072]{1,0:T(8,128)} custom-call(s32[8]{0:T(128)S(1)} %copy-done.20, bf16[1536,768]{1,0:T(8,128)(2,1)S(1)} %constant_dynamic-update-slice_fusion.12.refs_0_.own, bf16[1536,768]{1,0:T(8,128)(2,1)S(1)} %collective-permute-done.27.received, bf16[768,768]{1,0:T(8,128)(2,1)S(1)} %constant_dynamic-update-slice_fusion.14.refs_0_), custom_call_target="tpu_custom_call" | custom-call | tf_op jit(solution)/shard_map/pallas_call | solution.py:532
  205.5 11.6 %collective-permute-done.26 = bf16[768,768]{1,0:T(8,128)(2,1)S(1)} collective-permute-done((bf16[768,768]{1,0:T(8,128)(2,1)S(1)}, bf16[768,768]{1,0:T(8,128)(2,1)S(1)}, u32[]{:S(2)}, u32[]{:S(2)}) %collective-permute-start.26) | collective-permute-done | bytes 1179680 | tf_op jit(solution)/shard_map/ppermute | solution.py:397
  218.7 3.4 %collective-permute-done.28.received = bf16[1536,768]{1,0:T(8,128)(2,1)} collective-permute-done((bf16[1536,768]{1,0:T(8,128)(2,1)S(1)}, bf16[1536,768]{1,0:T(8,128)(2,1)}, u32[]{:S(2)}, u32[]{:S(2)}) %collective-permute-start.28) | collective-permute-done | bytes 2359328 | tf_op jit(solution)/shard_map/ppermute | solution.py:397
  222.0 5.5 %shard_map.348 = (f32[768,768]{1,0:T(8,128)}, f32[768,768]{1,0:T(8,128)}, f32[768,768]{1,0:T(8,128)}, f32[768,768]{1,0:T(8,128)}) custom-call(s32[8]{0:T(128)S(1)} %copy-done.20, bf16[1536,768]{1,0:T(8,128)(2,1)S(1)} %constant_dynamic-update-slice_fusion.16.own.refs_0_, bf16[1536,768]{1,0:T(8,128)(2,1)} %collective-permute-done.28.received, ...), custom_call_target="tpu_custom_call" | custom-call | tf_op jit(solution)/shard_map/pallas_call | solution.py:532
  (135 shorter events, 33.1 us)
Async XLA Ops:
  0.7 12.4 %collective-permute-start = (bf16[256,768]{1,0:T(8,128)(2,1)}, bf16[256,768]{1,0:T(8,128)(2,1)S(1)}, u32[]{:S(2)}, u32[]{:S(2)}) collective-permute-start(bf16[256,768]{1,0:T(8,128)(2,1)} %bitcast.14), channel_id=1, source_target_pairs={{0,1},{1,0},{2,3},{3,2},{4,5},{5,4},{6,7},{7,6},{8,9},{9,8},{10,11... | collective-permute-start | bytes 1179656 | tf_op jit(solution)/shard_map/ppermute | solution.py:471
  13.0 23.1 %slice-start = ((s8[4718592]{0:T(1024)(128)(4,1)}), s8[4194304]{0:T(1024)(128)(4,1)S(1)}, s32[]{:S(2)}) async-start(s8[4718592]{0:T(1024)(128)(4,1)} %bitcast.12), calls=%async_computation | async-start | bytes 8388608
  13.8 22.3 %slice-start.1 = ((s8[4718592]{0:T(1024)(128)(4,1)}), s8[524288]{0:T(1024)(128)(4,1)S(1)}, s32[]{:S(2)}) async-start(s8[4718592]{0:T(1024)(128)(4,1)} %bitcast.12), calls=%async_computation.1 | async-start | bytes 1048576
  13.8 22.3 %copy-start.20 = (s32[8]{0:T(128)S(1)}, s32[8]{0:T(128)}, u32[]{:S(2)}) copy-start(s32[8]{0:T(128)} %stack.35.scal) | copy-start | bytes 100
  36.0 11.6 %collective-permute-start.1 = (bf16[1536,768]{1,0:T(8,128)(2,1)}, bf16[1536,768]{1,0:T(8,128)(2,1)S(1)}, u32[]{:S(2)}, u32[]{:S(2)}) collective-permute-start(bf16[1536,768]{1,0:T(8,128)(2,1)} %get-tuple-element.120), channel_id=1, source_target_pairs={{0,2},{1,3},{2,0},{3,1},{4,6},{5,7},{6,4},{7,5},{8,10},{9,11},{10,... | collective-permute-start | bytes 7077896 | tf_op jit(solution)/shard_map/ppermute | solution.py:397
  47.0 8.4 %collective-permute-start.2 = (bf16[1536,768]{1,0:T(8,128)(2,1)S(1)}, bf16[1536,768]{1,0:T(8,128)(2,1)S(1)}, u32[]{:S(2)}, u32[]{:S(2)}) collective-permute-start(bf16[1536,768]{1,0:T(8,128)(2,1)S(1)} %get-tuple-element.129), channel_id=1, source_target_pairs={{0,2},{1,3},{2,0},{3,1},{4,6},{5,7},{6,4},{7,5},{8,10},{9,11},{10,... | collective-permute-start | bytes 7077896 | tf_op jit(solution)/shard_map/ppermute | solution.py:397
  47.8 17.9 %collective-permute-start.3 = (bf16[768,768]{1,0:T(8,128)(2,1)S(1)}, bf16[768,768]{1,0:T(8,128)(2,1)S(1)}, u32[]{:S(2)}, u32[]{:S(2)}) collective-permute-start(bf16[768,768]{1,0:T(8,128)(2,1)S(1)} %get-tuple-element.208), channel_id=1, source_target_pairs={{0,4},{1,5},{2,3},{3,2},{4,0},{5,1},{6,7},{7,6},{8,12},{9,13},{10,... | collective-permute-start | bytes 3538952 | tf_op jit(solution)/shard_map/ppermute | solution.py:397
  55.7 20.1 %collective-permute-start.5 = (bf16[768,768]{1,0:T(8,128)(2,1)S(1)}, bf16[768,768]{1,0:T(8,128)(2,1)S(1)}, u32[]{:S(2)}, u32[]{:S(2)}) collective-permute-start(bf16[768,768]{1,0:T(8,128)(2,1)S(1)} %get-tuple-element.206), channel_id=1, source_target_pairs={{0,1},{1,0},{2,10},{3,11},{4,5},{5,4},{6,14},{7,15},{8,9},{9,8},{1... | collective-permute-start | bytes 3538952 | tf_op jit(solution)/shard_map/ppermute | solution.py:397
  65.9 11.2 %collective-permute-start.4 = (bf16[384,768]{1,0:T(8,128)(2,1)S(1)}, bf16[384,768]{1,0:T(8,128)(2,1)S(1)}, u32[]{:S(2)}, u32[]{:S(2)}) collective-permute-start(bf16[384,768]{1,0:T(8,128)(2,1)S(1)} %get-tuple-element.214), channel_id=1, source_target_pairs={{0,8},{1,9},{2,6},{3,7},{4,12},{5,13},{6,2},{7,3},{8,0},{9,1},{10,... | collective-permute-start | bytes 1769480 | tf_op jit(solution)/shard_map/ppermute | solution.py:397
  77.2 4.6 %collective-permute-start.7 = (bf16[1552,768]{1,0:T(8,128)(2,1)S(1)}, bf16[1552,768]{1,0:T(8,128)(2,1)S(1)}, u32[]{:S(2)}, u32[]{:S(2)}) collective-permute-start(bf16[1552,768]{1,0:T(8,128)(2,1)S(1)} %get-tuple-element.152), channel_id=1, source_target_pairs={{0,2},{1,3},{2,0},{3,1},{4,6},{5,7},{6,4},{7,5},{8,10},{9,11},{10,... | collective-permute-start | bytes 7151624 | tf_op jit(solution)/shard_map/ppermute | solution.py:397
  82.2 19.7 %collective-permute-start.8 = (bf16[784,768]{1,0:T(8,128)(2,1)S(1)}, bf16[784,768]{1,0:T(8,128)(2,1)S(1)}, u32[]{:S(2)}, u32[]{:S(2)}) collective-permute-start(bf16[784,768]{1,0:T(8,128)(2,1)S(1)} %pad_maximum_fusion), channel_id=1, source_target_pairs={{0,8},{1,9},{2,6},{3,7},{4,12},{5,13},{6,2},{7,3},{8,0},{9,1},{10,... | collective-permute-start | bytes 3612680 | tf_op jit(solution)/shard_map/ppermute | solution.py:397
  84.0 16.3 %collective-permute-start.10 = (bf16[384,768]{1,0:T(8,128)(2,1)S(1)}, bf16[384,768]{1,0:T(8,128)(2,1)S(1)}, u32[]{:S(2)}, u32[]{:S(2)}) collective-permute-start(bf16[384,768]{1,0:T(8,128)(2,1)S(1)} %get-tuple-element.212), channel_id=1, source_target_pairs={{0,4},{1,5},{2,3},{3,2},{4,0},{5,1},{6,7},{7,6},{8,12},{9,13},{10,... | collective-permute-start | bytes 1769480 | tf_op jit(solution)/shard_map/ppermute | solution.py:397
  85.5 14.9 %collective-permute-start.9 = (bf16[192,768]{1,0:T(8,128)(2,1)S(1)}, bf16[192,768]{1,0:T(8,128)(2,1)S(1)}, u32[]{:S(2)}, u32[]{:S(2)}) collective-permute-start(bf16[192,768]{1,0:T(8,128)(2,1)S(1)} %get-tuple-element.220), channel_id=1, source_target_pairs={{0,1},{1,0},{2,10},{3,11},{4,5},{5,4},{6,14},{7,15},{8,9},{9,8},{1... | collective-permute-start | bytes 884744 | tf_op jit(solution)/shard_map/ppermute | solution.py:397
  102.1 21.7 %collective-permute-start.11 = (bf16[400,768]{1,0:T(8,128)(2,1)S(1)}, bf16[400,768]{1,0:T(8,128)(2,1)S(1)}, u32[]{:S(2)}, u32[]{:S(2)}) collective-permute-start(bf16[400,768]{1,0:T(8,128)(2,1)S(1)} %pad_maximum_fusion.1), channel_id=1, source_target_pairs={{0,1},{1,0},{2,10},{3,11},{4,5},{5,4},{6,14},{7,15},{8,9},{9,8},{1... | collective-permute-start | bytes 1843208 | tf_op jit(solution)/shard_map/ppermute | solution.py:397
  103.8 18.8 %collective-permute-start.13 = (bf16[192,768]{1,0:T(8,128)(2,1)S(1)}, bf16[192,768]{1,0:T(8,128)(2,1)S(1)}, u32[]{:S(2)}, u32[]{:S(2)}) collective-permute-start(bf16[192,768]{1,0:T(8,128)(2,1)S(1)} %get-tuple-element.218), channel_id=1, source_target_pairs={{0,8},{1,9},{2,6},{3,7},{4,12},{5,13},{6,2},{7,3},{8,0},{9,1},{10,... | collective-permute-start | bytes 884744 | tf_op jit(solution)/shard_map/ppermute | solution.py:397
  105.4 17.9 %collective-permute-start.12 = (bf16[192,768]{1,0:T(8,128)(2,1)S(1)}, bf16[192,768]{1,0:T(8,128)(2,1)S(1)}, u32[]{:S(2)}, u32[]{:S(2)}) collective-permute-start(bf16[192,768]{1,0:T(8,128)(2,1)S(1)} %add.136), channel_id=1, source_target_pairs={{0,16},{1,17},{2,18},{3,19},{4,20},{5,21},{6,22},{7,23},{8,24},{9,... | collective-permute-start | bytes 884744 | tf_op jit(solution)/shard_map/ppermute | solution.py:397
  108.0 30.7 %collective-permute-start.6 = (bf16[256,768]{1,0:T(8,128)(2,1)S(1)}, bf16[256,768]{1,0:T(8,128)(2,1)S(1)}, u32[]{:S(2)}, u32[]{:S(2)}) collective-permute-start(bf16[256,768]{1,0:T(8,128)(2,1)S(1)} %get-tuple-element.149), channel_id=1, source_target_pairs={{0,1},{1,0},{2,3},{3,2},{4,5},{5,4},{6,7},{7,6},{8,9},{9,8},{10,11... | collective-permute-start | bytes 1179656 | tf_op jit(solution)/shard_map/ppermute | solution.py:641
  122.7 12.5 %collective-permute-start.17 = (bf16[192,768]{1,0:T(8,128)(2,1)S(1)}, bf16[192,768]{1,0:T(8,128)(2,1)S(1)}, u32[]{:S(2)}, u32[]{:S(2)}) collective-permute-start(bf16[192,768]{1,0:T(8,128)(2,1)S(1)} %add.141), channel_id=1, source_target_pairs={{0,16},{1,17},{2,18},{3,19},{4,20},{5,21},{6,22},{7,23},{8,24},{9,... | collective-permute-start | bytes 884744 | tf_op jit(solution)/shard_map/ppermute | solution.py:397
  123.4 11.9 %collective-permute-start.16 = (bf16[192,768]{1,0:T(8,128)(2,1)S(1)}, bf16[192,768]{1,0:T(8,128)(2,1)S(1)}, u32[]{:S(2)}, u32[]{:S(2)}) collective-permute-start(bf16[192,768]{1,0:T(8,128)(2,1)S(1)} %add.142), channel_id=1, source_target_pairs={{0,1},{1,0},{2,10},{3,11},{4,5},{5,4},{6,14},{7,15},{8,9},{9,8},{1... | collective-permute-start | bytes 884744 | tf_op jit(solution)/shard_map/ppermute | solution.py:397
  135.2 10.7 %collective-permute-start.19 = (bf16[192,768]{1,0:T(8,128)(2,1)S(1)}, bf16[192,768]{1,0:T(8,128)(2,1)S(1)}, u32[]{:S(2)}, u32[]{:S(2)}) collective-permute-start(bf16[192,768]{1,0:T(8,128)(2,1)S(1)} %add.148), channel_id=1, source_target_pairs={{0,8},{1,9},{2,6},{3,7},{4,12},{5,13},{6,2},{7,3},{8,0},{9,1},{10,... | collective-permute-start | bytes 884744 | tf_op jit(solution)/shard_map/ppermute | solution.py:397
  135.4 10.5 %collective-permute-start.14 = (bf16[208,768]{1,0:T(8,128)(2,1)S(1)}, bf16[208,768]{1,0:T(8,128)(2,1)S(1)}, u32[]{:S(2)}, u32[]{:S(2)}) collective-permute-start(bf16[208,768]{1,0:T(8,128)(2,1)S(1)} %pad_maximum_fusion.2), channel_id=1, source_target_pairs={{0,4},{1,5},{2,3},{3,2},{4,0},{5,1},{6,7},{7,6},{8,12},{9,13},{10,... | collective-permute-start | bytes 958472 | tf_op jit(solution)/shard_map/ppermute | solution.py:397
  136.6 11.7 %collective-permute-start.18 = (bf16[384,768]{1,0:T(8,128)(2,1)S(1)}, bf16[384,768]{1,0:T(8,128)(2,1)S(1)}, u32[]{:S(2)}, u32[]{:S(2)}) collective-permute-start(bf16[384,768]{1,0:T(8,128)(2,1)S(1)} %constant_dynamic-update-slice_fusion), channel_id=1, source_target_pairs={{0,8},{1,9},{2,6},{3,7},{4,12},{5,13},{6,2},{7,3},{8,0},{9,1},{10,... | collective-permute-start | bytes 1769480 | tf_op jit(solution)/shard_map/ppermute | solution.py:397
  148.4 23.3 %collective-permute-start.21 = (bf16[768,768]{1,0:T(8,128)(2,1)S(1)}, bf16[768,768]{1,0:T(8,128)(2,1)S(1)}, u32[]{:S(2)}, u32[]{:S(2)}) collective-permute-start(bf16[768,768]{1,0:T(8,128)(2,1)S(1)} %constant_dynamic-update-slice_fusion.4), channel_id=1, source_target_pairs={{0,4},{1,5},{2,3},{3,2},{4,0},{5,1},{6,7},{7,6},{8,12},{9,13},{10,... | collective-permute-start | bytes 3538952 | tf_op jit(solution)/shard_map/ppermute | solution.py:397
  149.6 21.4 %collective-permute-start.22 = (bf16[384,768]{1,0:T(8,128)(2,1)S(1)}, bf16[384,768]{1,0:T(8,128)(2,1)S(1)}, u32[]{:S(2)}, u32[]{:S(2)}) collective-permute-start(bf16[384,768]{1,0:T(8,128)(2,1)S(1)} %constant_dynamic-update-slice_fusion.2), channel_id=1, source_target_pairs={{0,4},{1,5},{2,3},{3,2},{4,0},{5,1},{6,7},{7,6},{8,12},{9,13},{10,... | collective-permute-start | bytes 1769480 | tf_op jit(solution)/shard_map/ppermute | solution.py:397
  150.6 15.9 %collective-permute-start.15 = (bf16[208,768]{1,0:T(8,128)(2,1)S(1)}, bf16[208,768]{1,0:T(8,128)(2,1)S(1)}, u32[]{:S(2)}, u32[]{:S(2)}) collective-permute-start(bf16[208,768]{1,0:T(8,128)(2,1)S(1)} %pad_maximum_fusion.3), channel_id=1, source_target_pairs={{0,16},{1,17},{2,18},{3,19},{4,20},{5,21},{6,22},{7,23},{8,24},{9,... | collective-permute-start | bytes 958472 | tf_op jit(solution)/shard_map/ppermute | solution.py:397
  171.1 19.4 %collective-permute-start.25 = (bf16[768,768]{1,0:T(8,128)(2,1)S(1)}, bf16[768,768]{1,0:T(8,128)(2,1)S(1)}, u32[]{:S(2)}, u32[]{:S(2)}) collective-permute-start(bf16[768,768]{1,0:T(8,128)(2,1)S(1)} %constant_dynamic-update-slice_fusion.6), channel_id=1, source_target_pairs={{0,1},{1,0},{2,10},{3,11},{4,5},{5,4},{6,14},{7,15},{8,9},{9,8},{1... | collective-permute-start | bytes 3538952 | tf_op jit(solution)/shard_map/ppermute | solution.py:397
  171.9 19.5 %collective-permute-start.24 = (bf16[1536,768]{1,0:T(8,128)(2,1)S(1)}, bf16[1536,768]{1,0:T(8,128)(2,1)S(1)}, u32[]{:S(2)}, u32[]{:S(2)}) collective-permute-start(bf16[1536,768]{1,0:T(8,128)(2,1)S(1)} %constant_dynamic-update-slice_fusion.8.own), channel_id=1, source_target_pairs={{0,2},{1,3},{2,0},{3,1},{4,6},{5,7},{6,4},{7,5},{8,10},{9,11},{10,... | collective-permute-start | bytes 7077896 | tf_op jit(solution)/shard_map/ppermute | solution.py:397
  172.0 6.8 %collective-permute-start.20 = (bf16[192,768]{1,0:T(8,128)(2,1)S(1)}, bf16[192,768]{1,0:T(8,128)(2,1)S(1)}, u32[]{:S(2)}, u32[]{:S(2)}) collective-permute-start(bf16[192,768]{1,0:T(8,128)(2,1)S(1)} %slice.212), channel_id=1, source_target_pairs={{0,4},{1,5},{2,3},{3,2},{4,0},{5,1},{6,7},{7,6},{8,12},{9,13},{10,... | collective-permute-start | bytes 884744 | tf_op jit(solution)/shard_map/ppermute | solution.py:397
  190.7 10.4 %collective-permute-start.27 = (bf16[1536,768]{1,0:T(8,128)(2,1)S(1)}, bf16[1536,768]{1,0:T(8,128)(2,1)S(1)}, u32[]{:S(2)}, u32[]{:S(2)}) collective-permute-start(bf16[1536,768]{1,0:T(8,128)(2,1)S(1)} %constant_dynamic-update-slice_fusion.12.refs_0_.own), channel_id=1, source_target_pairs={{0,2},{1,3},{2,0},{3,1},{4,6},{5,7},{6,4},{7,5},{8,10},{9,11},{10,... | collective-permute-start | bytes 7077896 | tf_op jit(solution)/shard_map/ppermute | solution.py:397
  190.8 9.9 %collective-permute-start.23 = (bf16[384,768]{1,0:T(8,128)(2,1)S(1)}, bf16[384,768]{1,0:T(8,128)(2,1)S(1)}, u32[]{:S(2)}, u32[]{:S(2)}) collective-permute-start(bf16[384,768]{1,0:T(8,128)(2,1)S(1)} %constant_dynamic-update-slice_fusion.10), channel_id=1, source_target_pairs={{0,1},{1,0},{2,10},{3,11},{4,5},{5,4},{6,14},{7,15},{8,9},{9,8},{1... | collective-permute-start | bytes 1769480 | tf_op jit(solution)/shard_map/ppermute | solution.py:397
  200.8 16.3 %collective-permute-start.26 = (bf16[768,768]{1,0:T(8,128)(2,1)S(1)}, bf16[768,768]{1,0:T(8,128)(2,1)S(1)}, u32[]{:S(2)}, u32[]{:S(2)}) collective-permute-start(bf16[768,768]{1,0:T(8,128)(2,1)S(1)} %constant_dynamic-update-slice_fusion.14.refs_0_), channel_id=1, source_target_pairs={{0,8},{1,9},{2,6},{3,7},{4,12},{5,13},{6,2},{7,3},{8,0},{9,1},{10,... | collective-permute-start | bytes 3538952 | tf_op jit(solution)/shard_map/ppermute | solution.py:397
  217.3 4.7 %collective-permute-start.28 = (bf16[1536,768]{1,0:T(8,128)(2,1)S(1)}, bf16[1536,768]{1,0:T(8,128)(2,1)}, u32[]{:S(2)}, u32[]{:S(2)}) collective-permute-start(bf16[1536,768]{1,0:T(8,128)(2,1)S(1)} %constant_dynamic-update-slice_fusion.16.own.refs_0_), channel_id=1, source_target_pairs={{0,2},{1,3},{2,0},{3,1},{4,6},{5,7},{6,4},{7,5},{8,10},{9,11},{10,... | collective-permute-start | bytes 7077896 | tf_op jit(solution)/shard_map/ppermute | solution.py:397
  (22 other events, 39.0 us)

commit v3 on v1

v3 whole, which is shorter than its diff:
```python
from functools import partial

import jax
import jax.numpy as jnp
from jax import lax
from jax.experimental import pallas as pl
from jax.experimental.pallas import tpu as pltpu
from jax.sharding import PartitionSpec as P

HD = 64
EPS = 1e-06
MASKED = -1e30
bf16 = jnp.bfloat16
f32 = jnp.float32
AXES = ("batch", "seq")
PAIR = 2 * HD
VMEM = pl.BlockSpec(memory_space=pltpu.VMEM)
SMEM = pl.BlockSpec(memory_space=pltpu.SMEM)
HBM = pl.BlockSpec(memory_space=pl.ANY)


def dot(left, right, left_dim=1, right_dim=0):
    dims = (((left_dim,), (right_dim,)), ((), ()))
    return lax.dot_general(left, right, dims, preferred_element_type=f32)


def fetch(source, target, sem):
    copy = pltpu.make_async_copy(source, target, sem)
    copy.start()
    return copy


def column(row):
    return jnp.transpose(jnp.broadcast_to(row, (128, row.shape[1])))[:, :1]


def row_of(col):
    return jnp.transpose(jnp.broadcast_to(col, (col.shape[0], 128)))[:1]


def line(ref, part=slice(None)):
    return ref[part].reshape(1, -1)


def half_masks():
    lane = lax.broadcasted_iota(jnp.int32, (1, PAIR), 1)
    low = (lane < HD).astype(f32)
    return low.astype(bf16), (1.0 - low).astype(bf16)


def store_blocks(out, at, group, values, flip, rows):
    per = values.shape[0] // rows
    for i in range(per):
        place = (group * per + i) ^ flip
        start = pl.multiple_of(place * rows, 16)
        out[at, pl.ds(start, rows), :] = values[i * rows : (i + 1) * rows]


def project_kernel(x, wq, bq, wk, wv, bv, q, k, v):
    t = x[...]
    q[...] = (dot(t, wq[...]) + line(bq)).astype(bf16) * bf16(HD**-0.5)
    k[...] = dot(t, wk[...]).astype(bf16)
    v[...] = (dot(t, wv[...]) + line(bv)).astype(bf16)


def norm_forward(values):
    centered = values - jnp.mean(values, -1, keepdims=True)
    inverse = lax.rsqrt(jnp.mean(centered * centered, -1, keepdims=True) + EPS)
    return centered * inverse, inverse


def norm_backward(grad, gain, normed, inverse):
    g = grad * gain
    return inverse * (
        g - jnp.mean(g, -1, keepdims=True) - normed * jnp.mean(g * normed, -1, keepdims=True)
    )


def middle_kernel(
    scal, x_own, x_oth, q, k_own, v_own, seg, bv, b_out, gain1, shift1, b_up, b_down,
    gain2, shift2, w_head, cot, cot_weight, wk_h, wv_h, w_out_h, w_up_h, w_down_h,
    layer_out, term, probs_h, k_all, v_all, att_t, grad_sum1, grad_attn, grad_mix, vecs,
    send_d, keep_d, send_u, keep_u,
    wk, wv, w_out, w_up, w_down, v_t, probs, active, slope, packed_d, packed_u,
    w_sems, p_sems, o_sems,
):
    loads = [
        fetch(a, b, w_sems.at[n])
        for n, (a, b) in enumerate(
            ((wk_h, wk), (wv_h, wv), (w_out_h, w_out), (w_up_h, w_up), (w_down_h, w_down))
        )
    ]
    here, width = x_own.shape
    half, core = scal[0], scal[1]
    heads = width // HD
    loads[0].wait()
    loads[1].wait()
    other = x_oth[...]
    k_all[:here] = k_own[...]
    v_all[:here] = v_own[...]
    k_all[here:] = dot(other, wk[...]).astype(bf16)
    v_all[here:] = (dot(other, wv[...]) + line(bv)).astype(bf16)
    v_t[...] = jnp.transpose(v_all[...])

    own_ids = seg[:, pl.ds(pl.multiple_of(half * here, 128), here)].astype(f32)
    oth_ids = seg[:, pl.ds(pl.multiple_of((1 - half) * here, 128), here)].astype(f32)
    key_ids = jnp.concatenate([own_ids, oth_ids], 1)
    bias = jnp.where(column(key_ids) == own_ids, 0.0, MASKED)
    masks = half_masks()
    stores = []
    for p in range(heads // 2):
        lanes = slice(p * PAIR, (p + 1) * PAIR)
        q_pair, k_pair = q[:, lanes], k_all[:, lanes]
        for e in range(2):
            h = 2 * p + e
            scores = dot(k_pair, q_pair * masks[e], 1, 1) + bias
            weights = jnp.exp(scores - jnp.max(scores, 0, keepdims=True))
            weights = weights * (1.0 / jnp.sum(weights, 0, keepdims=True))
            low = weights.astype(bf16)
            probs[h] = low
            att_t[h * HD : (h + 1) * HD] = dot(v_t[h * HD : (h + 1) * HD], low).astype(bf16)
        stores.append(fetch(probs.at[pl.ds(2 * p, 2)], probs_h.at[pl.ds(2 * p, 2)], p_sems.at[p]))

    loads[2].wait()
    attn_out = dot(att_t[...], w_out[...], 0, 0) + line(b_out)
    n1, i1 = norm_forward(x_own[...].astype(f32) + attn_out)
    first = n1 * line(gain1) + line(shift1)
    f_low = first.astype(bf16)

    loads[3].wait()
    loads[4].wait()
    down = first + line(b_down)
    chunk = 512
    for j in range(w_up.shape[1] // chunk):
        cols = slice(j * chunk, (j + 1) * chunk)
        u = dot(f_low, w_up[:, cols]) + line(b_up, cols)
        cdf = 0.5 + 0.5 * lax.erf(u * (2.0**-0.5))
        pdf = jnp.exp(-0.5 * u * u) * 0.3989422804014327
        slope[:, cols] = (cdf + u * pdf).astype(bf16)
        act = (u * cdf).astype(bf16)
        active[:, cols] = act
        down = down + dot(act, w_down[cols, :])

    n2, i2 = norm_forward(down)
    second = n2 * line(gain2) + line(shift2)
    layer_out[...] = second.astype(bf16)
    head = line(w_head).astype(f32)
    logits = jnp.sum(second * head, -1, keepdims=True)
    softplus = jnp.maximum(logits, 0.0) + jnp.log1p(jnp.exp(-jnp.abs(logits)))
    term[...] = row_of(softplus)
    grad_logits = column(cot_weight[...]) * lax.logistic(logits)
    vecs[0:1] = jnp.sum(grad_logits * second, 0, keepdims=True)
    grad_second = cot[...].astype(f32) + grad_logits * head
    vecs[1:2] = jnp.sum(grad_second * n2, 0, keepdims=True)
    vecs[2:3] = jnp.sum(grad_second, 0, keepdims=True)
    g_sum2 = norm_backward(grad_second, line(gain2), n2, i2)
    g_down = g_sum2.astype(bf16)
    vecs[3:4] = jnp.sum(g_down.astype(f32), 0, keepdims=True)
    vecs[11:] = jnp.zeros((5, width), f32)

    rows = packed_d.shape[1] // BLOCKS
    outs = []
    halves = (1 - core, core)
    for e, which in enumerate(halves):
        for j in range(2):
            start = pl.multiple_of((which * 2 + j) * width, 128)
            grad = dot(active[:, pl.ds(start, width)], g_down, 0, 0).astype(bf16)
            store_blocks(packed_d, e, j, grad, scal[3 - e], rows)
        outs.append(fetch(packed_d.at[e], (send_d, keep_d)[e], o_sems.at[e]))

    first_t = jnp.transpose(f_low)
    grad_first = g_sum2
    for e, which in enumerate(halves):
        for j in range(2):
            start = pl.multiple_of((which * 2 + j) * width, 128)
            part = pl.ds(start, width)
            g_active = dot(g_down, w_down[part, :], 1, 1)
            g_upper = (g_active * slope[:, part].astype(f32)).astype(bf16)
            vecs[pl.ds(4 + which * 2 + j, 1), :] = jnp.sum(g_upper.astype(f32), 0, keepdims=True)
            grad = dot(first_t, g_upper).astype(bf16)
            store_blocks(packed_u, e, j, grad, scal[5 - e], rows)
            grad_first = grad_first + dot(g_upper, w_up[:, part], 1, 1)
        outs.append(fetch(packed_u.at[e], (send_u, keep_u)[e], o_sems.at[2 + e]))

    vecs[8:9] = jnp.sum(grad_first * n1, 0, keepdims=True)
    vecs[9:10] = jnp.sum(grad_first, 0, keepdims=True)
    g_sum1 = norm_backward(grad_first, line(gain1), n1, i1)
    grad_sum1[...] = g_sum1
    g_attn = g_sum1.astype(bf16)
    grad_attn[...] = g_attn
    vecs[10:11] = jnp.sum(g_attn.astype(f32), 0, keepdims=True)
    grad_mix[...] = dot(g_attn, w_out[...], 1, 1).astype(bf16)
    for copy in stores + outs:
        copy.wait()


def attention_back_kernel(
    scal, x_own, x_oth, q, k_all, v_all, probs_h, att_t, grad_attn, grad_mix, vecs, after,
    grad_query, grad_key, grad_value, extra, send_h, keep_h,
    probs, k_t, x_t, query_t, vec_all, packed, p_sems, o_sems,
):
    here = x_own.shape[0]
    core, flip_keep, flip_send = scal[1], scal[6], scal[7]
    width = q.shape[1]
    heads = width // HD
    loads = [
        fetch(probs_h.at[pl.ds(2 * p, 2)], probs.at[pl.ds(2 * p, 2)], p_sems.at[p])
        for p in range(heads // 2)
    ]
    k_t[...] = jnp.transpose(k_all[...])
    masks = half_masks()
    for p in range(heads // 2):
        lanes = slice(p * PAIR, (p + 1) * PAIR)
        mix_pair, q_pair, v_pair = grad_mix[:, lanes], q[:, lanes], v_all[:, lanes]
        mixes = [mix_pair * m for m in masks]
        queries = [q_pair * m for m in masks]
        loads[p].wait()
        grads = []
        for e in range(2):
            h = 2 * p + e
            weights = probs[h].astype(f32)
            product = weights * dot(v_pair, mixes[e], 1, 1)
            delta = jnp.sum(product, 0, keepdims=True)
            grad_scores = (product - weights * delta).astype(bf16)
            grads.append(grad_scores)
            query_t[h * HD : (h + 1) * HD] = (
                dot(k_t[h * HD : (h + 1) * HD], grad_scores) * (HD**-0.5)
            ).astype(bf16)
        both = jnp.concatenate([probs[2 * p], probs[2 * p + 1]], 1)
        grad_value[:, lanes] = dot(both, jnp.concatenate(mixes, 0)).astype(bf16)
        grad_key[:, lanes] = dot(
            jnp.concatenate(grads, 1), jnp.concatenate(queries, 0)
        ).astype(bf16)
    grad_query[...] = jnp.transpose(query_t[...])
    x_t[:, :here] = jnp.transpose(x_own[...])
    x_t[:, here:] = jnp.transpose(x_oth[...])

    vec_all[...] = vecs[...]
    vec_all[11:12] = jnp.sum(grad_query[...].astype(f32), 0, keepdims=True)
    vec_all[12:13] = jnp.sum(grad_value[...].astype(f32), 0, keepdims=True)
    extra_low = vec_all[...].astype(bf16)
    extra[...] = extra_low

    total = packed.shape[1] - 16
    rows = total // BLOCKS
    packed[0, total:] = extra_low
    outs = []
    for e, which in enumerate((1 - core, core)):
        part = pl.ds(pl.multiple_of(which * (width // 2), 16), width // 2)
        for n in range(4):
            if n == 0:
                grad = dot(x_t[part, :here], query_t[...], 1, 1)
            elif n == 1:
                grad = dot(att_t[part, :], grad_attn[...])
            else:
                grad = dot(x_t[part, :], (grad_key, grad_value)[n - 2][...])
            store_blocks(packed, e, n, grad.astype(bf16), (flip_send, flip_keep)[e], rows)
        if e == 0:
            outs.append(fetch(packed.at[0], send_h, o_sems.at[0]))
        else:
            outs.append(fetch(packed.at[1, pl.ds(0, total)], keep_h, o_sems.at[1]))
    for copy in outs:
        copy.wait()


def tokens_kernel(grad_sum1, grad_query, grad_key, grad_value, wq, wk, wv, after, own, other):
    here = grad_sum1.shape[0]
    w_key, w_value = wk[...], wv[...]
    other[...] = (
        dot(grad_key[here:], w_key, 1, 1) + dot(grad_value[here:], w_value, 1, 1)
    ).astype(bf16)
    own[...] = (
        grad_sum1[...]
        + dot(grad_query[...], wq[...], 1, 1)
        + dot(grad_key[:here], w_key, 1, 1)
        + dot(grad_value[:here], w_value, 1, 1)
    )


def unpack_kernel(parts, held, scal, *refs):
    sources, refs = refs[: len(parts)], refs[len(parts) + held :]
    outs, (mark, scratch, sems) = refs[:6], refs[6:]
    mark[...] = jnp.zeros_like(mark)
    width = sources[0].shape[1]
    rows = sources[0].shape[0] // 4
    half = width // 2
    for slot, (source, (n, own, quarter)) in enumerate(zip(sources, parts)):
        which = scal[1] if own else 1 - scal[1]
        flip = scal[2 + 2 * n + (not own)]
        place = quarter ^ (flip // 4)
        for i in range(4):
            start = pl.multiple_of((i ^ (flip % 4)) * rows, 16)
            scratch[slot, i * rows : (i + 1) * rows, :] = source[pl.ds(start, rows), :].astype(f32)
        part, sem = scratch.at[slot], sems.at[slot]
        start = pl.multiple_of((which * 2 + place) * width, 128)
        if n == 0:
            fetch(part, outs[0].at[pl.ds(start, width), :], sem)
        elif n == 1:
            fetch(part, outs[1].at[:, pl.ds(start, width)], sem)
        else:
            target = pl.ds(pl.multiple_of(which * half, 16), half)
            for group in range(2):
                @pl.when(place == group)
                def _():
                    for i in range(2):
                        fetch(
                            scratch.at[slot, pl.ds(i * half, half)],
                            outs[2 + 2 * group + i].at[target, :],
                            sem,
                        )
    for slot in range(len(parts)):
        part = scratch.at[slot]
        pltpu.make_async_copy(part, part, sems.at[slot]).wait()


def call(kernel, in_specs, out_shapes, out_specs, scratch, vmem, moved=0, aliases=None):
    return pl.pallas_call(
        kernel,
        in_specs=in_specs,
        out_shape=out_shapes,
        out_specs=out_specs,
        scratch_shapes=scratch,
        input_output_aliases=aliases or {},
        compiler_params=pltpu.CompilerParams(vmem_limit_bytes=vmem * 2**20),
        cost_estimate=pl.CostEstimate(flops=0, bytes_accessed=moved, transcendentals=0),
    )


SEQ, CORE, NEAR, LINE, FAR = range(5)

STEPS = (
    ((NEAR, SEQ), (LINE, NEAR), (SEQ, LINE)),
    ((SEQ, LINE), (NEAR, SEQ), (LINE, NEAR)),
    ((LINE, NEAR), (SEQ, LINE), (NEAR, SEQ)),
)
BLOCKS = 8
UNPACK_VMEM = 56


def flip_of(index, pairs, core):
    bits = [(index >> pair[core]) & 1 for pair in pairs]
    return sum(b << (len(pairs) - 1 - n) for n, b in enumerate(bits))


def swap(values, pair, count):
    perm = [(i, i ^ (1 << pair[(i >> CORE) & 1])) for i in range(count)]
    return lax.ppermute(values, AXES, perm)


class Order:
    def __init__(self):
        self.passed = []

    def after(self, values, before):
        values, before = lax.optimization_barrier((values, before))
        self.passed += before
        return values


def halve(keep, got, extra, more_halves):
    size = keep.shape[0]
    if extra is not None:
        extra = extra + got[size:]
    if not more_halves:
        return keep + got[:size], None, extra
    half = size // 2
    send = keep[half:] + got[half:size]
    if extra is not None:
        send = jnp.concatenate([send, extra], 0)
    return keep[:half] + got[:half], send, extra


def sum_stream(order, keep, send, pairs, more, count, extra=None, before=None):
    steps = ((CORE, CORE),) + pairs
    for n, pair in enumerate(steps):
        got = swap(send, pair, count)
        if n == 2 and before is not None:
            keep, got = order.after((keep, got), [before])
        keep, send, extra = halve(keep, got, extra, n < len(steps) - 1)
    size = keep.shape[0]
    for pair in more:
        both = keep if extra is None else jnp.concatenate([keep, extra], 0)
        both = both + swap(both, pair, count)
        keep, extra = both[:size], None if extra is None else both[size:]
    for pair in reversed(pairs[1:]):
        keep = jnp.concatenate([keep, swap(keep, pair, count)], 0)
    return keep, swap(keep, pairs[0], count), swap(keep, (CORE, CORE), count), extra


def body(
    count, tokens, segment_ids, w_query, b_query, w_key, w_value, b_value, w_out, b_out,
    gain_attn, shift_attn, w_up, b_up, w_down, b_down, gain_ffn, shift_ffn, w_head, cot_out,
    cot_weight,
):
    row_count, here, width = tokens.shape
    hidden = w_up.shape[1]
    heads = width // HD
    keys = segment_ids.shape[1]
    bits = count.bit_length() - 1
    share = hidden // 2

    seq = lax.axis_index("seq")
    index = lax.axis_index("batch") * 2 + seq
    core = (index >> CORE) & 1
    more = [(b, b) for b in range(FAR, bits)]
    scal = [seq, core]
    for pairs in STEPS:
        flips = [flip_of(index, pairs, c) for c in (0, 1)]
        scal.append(jnp.where(core == 0, flips[0], flips[1]))
        scal.append(jnp.where(core == 0, flips[1], flips[0]))
    scal = jnp.stack([jnp.asarray(v, jnp.int32) for v in scal])

    x_own = tokens.reshape(here, width)
    x_oth = lax.ppermute(x_own, "seq", [(0, 1), (1, 0)])
    sds = jax.ShapeDtypeStruct
    dma = pltpu.SemaphoreType.DMA

    q, k_own, v_own = call(
        project_kernel,
        [VMEM] * 6,
        [sds((here, width), bf16)] * 3,
        [VMEM] * 3,
        [],
        56,
    )(x_own, w_query, b_query, w_key, w_value, b_value)

    square, up, down = (
        pltpu.VMEM(x, bf16) for x in ((width, width), (width, hidden), (hidden, width))
    )
    (
        layer_out, term, probs, k_all, v_all, att_t, grad_sum1, grad_attn, grad_mix, vecs,
        send_d, keep_d, send_u, keep_u,
    ) = call(
        middle_kernel,
        [SMEM] + [VMEM] * 17 + [HBM] * 5,
        [
            sds((here, width), bf16),
            sds((1, here), f32),
            sds((heads, keys, here), bf16),
            sds((keys, width), bf16),
            sds((keys, width), bf16),
            sds((width, here), bf16),
            sds((here, width), f32),
            sds((here, width), bf16),
            sds((here, width), bf16),
            sds((16, width), f32),
        ]
        + [sds((share, width), bf16)] * 4,
        [VMEM, VMEM, HBM] + [VMEM] * 7 + [HBM] * 4,
        [
            square,
            square,
            square,
            up,
            down,
            pltpu.VMEM((width, keys), bf16),
            pltpu.VMEM((heads, keys, here), bf16),
            pltpu.VMEM((here, hidden), bf16),
            pltpu.VMEM((here, hidden), bf16),
            pltpu.VMEM((2, share, width), bf16),
            pltpu.VMEM((2, share, width), bf16),
            dma((5,)),
            dma((heads // 2,)),
            dma((4,)),
        ],
        58,
    )(
        scal, x_own, x_oth, q, k_own, v_own, segment_ids, b_value, b_out, gain_attn, shift_attn,
        b_up, b_down, gain_ffn, shift_ffn, w_head, cot_out.reshape(here, width), cot_weight,
        w_key, w_value, w_out, w_up, w_down,
    )

    def unpack(parts, sources, held, after):
        targets = [(hidden, width), (width, hidden)] + [(width, width)] * 4
        *outs, mark = call(
            partial(unpack_kernel, parts, len(held) + len(after)),
            [SMEM] + [VMEM] * len(sources) + [HBM] * (len(held) + len(after)),
            [sds(x, f32) for x in targets] + [sds((8, 128), f32)],
            [pl.BlockSpec(memory_space=pltpu.HBM)] * 6 + [VMEM],
            [pltpu.VMEM((len(parts), width, width), f32), dma((len(parts),))],
            UNPACK_VMEM,
            0,
            {1 + len(sources) + i: i for i in range(len(held))},
        )(scal, *sources, *held, *after)
        return outs, mark

    grad_query, grad_key, grad_value, extra, send_q, keep_q = call(
        attention_back_kernel,
        [SMEM] + [VMEM] * 5 + [HBM] + [VMEM] * 4 + [HBM],
        [
            sds((here, width), bf16),
            sds((keys, width), bf16),
            sds((keys, width), bf16),
            sds((16, width), bf16),
            sds((share + 16, width), bf16),
            sds((share, width), bf16),
        ],
        [VMEM] * 4 + [HBM] * 2,
        [
            pltpu.VMEM((heads, keys, here), bf16),
            pltpu.VMEM((width, keys), bf16),
            pltpu.VMEM((width, keys), bf16),
            pltpu.VMEM((width, here), bf16),
            pltpu.VMEM((16, width), f32),
            pltpu.VMEM((2, share + 16, width), bf16),
            dma((heads // 2,)),
            dma((2,)),
        ],
        56,
    )(
        scal, x_own, x_oth, q, k_all, v_all, probs, att_t, grad_attn, grad_mix, vecs,
        send_u,
    )
    own, other = call(
        tokens_kernel,
        [VMEM] * 7 + [HBM],
        [sds((here, width), f32), sds((here, width), bf16)],
        [VMEM] * 2,
        [],
        16,
    )(grad_sum1, grad_query, grad_key, grad_value, w_query, w_key, w_value, extra)
    received = lax.ppermute(other, "seq", [(0, 1), (1, 0)])

    order = Order()
    sums = [
        sum_stream(order, keep_d, send_d, STEPS[0], more, count),
        sum_stream(order, keep_u, send_u, STEPS[1], more, count, None, other),
        sum_stream(order, keep_q, send_q, STEPS[2], more, count, extra),
    ]
    vec = sums[2][3].astype(f32)
    small = [vec[n] for n in range(13)] + [vec[4:8].reshape(-1)]
    small, own = lax.optimization_barrier((small, own))
    grad_tokens = own + received.astype(f32)

    early = [x for n in range(3) for x in (sums[n][0], sums[n][2])]
    parts = tuple((n, o, 0) for n in range(3) for o in (True, False))
    outs, mark = unpack(parts, early, [], [grad_tokens])
    gots = order.after([sums[n][1] for n in range(3)], [mark])
    others = [swap(got, (CORE, CORE), count) for got in gots]
    outs, mark = unpack(tuple((n, True, 1) for n in range(3)), gots, outs, [])
    outs, mark = unpack(
        tuple((n, False, 1) for n in range(3)), others, outs, order.passed + [mark]
    )
    grad_w_down, grad_w_up, grad_w_query, grad_w_out, grad_w_key, grad_w_value = outs
    return (
        layer_out.reshape(row_count, here, width),
        term.reshape(row_count, here),
        grad_tokens.reshape(row_count, here, width),
        grad_w_query,
        small[11],
        grad_w_key,
        grad_w_value,
        small[12],
        grad_w_out,
        small[10],
        small[8],
        small[9],
        grad_w_up,
        small[13],
        grad_w_down,
        small[3],
        small[1],
        small[2],
        small[0],
    )


def solution(mesh):
    rows, places = P("batch", "seq", None), P("batch", "seq")
    in_specs = (rows, P("batch", None)) + (P(),) * 16 + (rows, places)
    out_specs = (rows, places, rows) + (P(),) * 16
    count = mesh.shape["batch"] * mesh.shape["seq"]
    return jax.shard_map(
        partial(body, count), mesh=mesh, in_specs=in_specs, out_specs=out_specs, check_vma=False
    )
```

time: 261 us -> 219 us (0.84)
  Pallas kernels: 83.1 us -> 67.4 us
  local copies, waits for them, and re-layouts: 21.4 us -> 7.43 us
  waiting for transfers between devices: 114 us -> 103 us
    pallas_call x8 -> x6, Pallas kernels: 79.1 us -> 63.5 us  [the longest x1 25.8 us: body(): call(middle_kernel, [SMEM] + [VMEM] * 17 + [HBM] * 5, [sds((here, width),...]
    ppermute x30, waiting for transfers between devices: 103 us -> 91.2 us  [swap(): return lax.ppermute(values, AXES, perm)]
    reshape x10 -> x1, local copies, waits for them, and re-layouts: 12 us -> 0.61 us  [body(): small = [vec[n] for n in range(13)] + [vec[4:8].reshape(-1)]]
    ppermute x1, waiting for transfers between devices: 0.01 us -> 4.68 us  [body(): x_oth = lax.ppermute(x_own, 'seq', [(0, 1), (1, 0)])]
    ppermute x1, waiting for transfers between devices: 11.5 us -> 7.34 us  [body(): received = lax.ppermute(other, 'seq', [(0, 1), (1, 0)])]
    unnamed x21 -> x40, local copies, waits for them, and re-layouts: 5.81 us -> 4.39 us
  transfers between devices with their start and end apart: 32 -> 32, of which waited for: 19 -> 19; matrix products, arithmetic and copies ran while one was open for 10% -> 3% of each run, Pallas kernels for 21% -> 16%
where the time goes in v3:
time: 219 us
  waiting for transfers between devices  103 us (47%)
  Pallas kernels  67.4 us (31%)
  starting transfers between devices  35.1 us (16%)
  local copies, waits for them, and re-layouts  7.43 us (3%)
  other arithmetic  4.13 us (2%)
    ppermute x30, waiting for transfers between devices, swap(): return lax.ppermute(values, AXES, perm)  91.2 us
    ppermute x30, starting transfers between devices, swap(): return lax.ppermute(values, AXES, perm)  30.4 us
    pallas_call x1, Pallas kernels, body(): call(middle_kernel, [SMEM] + [VMEM] * 17 + [HBM] * 5, [sds((here, width),...  25.8 us
    pallas_call x3, Pallas kernels, unpack(): call(partial(unpack_kernel, parts, len(held) + len(after)), [SMEM] + [VME...  20.3 us
    pallas_call x1, Pallas kernels, body(): call(attention_back_kernel, [SMEM] + [VMEM] * 5 + [HBM] + [VMEM] * 4 + [H...  15.6 us
    ppermute x1, waiting for transfers between devices, body(): received = lax.ppermute(other, 'seq', [(0, 1), (1, 0)])  7.34 us
    ppermute x1, waiting for transfers between devices, body(): x_oth = lax.ppermute(x_own, 'seq', [(0, 1), (1, 0)])  4.68 us
    unnamed x40, local copies, waits for them, and re-layouts  4.39 us
  transfers between devices with their start and end apart: 32, of which 19 were waited for; matrix products, arithmetic and copies ran while one was open for 3% of the time, Pallas kernels for 16%

profile of v3, /device:TPU:0, one launch (start us, length us, event | category | flops | bytes accessed | tf_op | source)
XLA Modules:
  0.0 218.6 jit_solution(2106951176452920584)
XLA Ops:
  0.7 3.0 %collective-permute-start = (bf16[256,768]{1,0:T(8,128)(2,1)}, bf16[256,768]{1,0:T(8,128)(2,1)S(1)}, u32[]{:S(2)}, u32[]{:S(2)}) collective-permute-start(bf16[256,768]{1,0:T(8,128)(2,1)} %bitcast.12), channel_id=1, source_target_pairs={{0,1},{1,0},{2,3},{3,2},{4,5},{5,4},{6,7},{7,6},{8,9},{9,8},{10,11... | collective-permute-start | bytes 1179656 | tf_op jit(solution)/shard_map/ppermute | solution.py:414
  3.7 4.0 %shard_map.339 = (bf16[256,768]{1,0:T(8,128)(2,1)}, bf16[256,768]{1,0:T(8,128)(2,1)}, bf16[256,768]{1,0:T(8,128)(2,1)}) custom-call(bf16[256,768]{1,0:T(8,128)(2,1)} %bitcast.13, bf16[768,768]{1,0:T(8,128)(2,1)} %wq.3, f32[768]{0:T(1024)} %bq.1, bf16[768,768]{1,0:T(8,128)(2,1)} %wk.3, bf16[768,768]{1,0:T(8,128)(2,1)} %wv.3, f32[768]{0:T(1024)} %bv.3), custom_call_target="tpu_custom_call" | custom-call | tf_op jit(solution)/shard_map/pallas_call | solution.py:418
  8.3 4.7 %collective-permute-done.x_oth = bf16[256,768]{1,0:T(8,128)(2,1)S(1)} collective-permute-done((bf16[256,768]{1,0:T(8,128)(2,1)}, bf16[256,768]{1,0:T(8,128)(2,1)S(1)}, u32[]{:S(2)}, u32[]{:S(2)}) %collective-permute-start) | collective-permute-done | bytes 393248 | tf_op jit(solution)/shard_map/ppermute | solution.py:414
  13.8 25.8 %shard_map.340 = (bf16[256,768]{1,0:T(8,128)(2,1)}, f32[1,256]{1,0:T(1,128)}, bf16[12,512,256]{2,1,0:T(8,128)(2,1)}, bf16[512,768]{1,0:T(8,128)(2,1)}, bf16[512,...) custom-call(s32[8]{0:T(128)} %stack.35.scal, ...), custom_call_target="tpu_custom_call" | custom-call | tf_op jit(solution)/shard_map/pallas_call | solution.py:433
  40.2 15.6 %shard_map.341 = (bf16[256,768]{1,0:T(8,128)(2,1)}, bf16[512,768]{1,0:T(8,128)(2,1)}, bf16[512,768]{1,0:T(8,128)(2,1)}, bf16[16,768]{1,0:T(8,128)(2,1)}, bf16[15...) custom-call(s32[8]{0:T(128)} %stack.35.scal, bf16[256,768]{1,0:T(8,128)(2,1)} %bitcast.15, bf16[256,768]{1,0:T(8,128)(2,1)} %copy-done.14, ...), custom_call_target="tpu_custom_call" | custom-call | tf_op jit(solution)/shard_map/pallas_call | solution.py:487
  56.2 1.8 collective-permute-start.8
  61.5 1.9 collective-permute-start.2
  63.3 17.3 %collective-permute-done.8 = bf16[768,768]{1,0:T(8,128)(2,1)S(1)} collective-permute-done((bf16[768,768]{1,0:T(8,128)(2,1)S(1)}, bf16[768,768]{1,0:T(8,128)(2,1)S(1)}, u32[]{:S(2)}, u32[]{:S(2)}) %collective-permute-start.8) | collective-permute-done | bytes 1179680 | tf_op jit(solution)/shard_map/ppermute | solution.py:347
  80.7 1.9 collective-permute-start.9
  82.6 2.0 collective-permute-done.16
  84.7 1.8 collective-permute-start.17
  86.9 1.7 collective-permute-start.3
  88.5 8.8 %collective-permute-done.9 = bf16[384,768]{1,0:T(8,128)(2,1)S(1)} collective-permute-done((bf16[384,768]{1,0:T(8,128)(2,1)S(1)}, bf16[384,768]{1,0:T(8,128)(2,1)S(1)}, u32[]{:S(2)}, u32[]{:S(2)}) %collective-permute-start.9) | collective-permute-done | bytes 589856 | tf_op jit(solution)/shard_map/ppermute | solution.py:347
  97.4 1.6 collective-permute-start.10
  99.1 1.8 shard_map.342
  104.2 2.7 %collective-permute-start.11 = (bf16[192,768]{1,0:T(8,128)(2,1)S(1)}, bf16[192,768]{1,0:T(8,128)(2,1)S(1)}, u32[]{:S(2)}, u32[]{:S(2)}) collective-permute-start(bf16[192,768]{1,0:T(8,128)(2,1)S(1)} %fusion), channel_id=1, source_target_pairs={{0,16},{1,17},{2,18},{3,19},{4,20},{5,21},{6,22},{7,23},{8,24},{9,... | collective-permute-start | bytes 884744 | tf_op jit(solution)/shard_map/ppermute | solution.py:347
  107.0 12.1 %collective-permute-done.11 = bf16[192,768]{1,0:T(8,128)(2,1)S(1)} collective-permute-done((bf16[192,768]{1,0:T(8,128)(2,1)S(1)}, bf16[192,768]{1,0:T(8,128)(2,1)S(1)}, u32[]{:S(2)}, u32[]{:S(2)}) %collective-permute-start.11) | collective-permute-done | bytes 294944 | tf_op jit(solution)/shard_map/ppermute | solution.py:347
  119.2 1.6 collective-permute-start.12
  122.6 6.2 %collective-permute-done.12 = bf16[192,768]{1,0:T(8,128)(2,1)S(1)} collective-permute-done((bf16[192,768]{1,0:T(8,128)(2,1)S(1)}, bf16[192,768]{1,0:T(8,128)(2,1)S(1)}, u32[]{:S(2)}, u32[]{:S(2)}) %collective-permute-start.12) | collective-permute-done | bytes 294944 | tf_op jit(solution)/shard_map/ppermute | solution.py:347
  129.3 3.4 %collective-permute-start.5 = (bf16[208,768]{1,0:T(8,128)(2,1)S(1)}, bf16[208,768]{1,0:T(8,128)(2,1)S(1)}, u32[]{:S(2)}, u32[]{:S(2)}) collective-permute-start(bf16[208,768]{1,0:T(8,128)(2,1)S(1)} %pad_maximum_fusion.9), channel_id=1, source_target_pairs={{0,16},{1,17},{2,18},{3,19},{4,20},{5,21},{6,22},{7,23},{8,24},{9,... | collective-permute-start | bytes 958472 | tf_op jit(solution)/shard_map/ppermute | solution.py:347
  132.8 12.8 %collective-permute-done.19 = bf16[192,768]{1,0:T(8,128)(2,1)S(1)} collective-permute-done((bf16[192,768]{1,0:T(8,128)(2,1)S(1)}, bf16[192,768]{1,0:T(8,128)(2,1)S(1)}, u32[]{:S(2)}, u32[]{:S(2)}) %collective-permute-start.19) | collective-permute-done | bytes 294944 | tf_op jit(solution)/shard_map/ppermute | solution.py:347
  145.9 6.1 %collective-permute-done.5 = bf16[208,768]{1,0:T(8,128)(2,1)S(1)} collective-permute-done((bf16[208,768]{1,0:T(8,128)(2,1)S(1)}, bf16[208,768]{1,0:T(8,128)(2,1)S(1)}, u32[]{:S(2)}, u32[]{:S(2)}) %collective-permute-start.5) | collective-permute-done | bytes 319520 | tf_op jit(solution)/shard_map/ppermute | solution.py:347
  156.6 2.2 %collective-permute-done.23 = bf16[192,768]{1,0:T(8,128)(2,1)S(1)} collective-permute-done((bf16[192,768]{1,0:T(8,128)(2,1)S(1)}, bf16[192,768]{1,0:T(8,128)(2,1)S(1)}, u32[]{:S(2)}, u32[]{:S(2)}) %collective-permute-start.23) | collective-permute-done | bytes 294944 | tf_op jit(solution)/shard_map/ppermute | solution.py:347
  159.2 1.7 collective-permute-start.6
  162.5 2.7 %collective-permute-done.21 = bf16[384,768]{1,0:T(8,128)(2,1)S(1)} collective-permute-done((bf16[384,768]{1,0:T(8,128)(2,1)S(1)}, bf16[384,768]{1,0:T(8,128)(2,1)S(1)}, u32[]{:S(2)}, u32[]{:S(2)}) %collective-permute-start.21) | collective-permute-done | bytes 589856 | tf_op jit(solution)/shard_map/ppermute | solution.py:347
  165.3 9.9 %collective-permute-done.24 = bf16[384,768]{1,0:T(8,128)(2,1)S(1)} collective-permute-done((bf16[384,768]{1,0:T(8,128)(2,1)S(1)}, bf16[384,768]{1,0:T(8,128)(2,1)S(1)}, u32[]{:S(2)}, u32[]{:S(2)}) %collective-permute-start.24) | collective-permute-done | bytes 589856 | tf_op jit(solution)/shard_map/ppermute | solution.py:347
  176.3 7.3 %collective-permute-done.6 = bf16[256,768]{1,0:T(8,128)(2,1)S(1)} collective-permute-done((bf16[256,768]{1,0:T(8,128)(2,1)S(1)}, bf16[256,768]{1,0:T(8,128)(2,1)S(1)}, u32[]{:S(2)}, u32[]{:S(2)}) %collective-permute-start.6) | collective-permute-done | bytes 393248 | tf_op jit(solution)/shard_map/ppermute | solution.py:522
  186.2 1.7 slice_reduce_fusion
  188.9 8.9 %shard_map.343 = (f32[3072,768]{1,0:T(8,128)}, f32[768,3072]{1,0:T(8,128)}, f32[768,768]{1,0:T(8,128)}, f32[768,768]{1,0:T(8,128)}, f32[768,768]{1,0:T(8,128)}, /*index=5*/f32[768,768]{1,0:T(8,128)}, f32[8,128]{1,0:T(8,128)}) custom-call(s32[8]{0:T(128)} %stack.35.scal, bf16[768,768]{1,0:T(8,128)(2,1)} %copy-done.9, bf16[768,768]{1,0:T(8,128)(2,1)} %copy-done.18, ...), custom_call_target="tpu_custom_call" | custom-call | tf_op jit(solution)/shard_map/pallas_call | solution.py:475
  197.8 6.0 %collective-permute-done.22.refs_1_ = bf16[768,768]{1,0:T(8,128)(2,1)} collective-permute-done((bf16[768,768]{1,0:T(8,128)(2,1)S(1)}, bf16[768,768]{1,0:T(8,128)(2,1)}, u32[]{:S(2)}, u32[]{:S(2)}) %collective-permute-start.22) | collective-permute-done | bytes 1179680 | tf_op jit(solution)/shard_map/ppermute | solution.py:347
  205.3 5.7 %shard_map.344 = (f32[3072,768]{1,0:T(8,128)}, f32[768,3072]{1,0:T(8,128)}, f32[768,768]{1,0:T(8,128)}, f32[768,768]{1,0:T(8,128)}, f32[768,768]{1,0:T(8,128)}, /*index=5*/f32[768,768]{1,0:T(8,128)}, f32[8,128]{1,0:T(8,128)}) custom-call(s32[8]{0:T(128)} %stack.35.scal, ...), custom_call_target="tpu_custom_call", output_to_operand_aliasing={{0}: (4, {}), {1}: (5, {}), {2}: (6, {}), {3}: (7, {}), {4}... | custom-call | tf_op jit(solution)/shard_map/pallas_call | solution.py:475
  212.7 5.7 %shard_map.345 = (f32[3072,768]{1,0:T(8,128)}, f32[768,3072]{1,0:T(8,128)}, f32[768,768]{1,0:T(8,128)}, f32[768,768]{1,0:T(8,128)}, f32[768,768]{1,0:T(8,128)}, /*index=5*/f32[768,768]{1,0:T(8,128)}, f32[8,128]{1,0:T(8,128)}) custom-call(s32[8]{0:T(128)} %stack.35.scal, ...), custom_call_target="tpu_custom_call", output_to_operand_aliasing={{0}: (4, {}), {1}: (5, {}), {2}: (6, {}), {3}: (7, {}), {4}... | custom-call | tf_op jit(solution)/shard_map/pallas_call | solution.py:475
  (115 shorter events, 27.0 us)
Async XLA Ops:
  0.7 12.4 %collective-permute-start = (bf16[256,768]{1,0:T(8,128)(2,1)}, bf16[256,768]{1,0:T(8,128)(2,1)S(1)}, u32[]{:S(2)}, u32[]{:S(2)}) collective-permute-start(bf16[256,768]{1,0:T(8,128)(2,1)} %bitcast.12), channel_id=1, source_target_pairs={{0,1},{1,0},{2,3},{3,2},{4,5},{5,4},{6,7},{7,6},{8,9},{9,8},{10,11... | collective-permute-start | bytes 1179656 | tf_op jit(solution)/shard_map/ppermute | solution.py:414
  39.6 16.4 %collective-permute-start.7 = (bf16[1536,768]{1,0:T(8,128)(2,1)}, bf16[1536,768]{1,0:T(8,128)(2,1)S(1)}, u32[]{:S(2)}, u32[]{:S(2)}) collective-permute-start(bf16[1536,768]{1,0:T(8,128)(2,1)} %get-tuple-element.106), channel_id=1, source_target_pairs={{0,2},{1,3},{2,0},{3,1},{4,6},{5,7},{6,4},{7,5},{8,10},{9,11},{10,... | collective-permute-start | bytes 7077896 | tf_op jit(solution)/shard_map/ppermute | solution.py:347
  39.7 18.3 %collective-permute-start.15 = (bf16[1536,768]{1,0:T(8,128)(2,1)}, bf16[1536,768]{1,0:T(8,128)(2,1)S(1)}, u32[]{:S(2)}, u32[]{:S(2)}) collective-permute-start(bf16[1536,768]{1,0:T(8,128)(2,1)} %get-tuple-element.94.after), channel_id=1, source_target_pairs={{0,2},{1,3},{2,0},{3,1},{4,6},{5,7},{6,4},{7,5},{8,10},{9,11},{10,... | collective-permute-start | bytes 7077896 | tf_op jit(solution)/shard_map/ppermute | solution.py:347
  55.8 4.8 %collective-permute-start.1 = (bf16[1552,768]{1,0:T(8,128)(2,1)}, bf16[1552,768]{1,0:T(8,128)(2,1)S(1)}, u32[]{:S(2)}, u32[]{:S(2)}) collective-permute-start(bf16[1552,768]{1,0:T(8,128)(2,1)} %get-tuple-element.96), channel_id=1, source_target_pairs={{0,2},{1,3},{2,0},{3,1},{4,6},{5,7},{6,4},{7,5},{8,10},{9,11},{10,... | collective-permute-start | bytes 7151624 | tf_op jit(solution)/shard_map/ppermute | solution.py:347
  56.2 24.4 %collective-permute-start.8 = (bf16[768,768]{1,0:T(8,128)(2,1)S(1)}, bf16[768,768]{1,0:T(8,128)(2,1)S(1)}, u32[]{:S(2)}, u32[]{:S(2)}) collective-permute-start(bf16[768,768]{1,0:T(8,128)(2,1)S(1)} %get-tuple-element.159), channel_id=1, source_target_pairs={{0,4},{1,5},{2,3},{3,2},{4,0},{5,1},{6,7},{7,6},{8,12},{9,13},{10,... | collective-permute-start | bytes 3538952 | tf_op jit(solution)/shard_map/ppermute | solution.py:347
  58.2 26.3 %collective-permute-start.16 = (bf16[768,768]{1,0:T(8,128)(2,1)S(1)}, bf16[768,768]{1,0:T(8,128)(2,1)S(1)}, u32[]{:S(2)}, u32[]{:S(2)}) collective-permute-start(bf16[768,768]{1,0:T(8,128)(2,1)S(1)} %get-tuple-element.157), channel_id=1, source_target_pairs={{0,1},{1,0},{2,10},{3,11},{4,5},{5,4},{6,14},{7,15},{8,9},{9,8},{1... | collective-permute-start | bytes 3538952 | tf_op jit(solution)/shard_map/ppermute | solution.py:347
  61.5 25.1 %collective-permute-start.2 = (bf16[784,768]{1,0:T(8,128)(2,1)S(1)}, bf16[784,768]{1,0:T(8,128)(2,1)S(1)}, u32[]{:S(2)}, u32[]{:S(2)}) collective-permute-start(bf16[784,768]{1,0:T(8,128)(2,1)S(1)} %pad_maximum_fusion), channel_id=1, source_target_pairs={{0,8},{1,9},{2,6},{3,7},{4,12},{5,13},{6,2},{7,3},{8,0},{9,1},{10,... | collective-permute-start | bytes 3612680 | tf_op jit(solution)/shard_map/ppermute | solution.py:347
  80.7 16.6 %collective-permute-start.9 = (bf16[384,768]{1,0:T(8,128)(2,1)S(1)}, bf16[384,768]{1,0:T(8,128)(2,1)S(1)}, u32[]{:S(2)}, u32[]{:S(2)}) collective-permute-start(bf16[384,768]{1,0:T(8,128)(2,1)S(1)} %get-tuple-element.165), channel_id=1, source_target_pairs={{0,8},{1,9},{2,6},{3,7},{4,12},{5,13},{6,2},{7,3},{8,0},{9,1},{10,... | collective-permute-start | bytes 1769480 | tf_op jit(solution)/shard_map/ppermute | solution.py:347
  84.7 16.2 %collective-permute-start.17 = (bf16[384,768]{1,0:T(8,128)(2,1)S(1)}, bf16[384,768]{1,0:T(8,128)(2,1)S(1)}, u32[]{:S(2)}, u32[]{:S(2)}) collective-permute-start(bf16[384,768]{1,0:T(8,128)(2,1)S(1)} %get-tuple-element.162), channel_id=1, source_target_pairs={{0,4},{1,5},{2,3},{3,2},{4,0},{5,1},{6,7},{7,6},{8,12},{9,13},{10,... | collective-permute-start | bytes 1769480 | tf_op jit(solution)/shard_map/ppermute | solution.py:347
  86.9 20.1 %collective-permute-start.3 = (bf16[400,768]{1,0:T(8,128)(2,1)S(1)}, bf16[400,768]{1,0:T(8,128)(2,1)S(1)}, u32[]{:S(2)}, u32[]{:S(2)}) collective-permute-start(bf16[400,768]{1,0:T(8,128)(2,1)S(1)} %pad_maximum_fusion.4), channel_id=1, source_target_pairs={{0,1},{1,0},{2,10},{3,11},{4,5},{5,4},{6,14},{7,15},{8,9},{9,8},{1... | collective-permute-start | bytes 1843208 | tf_op jit(solution)/shard_map/ppermute | solution.py:347
  97.4 6.8 %collective-permute-start.10 = (bf16[192,768]{1,0:T(8,128)(2,1)S(1)}, bf16[192,768]{1,0:T(8,128)(2,1)S(1)}, u32[]{:S(2)}, u32[]{:S(2)}) collective-permute-start(bf16[192,768]{1,0:T(8,128)(2,1)S(1)} %slice_add_fusion.12), channel_id=1, source_target_pairs={{0,1},{1,0},{2,10},{3,11},{4,5},{5,4},{6,14},{7,15},{8,9},{9,8},{1... | collective-permute-start | bytes 884744 | tf_op jit(solution)/shard_map/ppermute | solution.py:347
  100.9 21.5 %collective-permute-start.18 = (bf16[192,768]{1,0:T(8,128)(2,1)S(1)}, bf16[192,768]{1,0:T(8,128)(2,1)S(1)}, u32[]{:S(2)}, u32[]{:S(2)}) collective-permute-start(bf16[192,768]{1,0:T(8,128)(2,1)S(1)} %slice_add_fusion.17), channel_id=1, source_target_pairs={{0,8},{1,9},{2,6},{3,7},{4,12},{5,13},{6,2},{7,3},{8,0},{9,1},{10,... | collective-permute-start | bytes 884744 | tf_op jit(solution)/shard_map/ppermute | solution.py:347
  104.2 14.9 %collective-permute-start.11 = (bf16[192,768]{1,0:T(8,128)(2,1)S(1)}, bf16[192,768]{1,0:T(8,128)(2,1)S(1)}, u32[]{:S(2)}, u32[]{:S(2)}) collective-permute-start(bf16[192,768]{1,0:T(8,128)(2,1)S(1)} %fusion), channel_id=1, source_target_pairs={{0,16},{1,17},{2,18},{3,19},{4,20},{5,21},{6,22},{7,23},{8,24},{9,... | collective-permute-start | bytes 884744 | tf_op jit(solution)/shard_map/ppermute | solution.py:347
  119.2 9.6 %collective-permute-start.12 = (bf16[192,768]{1,0:T(8,128)(2,1)S(1)}, bf16[192,768]{1,0:T(8,128)(2,1)S(1)}, u32[]{:S(2)}, u32[]{:S(2)}) collective-permute-start(bf16[192,768]{1,0:T(8,128)(2,1)S(1)} %add.141), channel_id=1, source_target_pairs={{0,1},{1,0},{2,10},{3,11},{4,5},{5,4},{6,14},{7,15},{8,9},{9,8},{1... | collective-permute-start | bytes 884744 | tf_op jit(solution)/shard_map/ppermute | solution.py:347
  120.9 8.3 %collective-permute-start.4 = (bf16[208,768]{1,0:T(8,128)(2,1)S(1)}, bf16[208,768]{1,0:T(8,128)(2,1)S(1)}, u32[]{:S(2)}, u32[]{:S(2)}) collective-permute-start(bf16[208,768]{1,0:T(8,128)(2,1)S(1)} %pad_maximum_fusion.8), channel_id=1, source_target_pairs={{0,4},{1,5},{2,3},{3,2},{4,0},{5,1},{6,7},{7,6},{8,12},{9,13},{10,... | collective-permute-start | bytes 958472 | tf_op jit(solution)/shard_map/ppermute | solution.py:347
  122.5 23.0 %collective-permute-start.19 = (bf16[192,768]{1,0:T(8,128)(2,1)S(1)}, bf16[192,768]{1,0:T(8,128)(2,1)S(1)}, u32[]{:S(2)}, u32[]{:S(2)}) collective-permute-start(bf16[192,768]{1,0:T(8,128)(2,1)S(1)} %add_add_fusion), channel_id=1, source_target_pairs={{0,16},{1,17},{2,18},{3,19},{4,20},{5,21},{6,22},{7,23},{8,24},{9,... | collective-permute-start | bytes 884744 | tf_op jit(solution)/shard_map/ppermute | solution.py:347
  128.9 16.8 %collective-permute-start.13 = (bf16[384,768]{1,0:T(8,128)(2,1)S(1)}, bf16[384,768]{1,0:T(8,128)(2,1)S(1)}, u32[]{:S(2)}, u32[]{:S(2)}) collective-permute-start(bf16[384,768]{1,0:T(8,128)(2,1)S(1)} %pad_maximum_fusion.5), channel_id=1, source_target_pairs={{0,8},{1,9},{2,6},{3,7},{4,12},{5,13},{6,2},{7,3},{8,0},{9,1},{10,... | collective-permute-start | bytes 1769480 | tf_op jit(solution)/shard_map/ppermute | solution.py:347
  129.3 22.6 %collective-permute-start.5 = (bf16[208,768]{1,0:T(8,128)(2,1)S(1)}, bf16[208,768]{1,0:T(8,128)(2,1)S(1)}, u32[]{:S(2)}, u32[]{:S(2)}) collective-permute-start(bf16[208,768]{1,0:T(8,128)(2,1)S(1)} %pad_maximum_fusion.9), channel_id=1, source_target_pairs={{0,16},{1,17},{2,18},{3,19},{4,20},{5,21},{6,22},{7,23},{8,24},{9,... | collective-permute-start | bytes 958472 | tf_op jit(solution)/shard_map/ppermute | solution.py:347
  145.6 9.4 %collective-permute-start.20 = (bf16[192,768]{1,0:T(8,128)(2,1)S(1)}, bf16[192,768]{1,0:T(8,128)(2,1)S(1)}, u32[]{:S(2)}, u32[]{:S(2)}) collective-permute-start(bf16[192,768]{1,0:T(8,128)(2,1)S(1)} %add.149), channel_id=1, source_target_pairs={{0,8},{1,9},{2,6},{3,7},{4,12},{5,13},{6,2},{7,3},{8,0},{9,1},{10,... | collective-permute-start | bytes 884744 | tf_op jit(solution)/shard_map/ppermute | solution.py:347
  145.8 38.1 %collective-permute-start.26 = (bf16[768,768]{1,0:T(8,128)(2,1)S(1)}, bf16[768,768]{1,0:T(8,128)(2,1)S(1)}, u32[]{:S(2)}, u32[]{:S(2)}) collective-permute-start(bf16[768,768]{1,0:T(8,128)(2,1)S(1)} %pad_maximum_fusion.1.refs_0_), channel_id=1, source_target_pairs={{0,2},{1,3},{2,0},{3,1},{4,6},{5,7},{6,4},{7,5},{8,10},{9,11},{10,... | collective-permute-start | bytes 3538952 | tf_op jit(solution)/shard_map/ppermute | solution.py:347
  152.0 6.8 %collective-permute-start.23 = (bf16[192,768]{1,0:T(8,128)(2,1)S(1)}, bf16[192,768]{1,0:T(8,128)(2,1)S(1)}, u32[]{:S(2)}, u32[]{:S(2)}) collective-permute-start(bf16[192,768]{1,0:T(8,128)(2,1)S(1)} %slice.258), channel_id=1, source_target_pairs={{0,4},{1,5},{2,3},{3,2},{4,0},{5,1},{6,7},{7,6},{8,12},{9,13},{10,... | collective-permute-start | bytes 884744 | tf_op jit(solution)/shard_map/ppermute | solution.py:347
  155.0 10.1 %collective-permute-start.21 = (bf16[384,768]{1,0:T(8,128)(2,1)S(1)}, bf16[384,768]{1,0:T(8,128)(2,1)S(1)}, u32[]{:S(2)}, u32[]{:S(2)}) collective-permute-start(bf16[384,768]{1,0:T(8,128)(2,1)S(1)} %pad_maximum_fusion.6), channel_id=1, source_target_pairs={{0,4},{1,5},{2,3},{3,2},{4,0},{5,1},{6,7},{7,6},{8,12},{9,13},{10,... | collective-permute-start | bytes 1769480 | tf_op jit(solution)/shard_map/ppermute | solution.py:347
  158.9 16.3 %collective-permute-start.24 = (bf16[384,768]{1,0:T(8,128)(2,1)S(1)}, bf16[384,768]{1,0:T(8,128)(2,1)S(1)}, u32[]{:S(2)}, u32[]{:S(2)}) collective-permute-start(bf16[384,768]{1,0:T(8,128)(2,1)S(1)} %pad_maximum_fusion.7), channel_id=1, source_target_pairs={{0,1},{1,0},{2,10},{3,11},{4,5},{5,4},{6,14},{7,15},{8,9},{9,8},{1... | collective-permute-start | bytes 1769480 | tf_op jit(solution)/shard_map/ppermute | solution.py:347
  159.2 24.4 %collective-permute-start.6 = (bf16[256,768]{1,0:T(8,128)(2,1)S(1)}, bf16[256,768]{1,0:T(8,128)(2,1)S(1)}, u32[]{:S(2)}, u32[]{:S(2)}) collective-permute-start(bf16[256,768]{1,0:T(8,128)(2,1)S(1)} %get-tuple-element.126.refs_9_), channel_id=1, source_target_pairs={{0,1},{1,0},{2,3},{3,2},{4,5},{5,4},{6,7},{7,6},{8,9},{9,8},{10,11... | collective-permute-start | bytes 1179656 | tf_op jit(solution)/shard_map/ppermute | solution.py:522
  161.0 36.8 %collective-permute-start.14 = (bf16[768,768]{1,0:T(8,128)(2,1)S(1)}, bf16[768,768]{1,0:T(8,128)(2,1)}, u32[]{:S(2)}, u32[]{:S(2)}) collective-permute-start(bf16[768,768]{1,0:T(8,128)(2,1)S(1)} %pad_maximum_fusion.1.refs_0_), channel_id=1, source_target_pairs={{0,4},{1,5},{2,3},{3,2},{4,0},{5,1},{6,7},{7,6},{8,12},{9,13},{10,... | collective-permute-start | bytes 3538952 | tf_op jit(solution)/shard_map/ppermute | solution.py:347
  165.2 23.6 %collective-permute-start.27 = (bf16[768,768]{1,0:T(8,128)(2,1)S(1)}, bf16[768,768]{1,0:T(8,128)(2,1)}, u32[]{:S(2)}, u32[]{:S(2)}) collective-permute-start(bf16[768,768]{1,0:T(8,128)(2,1)S(1)} %pad_maximum_fusion.2.refs_2_), channel_id=1, source_target_pairs={{0,2},{1,3},{2,0},{3,1},{4,6},{5,7},{6,4},{7,5},{8,10},{9,11},{10,... | collective-permute-start | bytes 3538952 | tf_op jit(solution)/shard_map/ppermute | solution.py:347
  176.3 12.6 %collective-permute-start.28 = (bf16[768,768]{1,0:T(8,128)(2,1)}, bf16[768,768]{1,0:T(8,128)(2,1)}, u32[]{:S(2)}, u32[]{:S(2)}) collective-permute-start(bf16[768,768]{1,0:T(8,128)(2,1)} %pad_maximum_fusion.3.refs_4_), channel_id=1, source_target_pairs={{0,2},{1,3},{2,0},{3,1},{4,6},{5,7},{6,4},{7,5},{8,10},{9,11},{10,... | collective-permute-start | bytes 3538952 | tf_op jit(solution)/shard_map/ppermute | solution.py:347
  183.6 20.2 %collective-permute-start.22 = (bf16[768,768]{1,0:T(8,128)(2,1)S(1)}, bf16[768,768]{1,0:T(8,128)(2,1)}, u32[]{:S(2)}, u32[]{:S(2)}) collective-permute-start(bf16[768,768]{1,0:T(8,128)(2,1)S(1)} %pad_maximum_fusion.2.refs_2_), channel_id=1, source_target_pairs={{0,1},{1,0},{2,10},{3,11},{4,5},{5,4},{6,14},{7,15},{8,9},{9,8},{1... | collective-permute-start | bytes 3538952 | tf_op jit(solution)/shard_map/ppermute | solution.py:347
  183.9 20.8 %collective-permute-start.25 = (bf16[768,768]{1,0:T(8,128)(2,1)}, bf16[768,768]{1,0:T(8,128)(2,1)}, u32[]{:S(2)}, u32[]{:S(2)}) collective-permute-start(bf16[768,768]{1,0:T(8,128)(2,1)} %pad_maximum_fusion.3.refs_4_), channel_id=1, source_target_pairs={{0,8},{1,9},{2,6},{3,7},{4,12},{5,13},{6,2},{7,3},{8,0},{9,1},{10,... | collective-permute-start | bytes 3538952 | tf_op jit(solution)/shard_map/ppermute | solution.py:347
  204.8 6.2 %collective-permute-start.29 = (bf16[768,768]{1,0:T(8,128)(2,1)}, bf16[768,768]{1,0:T(8,128)(2,1)S(1)}, u32[]{:S(2)}, u32[]{:S(2)}) collective-permute-start(bf16[768,768]{1,0:T(8,128)(2,1)} %collective-permute-done.14.refs_0_), channel_id=1, source_target_pairs={{0,2},{1,3},{2,0},{3,1},{4,6},{5,7},{6,4},{7,5},{8,10},{9,11},{10,... | collective-permute-start | bytes 3538952 | tf_op jit(solution)/shard_map/ppermute | solution.py:347
  204.8 6.2 %collective-permute-start.30 = (bf16[768,768]{1,0:T(8,128)(2,1)}, bf16[768,768]{1,0:T(8,128)(2,1)S(1)}, u32[]{:S(2)}, u32[]{:S(2)}) collective-permute-start(bf16[768,768]{1,0:T(8,128)(2,1)} %collective-permute-done.22.refs_1_), channel_id=1, source_target_pairs={{0,2},{1,3},{2,0},{3,1},{4,6},{5,7},{6,4},{7,5},{8,10},{9,11},{10,... | collective-permute-start | bytes 3538952 | tf_op jit(solution)/shard_map/ppermute | solution.py:347
  205.3 5.9 %collective-permute-start.31 = (bf16[768,768]{1,0:T(8,128)(2,1)}, bf16[768,768]{1,0:T(8,128)(2,1)S(1)}, u32[]{:S(2)}, u32[]{:S(2)}) collective-permute-start(bf16[768,768]{1,0:T(8,128)(2,1)} %collective-permute-done.25.refs_2_), channel_id=1, source_target_pairs={{0,2},{1,3},{2,0},{3,1},{4,6},{5,7},{6,4},{7,5},{8,10},{9,11},{10,... | collective-permute-start | bytes 3538952 | tf_op jit(solution)/shard_map/ppermute | solution.py:347
  (20 other events, 208.3 us)

commit v4 on v3

--- a/solution.py
+++ b/solution.py
@@ -334,7 +334,7 @@
     ((LINE, NEAR), (SEQ, LINE), (NEAR, SEQ)),
 )
 BLOCKS = 8
-UNPACK_VMEM = 56
+UNPACK_VMEM = 24
 
 
 def flip_of(index, pairs, core):
@@ -370,7 +370,7 @@
     return keep[:half] + got[:half], send, extra
 
 
-def sum_stream(order, keep, send, pairs, more, count, extra=None, before=None):
+def sum_stream(order, keep, send, pairs, more, count, extra=None, before=None, late=None):
     steps = ((CORE, CORE),) + pairs
     for n, pair in enumerate(steps):
         got = swap(send, pair, count)
@@ -382,8 +382,11 @@
         both = keep if extra is None else jnp.concatenate([keep, extra], 0)
         both = both + swap(both, pair, count)
         keep, extra = both[:size], None if extra is None else both[size:]
-    for pair in reversed(pairs[1:]):
-        keep = jnp.concatenate([keep, swap(keep, pair, count)], 0)
+    for n, pair in enumerate(reversed(pairs[1:])):
+        got = swap(keep, pair, count)
+        if n == 0 and late is not None:
+            keep, got = order.after((keep, got), [late])
+        keep = jnp.concatenate([keep, got], 0)
     return keep, swap(keep, pairs[0], count), swap(keep, (CORE, CORE), count), extra
 
 
@@ -521,20 +524,20 @@
     )(grad_sum1, grad_query, grad_key, grad_value, w_query, w_key, w_value, extra)
     received = lax.ppermute(other, "seq", [(0, 1), (1, 0)])
 
+    grad_tokens = own + received.astype(f32)
+
     order = Order()
     sums = [
-        sum_stream(order, keep_d, send_d, STEPS[0], more, count),
+        sum_stream(order, keep_d, send_d, STEPS[0], more, count, None, None, grad_tokens),
         sum_stream(order, keep_u, send_u, STEPS[1], more, count, None, other),
         sum_stream(order, keep_q, send_q, STEPS[2], more, count, extra),
     ]
     vec = sums[2][3].astype(f32)
     small = [vec[n] for n in range(13)] + [vec[4:8].reshape(-1)]
-    small, own = lax.optimization_barrier((small, own))
-    grad_tokens = own + received.astype(f32)
-
     early = [x for n in range(3) for x in (sums[n][0], sums[n][2])]
+    small, early = lax.optimization_barrier((small, early))
     parts = tuple((n, o, 0) for n in range(3) for o in (True, False))
-    outs, mark = unpack(parts, early, [], [grad_tokens])
+    outs, mark = unpack(parts, early, [], [])
     gots = order.after([sums[n][1] for n in range(3)], [mark])
     others = [swap(got, (CORE, CORE), count) for got in gots]
     outs, mark = unpack(tuple((n, True, 1) for n in range(3)), gots, outs, [])

time: 219 us -> 210 us (0.959)
  waiting for transfers between devices: 103 us -> 93 us
  starting transfers between devices: 35.1 us -> 38.9 us
  Pallas kernels: 67.4 us -> 63.8 us
  local copies, waits for them, and re-layouts: 7.43 us -> 9.81 us
    ppermute x1, waiting for transfers between devices: 7.34 us -> 0.01 us  [body(): received = lax.ppermute(other, 'seq', [(0, 1), (1, 0)])]
    ppermute x30, starting transfers between devices: 30.4 us -> 34.1 us  [swap(): return lax.ppermute(values, AXES, perm)]
    pallas_call x3, Pallas kernels: 20.3 us -> 16.6 us  [unpack(): call(partial(unpack_kernel, parts, len(held) + len(after)), [SMEM] + [VME...]
    ppermute x30, waiting for transfers between devices: 91.2 us -> 88.3 us  [swap(): return lax.ppermute(values, AXES, perm)]
    unnamed x40 -> x36, local copies, waits for them, and re-layouts: 4.39 us -> 5.92 us
  transfers between devices with their start and end apart: 32 -> 32, of which waited for: 19 -> 20; matrix products, arithmetic and copies ran while one was open for 3% -> 4% of each run, Pallas kernels for 16% -> 16%
where the time goes in v4:
time: 210 us; the launch traced here: 209 us
  waiting for transfers between devices  93 us (44%)
  Pallas kernels  63.8 us (30%)
  starting transfers between devices  38.9 us (19%)
  local copies, waits for them, and re-layouts  9.81 us (5%)
  other arithmetic  2.22 us (1%)
    ppermute x30, waiting for transfers between devices, swap(): return lax.ppermute(values, AXES, perm)  88.3 us
    ppermute x30, starting transfers between devices, swap(): return lax.ppermute(values, AXES, perm)  34.1 us
    pallas_call x1, Pallas kernels, body(): call(middle_kernel, [SMEM] + [VMEM] * 17 + [HBM] * 5, [sds((here, width),...  25.8 us
    pallas_call x3, Pallas kernels, unpack(): call(partial(unpack_kernel, parts, len(held) + len(after)), [SMEM] + [VME...  16.6 us
    pallas_call x1, Pallas kernels, body(): call(attention_back_kernel, [SMEM] + [VMEM] * 5 + [HBM] + [VMEM] * 4 + [H...  15.7 us
    unnamed x36, local copies, waits for them, and re-layouts  5.92 us
    ppermute x1, waiting for transfers between devices, body(): x_oth = lax.ppermute(x_own, 'seq', [(0, 1), (1, 0)])  4.7 us
  transfers between devices with their start and end apart: 32, of which 20 were waited for; matrix products, arithmetic and copies ran while one was open for 4% of the time, Pallas kernels for 16%

profile of v4, /device:TPU:0, one launch (start us, length us, event | category | flops | bytes accessed | tf_op | source)
XLA Modules:
  0.0 209.0 jit_solution(3006561129876071483)
XLA Ops:
  0.7 3.0 %collective-permute-start = (bf16[256,768]{1,0:T(8,128)(2,1)}, bf16[256,768]{1,0:T(8,128)(2,1)S(1)}, u32[]{:S(2)}, u32[]{:S(2)}) collective-permute-start(bf16[256,768]{1,0:T(8,128)(2,1)} %bitcast.13), channel_id=1, source_target_pairs={{0,1},{1,0},{2,3},{3,2},{4,5},{5,4},{6,7},{7,6},{8,9},{9,8},{10,11... | collective-permute-start | bytes 1179656 | tf_op jit(solution)/shard_map/ppermute | solution.py:417
  3.7 4.0 %shard_map.339 = (bf16[256,768]{1,0:T(8,128)(2,1)}, bf16[256,768]{1,0:T(8,128)(2,1)}, bf16[256,768]{1,0:T(8,128)(2,1)}) custom-call(bf16[256,768]{1,0:T(8,128)(2,1)} %bitcast.14, bf16[768,768]{1,0:T(8,128)(2,1)} %wq.3, f32[768]{0:T(1024)} %bq.1, bf16[768,768]{1,0:T(8,128)(2,1)} %wk.3, bf16[768,768]{1,0:T(8,128)(2,1)} %wv.3, f32[768]{0:T(1024)} %bv.3), custom_call_target="tpu_custom_call" | custom-call | tf_op jit(solution)/shard_map/pallas_call | solution.py:421
  8.3 4.7 %collective-permute-done.x_oth = bf16[256,768]{1,0:T(8,128)(2,1)S(1)} collective-permute-done((bf16[256,768]{1,0:T(8,128)(2,1)}, bf16[256,768]{1,0:T(8,128)(2,1)S(1)}, u32[]{:S(2)}, u32[]{:S(2)}) %collective-permute-start) | collective-permute-done | bytes 393248 | tf_op jit(solution)/shard_map/ppermute | solution.py:417
  13.8 25.8 %shard_map.340 = (bf16[256,768]{1,0:T(8,128)(2,1)}, f32[1,256]{1,0:T(1,128)}, bf16[12,512,256]{2,1,0:T(8,128)(2,1)}, bf16[512,768]{1,0:T(8,128)(2,1)}, bf16[512,...) custom-call(s32[8]{0:T(128)} %stack.35.scal, ...), custom_call_target="tpu_custom_call" | custom-call | tf_op jit(solution)/shard_map/pallas_call | solution.py:436
  40.2 15.7 %shard_map.341 = (bf16[256,768]{1,0:T(8,128)(2,1)}, bf16[512,768]{1,0:T(8,128)(2,1)}, bf16[512,768]{1,0:T(8,128)(2,1)}, bf16[16,768]{1,0:T(8,128)(2,1)}, bf16[15...) custom-call(s32[8]{0:T(128)} %stack.35.scal, bf16[256,768]{1,0:T(8,128)(2,1)} %bitcast.16, bf16[256,768]{1,0:T(8,128)(2,1)} %copy-done.15, ...), custom_call_target="tpu_custom_call" | custom-call | tf_op jit(solution)/shard_map/pallas_call | solution.py:490
  56.3 1.8 collective-permute-start.3
  61.6 1.9 collective-permute-start.19
  63.7 1.8 shard_map.342
  65.5 1.8 collective-permute-start.1
  67.3 13.3 %collective-permute-done.3 = bf16[768,768]{1,0:T(8,128)(2,1)S(1)} collective-permute-done((bf16[768,768]{1,0:T(8,128)(2,1)S(1)}, bf16[768,768]{1,0:T(8,128)(2,1)S(1)}, u32[]{:S(2)}, u32[]{:S(2)}) %collective-permute-start.3) | collective-permute-done | bytes 1179680 | tf_op jit(solution)/shard_map/ppermute | solution.py:347
  80.8 1.9 collective-permute-start.4
  82.6 4.7 %collective-permute-done.11 = bf16[768,768]{1,0:T(8,128)(2,1)S(1)} collective-permute-done((bf16[768,768]{1,0:T(8,128)(2,1)S(1)}, bf16[768,768]{1,0:T(8,128)(2,1)S(1)}, u32[]{:S(2)}, u32[]{:S(2)}) %collective-permute-start.11) | collective-permute-done | bytes 1179680 | tf_op jit(solution)/shard_map/ppermute | solution.py:347
  90.7 6.8 %collective-permute-done.4 = bf16[384,768]{1,0:T(8,128)(2,1)S(1)} collective-permute-done((bf16[384,768]{1,0:T(8,128)(2,1)S(1)}, bf16[384,768]{1,0:T(8,128)(2,1)S(1)}, u32[]{:S(2)}, u32[]{:S(2)}) %collective-permute-start.4) | collective-permute-done | bytes 589856 | tf_op jit(solution)/shard_map/ppermute | solution.py:347
  101.0 8.2 %collective-permute-done.5 = bf16[192,768]{1,0:T(8,128)(2,1)S(1)} collective-permute-done((bf16[192,768]{1,0:T(8,128)(2,1)S(1)}, bf16[192,768]{1,0:T(8,128)(2,1)S(1)}, u32[]{:S(2)}, u32[]{:S(2)}) %collective-permute-start.5) | collective-permute-done | bytes 294944 | tf_op jit(solution)/shard_map/ppermute | solution.py:347
  109.2 2.9 %collective-permute-start.6 = (bf16[192,768]{1,0:T(8,128)(2,1)S(1)}, bf16[192,768]{1,0:T(8,128)(2,1)S(1)}, u32[]{:S(2)}, u32[]{:S(2)}) collective-permute-start(bf16[192,768]{1,0:T(8,128)(2,1)S(1)} %fusion), channel_id=1, source_target_pairs={{0,16},{1,17},{2,18},{3,19},{4,20},{5,21},{6,22},{7,23},{8,24},{9,... | collective-permute-start | bytes 884744 | tf_op jit(solution)/shard_map/ppermute | solution.py:347
  112.1 9.2 %collective-permute-done.6 = bf16[192,768]{1,0:T(8,128)(2,1)S(1)} collective-permute-done((bf16[192,768]{1,0:T(8,128)(2,1)S(1)}, bf16[192,768]{1,0:T(8,128)(2,1)S(1)}, u32[]{:S(2)}, u32[]{:S(2)}) %collective-permute-start.6) | collective-permute-done | bytes 294944 | tf_op jit(solution)/shard_map/ppermute | solution.py:347
  123.0 5.0 %collective-permute-start.21 = (bf16[208,768]{1,0:T(8,128)(2,1)S(1)}, bf16[208,768]{1,0:T(8,128)(2,1)S(1)}, u32[]{:S(2)}, u32[]{:S(2)}) collective-permute-start(bf16[208,768]{1,0:T(8,128)(2,1)S(1)} %pad_maximum_fusion.7), channel_id=1, source_target_pairs={{0,4},{1,5},{2,3},{3,2},{4,0},{5,1},{6,7},{7,6},{8,12},{9,13},{10,... | collective-permute-start | bytes 958472 | tf_op jit(solution)/shard_map/ppermute | solution.py:347
  128.9 4.1 %collective-permute-start.8 = (bf16[384,768]{1,0:T(8,128)(2,1)S(1)}, bf16[384,768]{1,0:T(8,128)(2,1)S(1)}, u32[]{:S(2)}, u32[]{:S(2)}) collective-permute-start(bf16[384,768]{1,0:T(8,128)(2,1)S(1)} %pad_maximum_fusion.4), channel_id=1, source_target_pairs={{0,8},{1,9},{2,6},{3,7},{4,12},{5,13},{6,2},{7,3},{8,0},{9,1},{10,... | collective-permute-start | bytes 1769480 | tf_op jit(solution)/shard_map/ppermute | solution.py:347
  133.0 3.4 %collective-permute-done.21 = bf16[208,768]{1,0:T(8,128)(2,1)S(1)} collective-permute-done((bf16[208,768]{1,0:T(8,128)(2,1)S(1)}, bf16[208,768]{1,0:T(8,128)(2,1)S(1)}, u32[]{:S(2)}, u32[]{:S(2)}) %collective-permute-start.21) | collective-permute-done | bytes 319520 | tf_op jit(solution)/shard_map/ppermute | solution.py:347
  136.6 8.6 %collective-permute-done.14 = bf16[192,768]{1,0:T(8,128)(2,1)S(1)} collective-permute-done((bf16[192,768]{1,0:T(8,128)(2,1)S(1)}, bf16[192,768]{1,0:T(8,128)(2,1)S(1)}, u32[]{:S(2)}, u32[]{:S(2)}) %collective-permute-start.14) | collective-permute-done | bytes 294944 | tf_op jit(solution)/shard_map/ppermute | solution.py:347
  148.1 4.0 %collective-permute-done.22 = bf16[208,768]{1,0:T(8,128)(2,1)S(1)} collective-permute-done((bf16[208,768]{1,0:T(8,128)(2,1)S(1)}, bf16[208,768]{1,0:T(8,128)(2,1)S(1)}, u32[]{:S(2)}, u32[]{:S(2)}) %collective-permute-start.22) | collective-permute-done | bytes 319520 | tf_op jit(solution)/shard_map/ppermute | solution.py:347
  152.3 2.9 %collective-permute-done.15 = bf16[192,768]{1,0:T(8,128)(2,1)S(1)} collective-permute-done((bf16[192,768]{1,0:T(8,128)(2,1)S(1)}, bf16[192,768]{1,0:T(8,128)(2,1)S(1)}, u32[]{:S(2)}, u32[]{:S(2)}) %collective-permute-start.15) | collective-permute-done | bytes 294944 | tf_op jit(solution)/shard_map/ppermute | solution.py:347
  155.3 3.7 %collective-permute-done.23 = bf16[192,768]{1,0:T(8,128)(2,1)S(1)} collective-permute-done((bf16[192,768]{1,0:T(8,128)(2,1)S(1)}, bf16[192,768]{1,0:T(8,128)(2,1)S(1)}, u32[]{:S(2)}, u32[]{:S(2)}) %collective-permute-start.23) | collective-permute-done | bytes 294944 | tf_op jit(solution)/shard_map/ppermute | solution.py:347
  159.8 5.6 %collective-permute-done.16 = bf16[384,768]{1,0:T(8,128)(2,1)S(1)} collective-permute-done((bf16[384,768]{1,0:T(8,128)(2,1)S(1)}, bf16[384,768]{1,0:T(8,128)(2,1)S(1)}, u32[]{:S(2)}, u32[]{:S(2)}) %collective-permute-start.16) | collective-permute-done | bytes 589856 | tf_op jit(solution)/shard_map/ppermute | solution.py:347
  165.5 3.5 %collective-permute-done.24 = bf16[384,768]{1,0:T(8,128)(2,1)S(1)} collective-permute-done((bf16[384,768]{1,0:T(8,128)(2,1)S(1)}, bf16[384,768]{1,0:T(8,128)(2,1)S(1)}, u32[]{:S(2)}, u32[]{:S(2)}) %collective-permute-start.24) | collective-permute-done | bytes 589856 | tf_op jit(solution)/shard_map/ppermute | solution.py:347
  169.2 2.4 %collective-permute-start.9 = (bf16[768,768]{1,0:T(8,128)(2,1)}, bf16[768,768]{1,0:T(8,128)(2,1)}, u32[]{:S(2)}, u32[]{:S(2)}) collective-permute-start(bf16[768,768]{1,0:T(8,128)(2,1)} %constant_dynamic-update-slice_fusion.refs_0_), channel_id=1, source_target_pairs={{0,4},{1,5},{2,3},{3,2},{4,0},{5,1},{6,7},{7,6},{8,12},{9,13},{10,... | collective-permute-start | bytes 3538952 | tf_op jit(solution)/shard_map/ppermute | solution.py:347
  171.6 1.7 collective-permute-start.17
  175.6 1.7 slice_reduce_fusion
  178.6 7.3 %shard_map.343 = (f32[3072,768]{1,0:T(8,128)}, f32[768,3072]{1,0:T(8,128)}, f32[768,768]{1,0:T(8,128)}, f32[768,768]{1,0:T(8,128)}, f32[768,768]{1,0:T(8,128)}, ...) custom-call(s32[8]{0:T(128)S(1)} %copy-done.11, bf16[768,768]{1,0:T(8,128)(2,1)} %constant_dynamic-update-slice_fusion.refs_0_, ...), custom_call_target="tpu_custom_call" | custom-call | tf_op jit(solution)/shard_map/pallas_call | solution.py:478
  185.9 10.8 %collective-permute-done.9.refs_0_ = bf16[768,768]{1,0:T(8,128)(2,1)} collective-permute-done((bf16[768,768]{1,0:T(8,128)(2,1)}, bf16[768,768]{1,0:T(8,128)(2,1)}, u32[]{:S(2)}, u32[]{:S(2)}) %collective-permute-start.9) | collective-permute-done | bytes 1179680 | tf_op jit(solution)/shard_map/ppermute | solution.py:347
  199.1 5.1 %shard_map.344 = (f32[3072,768]{1,0:T(8,128)}, f32[768,3072]{1,0:T(8,128)}, f32[768,768]{1,0:T(8,128)}, f32[768,768]{1,0:T(8,128)}, f32[768,768]{1,0:T(8,128)}, ...) custom-call(s32[8]{0:T(128)S(1)} %copy-done.11, ...), custom_call_target="tpu_custom_call", output_to_operand_aliasing={{0}: (4, {}), {1}: (5, {}), {2}: (6, {}), {3}: (7, {}), {4}... | custom-call | tf_op jit(solution)/shard_map/pallas_call | solution.py:478
  204.6 4.2 %shard_map.345 = (f32[3072,768]{1,0:T(8,128)}, f32[768,3072]{1,0:T(8,128)}, f32[768,768]{1,0:T(8,128)}, f32[768,768]{1,0:T(8,128)}, f32[768,768]{1,0:T(8,128)}, /*index=5*/f32[768,768]{1,0:T(8,128)}, f32[8,128]{1,0:T(8,128)}) custom-call(s32[8]{0:T(128)S(1)} %copy-done.11, ...), custom_call_target="tpu_custom_call", output_to_operand_aliasing={{0}: (4, {}), {1}: (5, {}), {2}: (6, {}), {3}: (7, {}), {4}... | custom-call | tf_op jit(solution)/shard_map/pallas_call | solution.py:478
  (111 shorter events, 26.5 us)
Async XLA Ops:
  0.7 12.4 %collective-permute-start = (bf16[256,768]{1,0:T(8,128)(2,1)}, bf16[256,768]{1,0:T(8,128)(2,1)S(1)}, u32[]{:S(2)}, u32[]{:S(2)}) collective-permute-start(bf16[256,768]{1,0:T(8,128)(2,1)} %bitcast.13), channel_id=1, source_target_pairs={{0,1},{1,0},{2,3},{3,2},{4,5},{5,4},{6,7},{7,6},{8,9},{9,8},{10,11... | collective-permute-start | bytes 1179656 | tf_op jit(solution)/shard_map/ppermute | solution.py:417
  39.6 16.4 %collective-permute-start.2 = (bf16[1536,768]{1,0:T(8,128)(2,1)}, bf16[1536,768]{1,0:T(8,128)(2,1)S(1)}, u32[]{:S(2)}, u32[]{:S(2)}) collective-permute-start(bf16[1536,768]{1,0:T(8,128)(2,1)} %get-tuple-element.111), channel_id=1, source_target_pairs={{0,2},{1,3},{2,0},{3,1},{4,6},{5,7},{6,4},{7,5},{8,10},{9,11},{10,... | collective-permute-start | bytes 7077896 | tf_op jit(solution)/shard_map/ppermute | solution.py:347
  39.7 18.4 %collective-permute-start.10 = (bf16[1536,768]{1,0:T(8,128)(2,1)}, bf16[1536,768]{1,0:T(8,128)(2,1)S(1)}, u32[]{:S(2)}, u32[]{:S(2)}) collective-permute-start(bf16[1536,768]{1,0:T(8,128)(2,1)} %get-tuple-element.103.after), channel_id=1, source_target_pairs={{0,2},{1,3},{2,0},{3,1},{4,6},{5,7},{6,4},{7,5},{8,10},{9,11},{10,... | collective-permute-start | bytes 7077896 | tf_op jit(solution)/shard_map/ppermute | solution.py:347
  55.9 4.8 %collective-permute-start.18 = (bf16[1552,768]{1,0:T(8,128)(2,1)}, bf16[1552,768]{1,0:T(8,128)(2,1)S(1)}, u32[]{:S(2)}, u32[]{:S(2)}) collective-permute-start(bf16[1552,768]{1,0:T(8,128)(2,1)} %get-tuple-element.118), channel_id=1, source_target_pairs={{0,2},{1,3},{2,0},{3,1},{4,6},{5,7},{6,4},{7,5},{8,10},{9,11},{10,... | collective-permute-start | bytes 7151624 | tf_op jit(solution)/shard_map/ppermute | solution.py:347
  56.3 24.4 %collective-permute-start.3 = (bf16[768,768]{1,0:T(8,128)(2,1)S(1)}, bf16[768,768]{1,0:T(8,128)(2,1)S(1)}, u32[]{:S(2)}, u32[]{:S(2)}) collective-permute-start(bf16[768,768]{1,0:T(8,128)(2,1)S(1)} %get-tuple-element.175), channel_id=1, source_target_pairs={{0,4},{1,5},{2,3},{3,2},{4,0},{5,1},{6,7},{7,6},{8,12},{9,13},{10,... | collective-permute-start | bytes 3538952 | tf_op jit(solution)/shard_map/ppermute | solution.py:347
  58.3 29.0 %collective-permute-start.11 = (bf16[768,768]{1,0:T(8,128)(2,1)S(1)}, bf16[768,768]{1,0:T(8,128)(2,1)S(1)}, u32[]{:S(2)}, u32[]{:S(2)}) collective-permute-start(bf16[768,768]{1,0:T(8,128)(2,1)S(1)} %get-tuple-element.173), channel_id=1, source_target_pairs={{0,1},{1,0},{2,10},{3,11},{4,5},{5,4},{6,14},{7,15},{8,9},{9,8},{1... | collective-permute-start | bytes 3538952 | tf_op jit(solution)/shard_map/ppermute | solution.py:347
  61.6 27.3 %collective-permute-start.19 = (bf16[784,768]{1,0:T(8,128)(2,1)S(1)}, bf16[784,768]{1,0:T(8,128)(2,1)S(1)}, u32[]{:S(2)}, u32[]{:S(2)}) collective-permute-start(bf16[784,768]{1,0:T(8,128)(2,1)S(1)} %pad_maximum_fusion), channel_id=1, source_target_pairs={{0,8},{1,9},{2,6},{3,7},{4,12},{5,13},{6,2},{7,3},{8,0},{9,1},{10,... | collective-permute-start | bytes 3612680 | tf_op jit(solution)/shard_map/ppermute | solution.py:347
  65.5 33.7 %collective-permute-start.1 = (bf16[256,768]{1,0:T(8,128)(2,1)S(1)}, bf16[256,768]{1,0:T(8,128)(2,1)S(1)}, u32[]{:S(2)}, u32[]{:S(2)}) collective-permute-start(bf16[256,768]{1,0:T(8,128)(2,1)S(1)} %get-tuple-element.142.refs_10_), channel_id=1, source_target_pairs={{0,1},{1,0},{2,3},{3,2},{4,5},{5,4},{6,7},{7,6},{8,9},{9,8},{10,11... | collective-permute-start | bytes 1179656 | tf_op jit(solution)/shard_map/ppermute | solution.py:525
  80.8 16.7 %collective-permute-start.4 = (bf16[384,768]{1,0:T(8,128)(2,1)S(1)}, bf16[384,768]{1,0:T(8,128)(2,1)S(1)}, u32[]{:S(2)}, u32[]{:S(2)}) collective-permute-start(bf16[384,768]{1,0:T(8,128)(2,1)S(1)} %get-tuple-element.181), channel_id=1, source_target_pairs={{0,8},{1,9},{2,6},{3,7},{4,12},{5,13},{6,2},{7,3},{8,0},{9,1},{10,... | collective-permute-start | bytes 1769480 | tf_op jit(solution)/shard_map/ppermute | solution.py:347
  87.4 11.8 %collective-permute-start.12 = (bf16[384,768]{1,0:T(8,128)(2,1)S(1)}, bf16[384,768]{1,0:T(8,128)(2,1)S(1)}, u32[]{:S(2)}, u32[]{:S(2)}) collective-permute-start(bf16[384,768]{1,0:T(8,128)(2,1)S(1)} %get-tuple-element.178), channel_id=1, source_target_pairs={{0,4},{1,5},{2,3},{3,2},{4,0},{5,1},{6,7},{7,6},{8,12},{9,13},{10,... | collective-permute-start | bytes 1769480 | tf_op jit(solution)/shard_map/ppermute | solution.py:347
  89.1 22.9 %collective-permute-start.20 = (bf16[400,768]{1,0:T(8,128)(2,1)S(1)}, bf16[400,768]{1,0:T(8,128)(2,1)S(1)}, u32[]{:S(2)}, u32[]{:S(2)}) collective-permute-start(bf16[400,768]{1,0:T(8,128)(2,1)S(1)} %pad_maximum_fusion.3), channel_id=1, source_target_pairs={{0,1},{1,0},{2,10},{3,11},{4,5},{5,4},{6,14},{7,15},{8,9},{9,8},{1... | collective-permute-start | bytes 1843208 | tf_op jit(solution)/shard_map/ppermute | solution.py:347
  97.5 11.6 %collective-permute-start.5 = (bf16[192,768]{1,0:T(8,128)(2,1)S(1)}, bf16[192,768]{1,0:T(8,128)(2,1)S(1)}, u32[]{:S(2)}, u32[]{:S(2)}) collective-permute-start(bf16[192,768]{1,0:T(8,128)(2,1)S(1)} %slice_add_fusion.15), channel_id=1, source_target_pairs={{0,1},{1,0},{2,10},{3,11},{4,5},{5,4},{6,14},{7,15},{8,9},{9,8},{1... | collective-permute-start | bytes 884744 | tf_op jit(solution)/shard_map/ppermute | solution.py:347
  99.3 28.7 %collective-permute-start.13 = (bf16[192,768]{1,0:T(8,128)(2,1)S(1)}, bf16[192,768]{1,0:T(8,128)(2,1)S(1)}, u32[]{:S(2)}, u32[]{:S(2)}) collective-permute-start(bf16[192,768]{1,0:T(8,128)(2,1)S(1)} %slice_add_fusion.17), channel_id=1, source_target_pairs={{0,8},{1,9},{2,6},{3,7},{4,12},{5,13},{6,2},{7,3},{8,0},{9,1},{10,... | collective-permute-start | bytes 884744 | tf_op jit(solution)/shard_map/ppermute | solution.py:347
  109.2 12.1 %collective-permute-start.6 = (bf16[192,768]{1,0:T(8,128)(2,1)S(1)}, bf16[192,768]{1,0:T(8,128)(2,1)S(1)}, u32[]{:S(2)}, u32[]{:S(2)}) collective-permute-start(bf16[192,768]{1,0:T(8,128)(2,1)S(1)} %fusion), channel_id=1, source_target_pairs={{0,16},{1,17},{2,18},{3,19},{4,20},{5,21},{6,22},{7,23},{8,24},{9,... | collective-permute-start | bytes 884744 | tf_op jit(solution)/shard_map/ppermute | solution.py:347
  121.4 7.5 %collective-permute-start.7 = (bf16[192,768]{1,0:T(8,128)(2,1)S(1)}, bf16[192,768]{1,0:T(8,128)(2,1)S(1)}, u32[]{:S(2)}, u32[]{:S(2)}) collective-permute-start(bf16[192,768]{1,0:T(8,128)(2,1)S(1)} %add.129), channel_id=1, source_target_pairs={{0,1},{1,0},{2,10},{3,11},{4,5},{5,4},{6,14},{7,15},{8,9},{9,8},{1... | collective-permute-start | bytes 884744 | tf_op jit(solution)/shard_map/ppermute | solution.py:347
  123.0 13.5 %collective-permute-start.21 = (bf16[208,768]{1,0:T(8,128)(2,1)S(1)}, bf16[208,768]{1,0:T(8,128)(2,1)S(1)}, u32[]{:S(2)}, u32[]{:S(2)}) collective-permute-start(bf16[208,768]{1,0:T(8,128)(2,1)S(1)} %pad_maximum_fusion.7), channel_id=1, source_target_pairs={{0,4},{1,5},{2,3},{3,2},{4,0},{5,1},{6,7},{7,6},{8,12},{9,13},{10,... | collective-permute-start | bytes 958472 | tf_op jit(solution)/shard_map/ppermute | solution.py:347
  128.0 17.2 %collective-permute-start.14 = (bf16[192,768]{1,0:T(8,128)(2,1)S(1)}, bf16[192,768]{1,0:T(8,128)(2,1)S(1)}, u32[]{:S(2)}, u32[]{:S(2)}) collective-permute-start(bf16[192,768]{1,0:T(8,128)(2,1)S(1)} %add_add_fusion), channel_id=1, source_target_pairs={{0,16},{1,17},{2,18},{3,19},{4,20},{5,21},{6,22},{7,23},{8,24},{9,... | collective-permute-start | bytes 884744 | tf_op jit(solution)/shard_map/ppermute | solution.py:347
  128.9 18.3 %collective-permute-start.8 = (bf16[384,768]{1,0:T(8,128)(2,1)S(1)}, bf16[384,768]{1,0:T(8,128)(2,1)S(1)}, u32[]{:S(2)}, u32[]{:S(2)}) collective-permute-start(bf16[384,768]{1,0:T(8,128)(2,1)S(1)} %pad_maximum_fusion.4), channel_id=1, source_target_pairs={{0,8},{1,9},{2,6},{3,7},{4,12},{5,13},{6,2},{7,3},{8,0},{9,1},{10,... | collective-permute-start | bytes 1769480 | tf_op jit(solution)/shard_map/ppermute | solution.py:347
  136.5 15.6 %collective-permute-start.22 = (bf16[208,768]{1,0:T(8,128)(2,1)S(1)}, bf16[208,768]{1,0:T(8,128)(2,1)S(1)}, u32[]{:S(2)}, u32[]{:S(2)}) collective-permute-start(bf16[208,768]{1,0:T(8,128)(2,1)S(1)} %pad_maximum_fusion.8), channel_id=1, source_target_pairs={{0,16},{1,17},{2,18},{3,19},{4,20},{5,21},{6,22},{7,23},{8,24},{9,... | collective-permute-start | bytes 958472 | tf_op jit(solution)/shard_map/ppermute | solution.py:347
  145.3 9.9 %collective-permute-start.15 = (bf16[192,768]{1,0:T(8,128)(2,1)S(1)}, bf16[192,768]{1,0:T(8,128)(2,1)S(1)}, u32[]{:S(2)}, u32[]{:S(2)}) collective-permute-start(bf16[192,768]{1,0:T(8,128)(2,1)S(1)} %add.137), channel_id=1, source_target_pairs={{0,8},{1,9},{2,6},{3,7},{4,12},{5,13},{6,2},{7,3},{8,0},{9,1},{10,... | collective-permute-start | bytes 884744 | tf_op jit(solution)/shard_map/ppermute | solution.py:347
  148.1 25.2 %collective-permute-start.26 = (bf16[768,768]{1,0:T(8,128)(2,1)}, bf16[768,768]{1,0:T(8,128)(2,1)S(1)}, u32[]{:S(2)}, u32[]{:S(2)}) collective-permute-start(bf16[768,768]{1,0:T(8,128)(2,1)} %constant_dynamic-update-slice_fusion.refs_0_), channel_id=1, source_target_pairs={{0,2},{1,3},{2,0},{3,1},{4,6},{5,7},{6,4},{7,5},{8,10},{9,11},{10,... | collective-permute-start | bytes 3538952 | tf_op jit(solution)/shard_map/ppermute | solution.py:347
  152.2 6.8 %collective-permute-start.23 = (bf16[192,768]{1,0:T(8,128)(2,1)S(1)}, bf16[192,768]{1,0:T(8,128)(2,1)S(1)}, u32[]{:S(2)}, u32[]{:S(2)}) collective-permute-start(bf16[192,768]{1,0:T(8,128)(2,1)S(1)} %slice.247), channel_id=1, source_target_pairs={{0,4},{1,5},{2,3},{3,2},{4,0},{5,1},{6,7},{7,6},{8,12},{9,13},{10,... | collective-permute-start | bytes 884744 | tf_op jit(solution)/shard_map/ppermute | solution.py:347
  155.2 10.1 %collective-permute-start.16 = (bf16[384,768]{1,0:T(8,128)(2,1)S(1)}, bf16[384,768]{1,0:T(8,128)(2,1)S(1)}, u32[]{:S(2)}, u32[]{:S(2)}) collective-permute-start(bf16[384,768]{1,0:T(8,128)(2,1)S(1)} %pad_maximum_fusion.5), channel_id=1, source_target_pairs={{0,4},{1,5},{2,3},{3,2},{4,0},{5,1},{6,7},{7,6},{8,12},{9,13},{10,... | collective-permute-start | bytes 1769480 | tf_op jit(solution)/shard_map/ppermute | solution.py:347
  159.1 9.9 %collective-permute-start.24 = (bf16[384,768]{1,0:T(8,128)(2,1)S(1)}, bf16[384,768]{1,0:T(8,128)(2,1)S(1)}, u32[]{:S(2)}, u32[]{:S(2)}) collective-permute-start(bf16[384,768]{1,0:T(8,128)(2,1)S(1)} %pad_maximum_fusion.6), channel_id=1, source_target_pairs={{0,1},{1,0},{2,10},{3,11},{4,5},{5,4},{6,14},{7,15},{8,9},{9,8},{1... | collective-permute-start | bytes 1769480 | tf_op jit(solution)/shard_map/ppermute | solution.py:347
  165.4 11.9 %collective-permute-start.27 = (bf16[768,768]{1,0:T(8,128)(2,1)S(1)}, bf16[768,768]{1,0:T(8,128)(2,1)}, u32[]{:S(2)}, u32[]{:S(2)}) collective-permute-start(bf16[768,768]{1,0:T(8,128)(2,1)S(1)} %pad_maximum_fusion.1.refs_2_), channel_id=1, source_target_pairs={{0,2},{1,3},{2,0},{3,1},{4,6},{5,7},{6,4},{7,5},{8,10},{9,11},{10,... | collective-permute-start | bytes 3538952 | tf_op jit(solution)/shard_map/ppermute | solution.py:347
  169.1 8.2 %collective-permute-start.28 = (bf16[768,768]{1,0:T(8,128)(2,1)S(1)}, bf16[768,768]{1,0:T(8,128)(2,1)}, u32[]{:S(2)}, u32[]{:S(2)}) collective-permute-start(bf16[768,768]{1,0:T(8,128)(2,1)S(1)} %pad_maximum_fusion.2.refs_4_), channel_id=1, source_target_pairs={{0,2},{1,3},{2,0},{3,1},{4,6},{5,7},{6,4},{7,5},{8,10},{9,11},{10,... | collective-permute-start | bytes 3538952 | tf_op jit(solution)/shard_map/ppermute | solution.py:347
  169.2 27.5 %collective-permute-start.9 = (bf16[768,768]{1,0:T(8,128)(2,1)}, bf16[768,768]{1,0:T(8,128)(2,1)}, u32[]{:S(2)}, u32[]{:S(2)}) collective-permute-start(bf16[768,768]{1,0:T(8,128)(2,1)} %constant_dynamic-update-slice_fusion.refs_0_), channel_id=1, source_target_pairs={{0,4},{1,5},{2,3},{3,2},{4,0},{5,1},{6,7},{7,6},{8,12},{9,13},{10,... | collective-permute-start | bytes 3538952 | tf_op jit(solution)/shard_map/ppermute | solution.py:347
  171.6 26.3 %collective-permute-start.17 = (bf16[768,768]{1,0:T(8,128)(2,1)S(1)}, bf16[768,768]{1,0:T(8,128)(2,1)}, u32[]{:S(2)}, u32[]{:S(2)}) collective-permute-start(bf16[768,768]{1,0:T(8,128)(2,1)S(1)} %pad_maximum_fusion.1.refs_2_), channel_id=1, source_target_pairs={{0,1},{1,0},{2,10},{3,11},{4,5},{5,4},{6,14},{7,15},{8,9},{9,8},{1... | collective-permute-start | bytes 3538952 | tf_op jit(solution)/shard_map/ppermute | solution.py:347
  174.3 23.6 %collective-permute-start.25 = (bf16[768,768]{1,0:T(8,128)(2,1)S(1)}, bf16[768,768]{1,0:T(8,128)(2,1)}, u32[]{:S(2)}, u32[]{:S(2)}) collective-permute-start(bf16[768,768]{1,0:T(8,128)(2,1)S(1)} %pad_maximum_fusion.2.refs_4_), channel_id=1, source_target_pairs={{0,8},{1,9},{2,6},{3,7},{4,12},{5,13},{6,2},{7,3},{8,0},{9,1},{10,... | collective-permute-start | bytes 3538952 | tf_op jit(solution)/shard_map/ppermute | solution.py:347
  198.0 6.2 %collective-permute-start.29 = (bf16[768,768]{1,0:T(8,128)(2,1)}, bf16[768,768]{1,0:T(8,128)(2,1)S(1)}, u32[]{:S(2)}, u32[]{:S(2)}) collective-permute-start(bf16[768,768]{1,0:T(8,128)(2,1)} %collective-permute-done.9.refs_0_), channel_id=1, source_target_pairs={{0,2},{1,3},{2,0},{3,1},{4,6},{5,7},{6,4},{7,5},{8,10},{9,11},{10,... | collective-permute-start | bytes 3538952 | tf_op jit(solution)/shard_map/ppermute | solution.py:347
  198.6 5.6 %collective-permute-start.30 = (bf16[768,768]{1,0:T(8,128)(2,1)}, bf16[768,768]{1,0:T(8,128)(2,1)S(1)}, u32[]{:S(2)}, u32[]{:S(2)}) collective-permute-start(bf16[768,768]{1,0:T(8,128)(2,1)} %collective-permute-done.17.refs_1_), channel_id=1, source_target_pairs={{0,2},{1,3},{2,0},{3,1},{4,6},{5,7},{6,4},{7,5},{8,10},{9,11},{10,... | collective-permute-start | bytes 3538952 | tf_op jit(solution)/shard_map/ppermute | solution.py:347
  198.6 6.1 %collective-permute-start.31 = (bf16[768,768]{1,0:T(8,128)(2,1)}, bf16[768,768]{1,0:T(8,128)(2,1)S(1)}, u32[]{:S(2)}, u32[]{:S(2)}) collective-permute-start(bf16[768,768]{1,0:T(8,128)(2,1)} %collective-permute-done.25.refs_2_), channel_id=1, source_target_pairs={{0,2},{1,3},{2,0},{3,1},{4,6},{5,7},{6,4},{7,5},{8,10},{9,11},{10,... | collective-permute-start | bytes 3538952 | tf_op jit(solution)/shard_map/ppermute | solution.py:347
  (17 other events, 160.0 us)

commit v5 on v4

--- a/solution.py
+++ b/solution.py
@@ -130,7 +130,7 @@
     loads[3].wait()
     loads[4].wait()
     down = first + line(b_down)
-    chunk = 512
+    chunk = 1024
     for j in range(w_up.shape[1] // chunk):
         cols = slice(j * chunk, (j + 1) * chunk)
         u = dot(f_low, w_up[:, cols]) + line(b_up, cols)
@@ -329,9 +329,9 @@
 SEQ, CORE, NEAR, LINE, FAR = range(5)
 
 STEPS = (
-    ((NEAR, SEQ), (LINE, NEAR), (SEQ, LINE)),
     ((SEQ, LINE), (NEAR, SEQ), (LINE, NEAR)),
     ((LINE, NEAR), (SEQ, LINE), (NEAR, SEQ)),
+    ((NEAR, SEQ), (LINE, NEAR), (SEQ, LINE)),
 )
 BLOCKS = 8
 UNPACK_VMEM = 24

time: 210 us -> 207 us (0.986)
  waiting for transfers between devices: 93 us -> 75.9 us
  starting transfers between devices: 38.9 us -> 54.8 us
    ppermute x30, waiting for transfers between devices: 88.3 us -> 71.2 us  [swap(): return lax.ppermute(values, AXES, perm)]
    ppermute x30, starting transfers between devices: 34.1 us -> 50 us  [swap(): return lax.ppermute(values, AXES, perm)]
  transfers between devices with their start and end apart: 32 -> 32, of which waited for: 20 -> 18; matrix products, arithmetic and copies ran while one was open for 4% -> 4% of each run, Pallas kernels for 16% -> 16%
where the time goes in v5:
time: 207 us; the launch traced here: 206 us
  waiting for transfers between devices  75.9 us (37%)
  Pallas kernels  62.4 us (30%)
  starting transfers between devices  54.8 us (26%)
  local copies, waits for them, and re-layouts  9.91 us (5%)
  other arithmetic  2.22 us (1%)
    ppermute x30, waiting for transfers between devices, swap(): return lax.ppermute(values, AXES, perm)  71.2 us
    ppermute x30, starting transfers between devices, swap(): return lax.ppermute(values, AXES, perm)  50 us
    pallas_call x1, Pallas kernels, body(): call(middle_kernel, [SMEM] + [VMEM] * 17 + [HBM] * 5, [sds((here, width),...  24.5 us
    pallas_call x3, Pallas kernels, unpack(): call(partial(unpack_kernel, parts, len(held) + len(after)), [SMEM] + [VME...  16.6 us
    pallas_call x1, Pallas kernels, body(): call(attention_back_kernel, [SMEM] + [VMEM] * 5 + [HBM] + [VMEM] * 4 + [H...  15.7 us
    unnamed x36, local copies, waits for them, and re-layouts  6.02 us
    ppermute x1, waiting for transfers between devices, body(): x_oth = lax.ppermute(x_own, 'seq', [(0, 1), (1, 0)])  4.7 us
  transfers between devices with their start and end apart: 32, of which 18 were waited for; matrix products, arithmetic and copies ran while one was open for 4% of the time, Pallas kernels for 16%

profile of v5, /device:TPU:0, one launch (start us, length us, event | category | flops | bytes accessed | tf_op | source)
XLA Modules:
  0.0 206.5 jit_solution(3653481007113144337)
XLA Ops:
  0.7 3.0 %collective-permute-start = (bf16[256,768]{1,0:T(8,128)(2,1)}, bf16[256,768]{1,0:T(8,128)(2,1)S(1)}, u32[]{:S(2)}, u32[]{:S(2)}) collective-permute-start(bf16[256,768]{1,0:T(8,128)(2,1)} %bitcast.13), channel_id=1, source_target_pairs={{0,1},{1,0},{2,3},{3,2},{4,5},{5,4},{6,7},{7,6},{8,9},{9,8},{10,11... | collective-permute-start | bytes 1179656 | tf_op jit(solution)/shard_map/ppermute | solution.py:417
  3.7 4.0 %shard_map.339 = (bf16[256,768]{1,0:T(8,128)(2,1)}, bf16[256,768]{1,0:T(8,128)(2,1)}, bf16[256,768]{1,0:T(8,128)(2,1)}) custom-call(bf16[256,768]{1,0:T(8,128)(2,1)} %bitcast.14, bf16[768,768]{1,0:T(8,128)(2,1)} %wq.3, f32[768]{0:T(1024)} %bq.1, bf16[768,768]{1,0:T(8,128)(2,1)} %wk.3, bf16[768,768]{1,0:T(8,128)(2,1)} %wv.3, f32[768]{0:T(1024)} %bv.3), custom_call_target="tpu_custom_call" | custom-call | tf_op jit(solution)/shard_map/pallas_call | solution.py:421
  8.3 4.7 %collective-permute-done.x_oth = bf16[256,768]{1,0:T(8,128)(2,1)S(1)} collective-permute-done((bf16[256,768]{1,0:T(8,128)(2,1)}, bf16[256,768]{1,0:T(8,128)(2,1)S(1)}, u32[]{:S(2)}, u32[]{:S(2)}) %collective-permute-start) | collective-permute-done | bytes 393248 | tf_op jit(solution)/shard_map/ppermute | solution.py:417
  13.8 24.5 %shard_map.340 = (bf16[256,768]{1,0:T(8,128)(2,1)}, f32[1,256]{1,0:T(1,128)}, bf16[12,512,256]{2,1,0:T(8,128)(2,1)}, bf16[512,768]{1,0:T(8,128)(2,1)}, bf16[512,...) custom-call(s32[8]{0:T(128)} %stack.35.scal, ...), custom_call_target="tpu_custom_call" | custom-call | tf_op jit(solution)/shard_map/pallas_call | solution.py:436
  38.8 15.7 %shard_map.341 = (bf16[256,768]{1,0:T(8,128)(2,1)}, bf16[512,768]{1,0:T(8,128)(2,1)}, bf16[512,768]{1,0:T(8,128)(2,1)}, bf16[16,768]{1,0:T(8,128)(2,1)}, bf16[15...) custom-call(s32[8]{0:T(128)} %stack.35.scal, bf16[256,768]{1,0:T(8,128)(2,1)} %bitcast.16, bf16[256,768]{1,0:T(8,128)(2,1)} %copy-done.15, ...), custom_call_target="tpu_custom_call" | custom-call | tf_op jit(solution)/shard_map/pallas_call | solution.py:490
  54.9 1.8 collective-permute-start.3
  60.2 1.8 collective-permute-start.19
  62.3 1.8 shard_map.342
  64.1 1.8 collective-permute-start.1
  65.9 13.3 %collective-permute-done.3 = bf16[768,768]{1,0:T(8,128)(2,1)S(1)} collective-permute-done((bf16[768,768]{1,0:T(8,128)(2,1)S(1)}, bf16[768,768]{1,0:T(8,128)(2,1)S(1)}, u32[]{:S(2)}, u32[]{:S(2)}) %collective-permute-start.3) | collective-permute-done | bytes 1179680 | tf_op jit(solution)/shard_map/ppermute | solution.py:347
  81.1 2.2 %collective-permute-done.11 = bf16[768,768]{1,0:T(8,128)(2,1)S(1)} collective-permute-done((bf16[768,768]{1,0:T(8,128)(2,1)S(1)}, bf16[768,768]{1,0:T(8,128)(2,1)S(1)}, u32[]{:S(2)}, u32[]{:S(2)}) %collective-permute-start.11) | collective-permute-done | bytes 1179680 | tf_op jit(solution)/shard_map/ppermute | solution.py:347
  87.3 4.4 %collective-permute-done.4 = bf16[384,768]{1,0:T(8,128)(2,1)S(1)} collective-permute-done((bf16[384,768]{1,0:T(8,128)(2,1)S(1)}, bf16[384,768]{1,0:T(8,128)(2,1)S(1)}, u32[]{:S(2)}, u32[]{:S(2)}) %collective-permute-start.4) | collective-permute-done | bytes 589856 | tf_op jit(solution)/shard_map/ppermute | solution.py:347
  93.5 6.8 %collective-permute-done.12 = bf16[384,768]{1,0:T(8,128)(2,1)S(1)} collective-permute-done((bf16[384,768]{1,0:T(8,128)(2,1)S(1)}, bf16[384,768]{1,0:T(8,128)(2,1)S(1)}, u32[]{:S(2)}, u32[]{:S(2)}) %collective-permute-start.12) | collective-permute-done | bytes 589856 | tf_op jit(solution)/shard_map/ppermute | solution.py:347
  102.2 2.7 %collective-permute-start.6 = (bf16[192,768]{1,0:T(8,128)(2,1)S(1)}, bf16[192,768]{1,0:T(8,128)(2,1)S(1)}, u32[]{:S(2)}, u32[]{:S(2)}) collective-permute-start(bf16[192,768]{1,0:T(8,128)(2,1)S(1)} %fusion), channel_id=1, source_target_pairs={{0,16},{1,17},{2,18},{3,19},{4,20},{5,21},{6,22},{7,23},{8,24},{9,... | collective-permute-start | bytes 884744 | tf_op jit(solution)/shard_map/ppermute | solution.py:347
  104.9 8.1 %collective-permute-done.6 = bf16[192,768]{1,0:T(8,128)(2,1)S(1)} collective-permute-done((bf16[192,768]{1,0:T(8,128)(2,1)S(1)}, bf16[192,768]{1,0:T(8,128)(2,1)S(1)}, u32[]{:S(2)}, u32[]{:S(2)}) %collective-permute-start.6) | collective-permute-done | bytes 294944 | tf_op jit(solution)/shard_map/ppermute | solution.py:347
  115.5 3.4 %collective-permute-start.14 = (bf16[192,768]{1,0:T(8,128)(2,1)S(1)}, bf16[192,768]{1,0:T(8,128)(2,1)S(1)}, u32[]{:S(2)}, u32[]{:S(2)}) collective-permute-start(bf16[192,768]{1,0:T(8,128)(2,1)S(1)} %add_add_fusion), channel_id=1, source_target_pairs={{0,16},{1,17},{2,18},{3,19},{4,20},{5,21},{6,22},{7,23},{8,24},{9,... | collective-permute-start | bytes 884744 | tf_op jit(solution)/shard_map/ppermute | solution.py:347
  118.9 4.1 %collective-permute-done.7 = bf16[192,768]{1,0:T(8,128)(2,1)S(1)} collective-permute-done((bf16[192,768]{1,0:T(8,128)(2,1)S(1)}, bf16[192,768]{1,0:T(8,128)(2,1)S(1)}, u32[]{:S(2)}, u32[]{:S(2)}) %collective-permute-start.7) | collective-permute-done | bytes 294944 | tf_op jit(solution)/shard_map/ppermute | solution.py:347
  123.3 2.1 %collective-permute-start.22 = (bf16[208,768]{1,0:T(8,128)(2,1)S(1)}, bf16[208,768]{1,0:T(8,128)(2,1)S(1)}, u32[]{:S(2)}, u32[]{:S(2)}) collective-permute-start(bf16[208,768]{1,0:T(8,128)(2,1)S(1)} %pad_maximum_fusion.8), channel_id=1, source_target_pairs={{0,16},{1,17},{2,18},{3,19},{4,20},{5,21},{6,22},{7,23},{8,24},{9,... | collective-permute-start | bytes 958472 | tf_op jit(solution)/shard_map/ppermute | solution.py:347
  125.4 2.1 %collective-permute-done.14 = bf16[192,768]{1,0:T(8,128)(2,1)S(1)} collective-permute-done((bf16[192,768]{1,0:T(8,128)(2,1)S(1)}, bf16[192,768]{1,0:T(8,128)(2,1)S(1)}, u32[]{:S(2)}, u32[]{:S(2)}) %collective-permute-start.14) | collective-permute-done | bytes 294944 | tf_op jit(solution)/shard_map/ppermute | solution.py:347
  130.8 5.4 %collective-permute-done.8 = bf16[384,768]{1,0:T(8,128)(2,1)S(1)} collective-permute-done((bf16[384,768]{1,0:T(8,128)(2,1)S(1)}, bf16[384,768]{1,0:T(8,128)(2,1)S(1)}, u32[]{:S(2)}, u32[]{:S(2)}) %collective-permute-start.8) | collective-permute-done | bytes 589856 | tf_op jit(solution)/shard_map/ppermute | solution.py:347
  137.1 7.8 %collective-permute-start.26 = (bf16[768,768]{1,0:T(8,128)(2,1)}, bf16[768,768]{1,0:T(8,128)(2,1)S(1)}, u32[]{:S(2)}, u32[]{:S(2)}) collective-permute-start(bf16[768,768]{1,0:T(8,128)(2,1)} %constant_dynamic-update-slice_fusion.refs_0_), channel_id=1, source_target_pairs={{0,2},{1,3},{2,0},{3,1},{4,6},{5,7},{6,4},{7,5},{8,10},{9,11},{10,... | collective-permute-start | bytes 3538952 | tf_op jit(solution)/shard_map/ppermute | solution.py:347
  145.0 1.8 collective-permute-start.23
  147.2 4.6 %collective-permute-done.23 = bf16[192,768]{1,0:T(8,128)(2,1)S(1)} collective-permute-done((bf16[192,768]{1,0:T(8,128)(2,1)S(1)}, bf16[192,768]{1,0:T(8,128)(2,1)S(1)}, u32[]{:S(2)}, u32[]{:S(2)}) %collective-permute-start.23) | collective-permute-done | bytes 294944 | tf_op jit(solution)/shard_map/ppermute | solution.py:347
  151.8 3.8 %collective-permute-start.24 = (bf16[384,768]{1,0:T(8,128)(2,1)S(1)}, bf16[384,768]{1,0:T(8,128)(2,1)S(1)}, u32[]{:S(2)}, u32[]{:S(2)}) collective-permute-start(bf16[384,768]{1,0:T(8,128)(2,1)S(1)} %pad_maximum_fusion.6), channel_id=1, source_target_pairs={{0,8},{1,9},{2,6},{3,7},{4,12},{5,13},{6,2},{7,3},{8,0},{9,1},{10,... | collective-permute-start | bytes 1769480 | tf_op jit(solution)/shard_map/ppermute | solution.py:347
  155.6 2.5 %collective-permute-done.16 = bf16[384,768]{1,0:T(8,128)(2,1)S(1)} collective-permute-done((bf16[384,768]{1,0:T(8,128)(2,1)S(1)}, bf16[384,768]{1,0:T(8,128)(2,1)S(1)}, u32[]{:S(2)}, u32[]{:S(2)}) %collective-permute-start.16) | collective-permute-done | bytes 589856 | tf_op jit(solution)/shard_map/ppermute | solution.py:347
  158.2 4.8 %collective-permute-start.27 = (bf16[768,768]{1,0:T(8,128)(2,1)S(1)}, bf16[768,768]{1,0:T(8,128)(2,1)}, u32[]{:S(2)}, u32[]{:S(2)}) collective-permute-start(bf16[768,768]{1,0:T(8,128)(2,1)S(1)} %pad_maximum_fusion.1.refs_2_), channel_id=1, source_target_pairs={{0,2},{1,3},{2,0},{3,1},{4,6},{5,7},{6,4},{7,5},{8,10},{9,11},{10,... | collective-permute-start | bytes 3538952 | tf_op jit(solution)/shard_map/ppermute | solution.py:347
  163.0 3.3 %collective-permute-done.24 = bf16[384,768]{1,0:T(8,128)(2,1)S(1)} collective-permute-done((bf16[384,768]{1,0:T(8,128)(2,1)S(1)}, bf16[384,768]{1,0:T(8,128)(2,1)S(1)}, u32[]{:S(2)}, u32[]{:S(2)}) %collective-permute-start.24) | collective-permute-done | bytes 589856 | tf_op jit(solution)/shard_map/ppermute | solution.py:347
  175.6 7.3 %shard_map.343 = (f32[3072,768]{1,0:T(8,128)}, f32[768,3072]{1,0:T(8,128)}, f32[768,768]{1,0:T(8,128)}, f32[768,768]{1,0:T(8,128)}, f32[768,768]{1,0:T(8,128)}, ...) custom-call(s32[8]{0:T(128)S(1)} %copy-done.11, bf16[768,768]{1,0:T(8,128)(2,1)} %constant_dynamic-update-slice_fusion.refs_0_, ...), custom_call_target="tpu_custom_call" | custom-call | tf_op jit(solution)/shard_map/pallas_call | solution.py:478
  182.8 10.3 %collective-permute-done.9.refs_0_ = bf16[768,768]{1,0:T(8,128)(2,1)} collective-permute-done((bf16[768,768]{1,0:T(8,128)(2,1)}, bf16[768,768]{1,0:T(8,128)(2,1)}, u32[]{:S(2)}, u32[]{:S(2)}) %collective-permute-start.9) | collective-permute-done | bytes 1179680 | tf_op jit(solution)/shard_map/ppermute | solution.py:347
  193.1 2.0 collective-permute-done.17.refs_1_
  196.3 5.1 %shard_map.344 = (f32[3072,768]{1,0:T(8,128)}, f32[768,3072]{1,0:T(8,128)}, f32[768,768]{1,0:T(8,128)}, f32[768,768]{1,0:T(8,128)}, f32[768,768]{1,0:T(8,128)}, ...) custom-call(s32[8]{0:T(128)S(1)} %copy-done.11, ...), custom_call_target="tpu_custom_call", output_to_operand_aliasing={{0}: (4, {}), {1}: (5, {}), {2}: (6, {}), {3}: (7, {}), {4}... | custom-call | tf_op jit(solution)/shard_map/pallas_call | solution.py:478
  202.1 4.2 %shard_map.345 = (f32[3072,768]{1,0:T(8,128)}, f32[768,3072]{1,0:T(8,128)}, f32[768,768]{1,0:T(8,128)}, f32[768,768]{1,0:T(8,128)}, f32[768,768]{1,0:T(8,128)}, /*index=5*/f32[768,768]{1,0:T(8,128)}, f32[8,128]{1,0:T(8,128)}) custom-call(s32[8]{0:T(128)S(1)} %copy-done.11, ...), custom_call_target="tpu_custom_call", output_to_operand_aliasing={{0}: (4, {}), {1}: (5, {}), {2}: (6, {}), {3}: (7, {}), {4}... | custom-call | tf_op jit(solution)/shard_map/pallas_call | solution.py:478
  (111 shorter events, 34.4 us)
Async XLA Ops:
  0.7 12.4 %collective-permute-start = (bf16[256,768]{1,0:T(8,128)(2,1)}, bf16[256,768]{1,0:T(8,128)(2,1)S(1)}, u32[]{:S(2)}, u32[]{:S(2)}) collective-permute-start(bf16[256,768]{1,0:T(8,128)(2,1)} %bitcast.13), channel_id=1, source_target_pairs={{0,1},{1,0},{2,3},{3,2},{4,5},{5,4},{6,7},{7,6},{8,9},{9,8},{10,11... | collective-permute-start | bytes 1179656 | tf_op jit(solution)/shard_map/ppermute | solution.py:417
  38.2 16.4 %collective-permute-start.2 = (bf16[1536,768]{1,0:T(8,128)(2,1)}, bf16[1536,768]{1,0:T(8,128)(2,1)S(1)}, u32[]{:S(2)}, u32[]{:S(2)}) collective-permute-start(bf16[1536,768]{1,0:T(8,128)(2,1)} %get-tuple-element.111), channel_id=1, source_target_pairs={{0,2},{1,3},{2,0},{3,1},{4,6},{5,7},{6,4},{7,5},{8,10},{9,11},{10,... | collective-permute-start | bytes 7077896 | tf_op jit(solution)/shard_map/ppermute | solution.py:347
  38.3 18.4 %collective-permute-start.10 = (bf16[1536,768]{1,0:T(8,128)(2,1)}, bf16[1536,768]{1,0:T(8,128)(2,1)S(1)}, u32[]{:S(2)}, u32[]{:S(2)}) collective-permute-start(bf16[1536,768]{1,0:T(8,128)(2,1)} %get-tuple-element.103.after), channel_id=1, source_target_pairs={{0,2},{1,3},{2,0},{3,1},{4,6},{5,7},{6,4},{7,5},{8,10},{9,11},{10,... | collective-permute-start | bytes 7077896 | tf_op jit(solution)/shard_map/ppermute | solution.py:347
  54.5 4.8 %collective-permute-start.18 = (bf16[1552,768]{1,0:T(8,128)(2,1)}, bf16[1552,768]{1,0:T(8,128)(2,1)S(1)}, u32[]{:S(2)}, u32[]{:S(2)}) collective-permute-start(bf16[1552,768]{1,0:T(8,128)(2,1)} %get-tuple-element.118), channel_id=1, source_target_pairs={{0,2},{1,3},{2,0},{3,1},{4,6},{5,7},{6,4},{7,5},{8,10},{9,11},{10,... | collective-permute-start | bytes 7151624 | tf_op jit(solution)/shard_map/ppermute | solution.py:347
  54.9 24.4 %collective-permute-start.3 = (bf16[768,768]{1,0:T(8,128)(2,1)S(1)}, bf16[768,768]{1,0:T(8,128)(2,1)S(1)}, u32[]{:S(2)}, u32[]{:S(2)}) collective-permute-start(bf16[768,768]{1,0:T(8,128)(2,1)S(1)} %get-tuple-element.175), channel_id=1, source_target_pairs={{0,1},{1,0},{2,10},{3,11},{4,5},{5,4},{6,14},{7,15},{8,9},{9,8},{1... | collective-permute-start | bytes 3538952 | tf_op jit(solution)/shard_map/ppermute | solution.py:347
  57.0 26.3 %collective-permute-start.11 = (bf16[768,768]{1,0:T(8,128)(2,1)S(1)}, bf16[768,768]{1,0:T(8,128)(2,1)S(1)}, u32[]{:S(2)}, u32[]{:S(2)}) collective-permute-start(bf16[768,768]{1,0:T(8,128)(2,1)S(1)} %get-tuple-element.173), channel_id=1, source_target_pairs={{0,8},{1,9},{2,6},{3,7},{4,12},{5,13},{6,2},{7,3},{8,0},{9,1},{10,... | collective-permute-start | bytes 3538952 | tf_op jit(solution)/shard_map/ppermute | solution.py:347
  60.2 25.2 %collective-permute-start.19 = (bf16[784,768]{1,0:T(8,128)(2,1)S(1)}, bf16[784,768]{1,0:T(8,128)(2,1)S(1)}, u32[]{:S(2)}, u32[]{:S(2)}) collective-permute-start(bf16[784,768]{1,0:T(8,128)(2,1)S(1)} %pad_maximum_fusion), channel_id=1, source_target_pairs={{0,4},{1,5},{2,3},{3,2},{4,0},{5,1},{6,7},{7,6},{8,12},{9,13},{10,... | collective-permute-start | bytes 3612680 | tf_op jit(solution)/shard_map/ppermute | solution.py:347
  64.1 29.3 %collective-permute-start.1 = (bf16[256,768]{1,0:T(8,128)(2,1)S(1)}, bf16[256,768]{1,0:T(8,128)(2,1)S(1)}, u32[]{:S(2)}, u32[]{:S(2)}) collective-permute-start(bf16[256,768]{1,0:T(8,128)(2,1)S(1)} %get-tuple-element.142.refs_10_), channel_id=1, source_target_pairs={{0,1},{1,0},{2,3},{3,2},{4,5},{5,4},{6,7},{7,6},{8,9},{9,8},{10,11... | collective-permute-start | bytes 1179656 | tf_op jit(solution)/shard_map/ppermute | solution.py:525
  79.4 12.4 %collective-permute-start.4 = (bf16[384,768]{1,0:T(8,128)(2,1)S(1)}, bf16[384,768]{1,0:T(8,128)(2,1)S(1)}, u32[]{:S(2)}, u32[]{:S(2)}) collective-permute-start(bf16[384,768]{1,0:T(8,128)(2,1)S(1)} %get-tuple-element.181), channel_id=1, source_target_pairs={{0,4},{1,5},{2,3},{3,2},{4,0},{5,1},{6,7},{7,6},{8,12},{9,13},{10,... | collective-permute-start | bytes 1769480 | tf_op jit(solution)/shard_map/ppermute | solution.py:347
  83.4 16.9 %collective-permute-start.12 = (bf16[384,768]{1,0:T(8,128)(2,1)S(1)}, bf16[384,768]{1,0:T(8,128)(2,1)S(1)}, u32[]{:S(2)}, u32[]{:S(2)}) collective-permute-start(bf16[384,768]{1,0:T(8,128)(2,1)S(1)} %get-tuple-element.178), channel_id=1, source_target_pairs={{0,1},{1,0},{2,10},{3,11},{4,5},{5,4},{6,14},{7,15},{8,9},{9,8},{1... | collective-permute-start | bytes 1769480 | tf_op jit(solution)/shard_map/ppermute | solution.py:347
  85.6 19.2 %collective-permute-start.20 = (bf16[400,768]{1,0:T(8,128)(2,1)S(1)}, bf16[400,768]{1,0:T(8,128)(2,1)S(1)}, u32[]{:S(2)}, u32[]{:S(2)}) collective-permute-start(bf16[400,768]{1,0:T(8,128)(2,1)S(1)} %pad_maximum_fusion.3), channel_id=1, source_target_pairs={{0,8},{1,9},{2,6},{3,7},{4,12},{5,13},{6,2},{7,3},{8,0},{9,1},{10,... | collective-permute-start | bytes 1843208 | tf_op jit(solution)/shard_map/ppermute | solution.py:347
  91.8 10.4 %collective-permute-start.5 = (bf16[192,768]{1,0:T(8,128)(2,1)S(1)}, bf16[192,768]{1,0:T(8,128)(2,1)S(1)}, u32[]{:S(2)}, u32[]{:S(2)}) collective-permute-start(bf16[192,768]{1,0:T(8,128)(2,1)S(1)} %slice_add_fusion.15), channel_id=1, source_target_pairs={{0,8},{1,9},{2,6},{3,7},{4,12},{5,13},{6,2},{7,3},{8,0},{9,1},{10,... | collective-permute-start | bytes 884744 | tf_op jit(solution)/shard_map/ppermute | solution.py:347
  100.3 15.1 %collective-permute-start.13 = (bf16[192,768]{1,0:T(8,128)(2,1)S(1)}, bf16[192,768]{1,0:T(8,128)(2,1)S(1)}, u32[]{:S(2)}, u32[]{:S(2)}) collective-permute-start(bf16[192,768]{1,0:T(8,128)(2,1)S(1)} %slice_add_fusion.17), channel_id=1, source_target_pairs={{0,4},{1,5},{2,3},{3,2},{4,0},{5,1},{6,7},{7,6},{8,12},{9,13},{10,... | collective-permute-start | bytes 884744 | tf_op jit(solution)/shard_map/ppermute | solution.py:347
  102.2 10.8 %collective-permute-start.6 = (bf16[192,768]{1,0:T(8,128)(2,1)S(1)}, bf16[192,768]{1,0:T(8,128)(2,1)S(1)}, u32[]{:S(2)}, u32[]{:S(2)}) collective-permute-start(bf16[192,768]{1,0:T(8,128)(2,1)S(1)} %fusion), channel_id=1, source_target_pairs={{0,16},{1,17},{2,18},{3,19},{4,20},{5,21},{6,22},{7,23},{8,24},{9,... | collective-permute-start | bytes 884744 | tf_op jit(solution)/shard_map/ppermute | solution.py:347
  113.1 9.9 %collective-permute-start.7 = (bf16[192,768]{1,0:T(8,128)(2,1)S(1)}, bf16[192,768]{1,0:T(8,128)(2,1)S(1)}, u32[]{:S(2)}, u32[]{:S(2)}) collective-permute-start(bf16[192,768]{1,0:T(8,128)(2,1)S(1)} %add.129), channel_id=1, source_target_pairs={{0,8},{1,9},{2,6},{3,7},{4,12},{5,13},{6,2},{7,3},{8,0},{9,1},{10,... | collective-permute-start | bytes 884744 | tf_op jit(solution)/shard_map/ppermute | solution.py:347
  113.9 9.3 %collective-permute-start.21 = (bf16[208,768]{1,0:T(8,128)(2,1)S(1)}, bf16[208,768]{1,0:T(8,128)(2,1)S(1)}, u32[]{:S(2)}, u32[]{:S(2)}) collective-permute-start(bf16[208,768]{1,0:T(8,128)(2,1)S(1)} %pad_maximum_fusion.7), channel_id=1, source_target_pairs={{0,1},{1,0},{2,10},{3,11},{4,5},{5,4},{6,14},{7,15},{8,9},{9,8},{1... | collective-permute-start | bytes 958472 | tf_op jit(solution)/shard_map/ppermute | solution.py:347
  115.5 12.0 %collective-permute-start.14 = (bf16[192,768]{1,0:T(8,128)(2,1)S(1)}, bf16[192,768]{1,0:T(8,128)(2,1)S(1)}, u32[]{:S(2)}, u32[]{:S(2)}) collective-permute-start(bf16[192,768]{1,0:T(8,128)(2,1)S(1)} %add_add_fusion), channel_id=1, source_target_pairs={{0,16},{1,17},{2,18},{3,19},{4,20},{5,21},{6,22},{7,23},{8,24},{9,... | collective-permute-start | bytes 884744 | tf_op jit(solution)/shard_map/ppermute | solution.py:347
  123.1 13.1 %collective-permute-start.8 = (bf16[384,768]{1,0:T(8,128)(2,1)S(1)}, bf16[384,768]{1,0:T(8,128)(2,1)S(1)}, u32[]{:S(2)}, u32[]{:S(2)}) collective-permute-start(bf16[384,768]{1,0:T(8,128)(2,1)S(1)} %pad_maximum_fusion.4), channel_id=1, source_target_pairs={{0,4},{1,5},{2,3},{3,2},{4,0},{5,1},{6,7},{7,6},{8,12},{9,13},{10,... | collective-permute-start | bytes 1769480 | tf_op jit(solution)/shard_map/ppermute | solution.py:347
  123.3 21.6 %collective-permute-start.22 = (bf16[208,768]{1,0:T(8,128)(2,1)S(1)}, bf16[208,768]{1,0:T(8,128)(2,1)S(1)}, u32[]{:S(2)}, u32[]{:S(2)}) collective-permute-start(bf16[208,768]{1,0:T(8,128)(2,1)S(1)} %pad_maximum_fusion.8), channel_id=1, source_target_pairs={{0,16},{1,17},{2,18},{3,19},{4,20},{5,21},{6,22},{7,23},{8,24},{9,... | collective-permute-start | bytes 958472 | tf_op jit(solution)/shard_map/ppermute | solution.py:347
  127.6 19.2 %collective-permute-start.15 = (bf16[192,768]{1,0:T(8,128)(2,1)S(1)}, bf16[192,768]{1,0:T(8,128)(2,1)S(1)}, u32[]{:S(2)}, u32[]{:S(2)}) collective-permute-start(bf16[192,768]{1,0:T(8,128)(2,1)S(1)} %add.137), channel_id=1, source_target_pairs={{0,4},{1,5},{2,3},{3,2},{4,0},{5,1},{6,7},{7,6},{8,12},{9,13},{10,... | collective-permute-start | bytes 884744 | tf_op jit(solution)/shard_map/ppermute | solution.py:347
  137.1 31.5 %collective-permute-start.26 = (bf16[768,768]{1,0:T(8,128)(2,1)}, bf16[768,768]{1,0:T(8,128)(2,1)S(1)}, u32[]{:S(2)}, u32[]{:S(2)}) collective-permute-start(bf16[768,768]{1,0:T(8,128)(2,1)} %constant_dynamic-update-slice_fusion.refs_0_), channel_id=1, source_target_pairs={{0,2},{1,3},{2,0},{3,1},{4,6},{5,7},{6,4},{7,5},{8,10},{9,11},{10,... | collective-permute-start | bytes 3538952 | tf_op jit(solution)/shard_map/ppermute | solution.py:347
  145.0 6.8 %collective-permute-start.23 = (bf16[192,768]{1,0:T(8,128)(2,1)S(1)}, bf16[192,768]{1,0:T(8,128)(2,1)S(1)}, u32[]{:S(2)}, u32[]{:S(2)}) collective-permute-start(bf16[192,768]{1,0:T(8,128)(2,1)S(1)} %slice.247), channel_id=1, source_target_pairs={{0,1},{1,0},{2,10},{3,11},{4,5},{5,4},{6,14},{7,15},{8,9},{9,8},{1... | collective-permute-start | bytes 884744 | tf_op jit(solution)/shard_map/ppermute | solution.py:347
  146.8 11.3 %collective-permute-start.16 = (bf16[384,768]{1,0:T(8,128)(2,1)S(1)}, bf16[384,768]{1,0:T(8,128)(2,1)S(1)}, u32[]{:S(2)}, u32[]{:S(2)}) collective-permute-start(bf16[384,768]{1,0:T(8,128)(2,1)S(1)} %pad_maximum_fusion.5), channel_id=1, source_target_pairs={{0,1},{1,0},{2,10},{3,11},{4,5},{5,4},{6,14},{7,15},{8,9},{9,8},{1... | collective-permute-start | bytes 1769480 | tf_op jit(solution)/shard_map/ppermute | solution.py:347
  151.8 14.5 %collective-permute-start.24 = (bf16[384,768]{1,0:T(8,128)(2,1)S(1)}, bf16[384,768]{1,0:T(8,128)(2,1)S(1)}, u32[]{:S(2)}, u32[]{:S(2)}) collective-permute-start(bf16[384,768]{1,0:T(8,128)(2,1)S(1)} %pad_maximum_fusion.6), channel_id=1, source_target_pairs={{0,8},{1,9},{2,6},{3,7},{4,12},{5,13},{6,2},{7,3},{8,0},{9,1},{10,... | collective-permute-start | bytes 1769480 | tf_op jit(solution)/shard_map/ppermute | solution.py:347
  158.2 16.1 %collective-permute-start.27 = (bf16[768,768]{1,0:T(8,128)(2,1)S(1)}, bf16[768,768]{1,0:T(8,128)(2,1)}, u32[]{:S(2)}, u32[]{:S(2)}) collective-permute-start(bf16[768,768]{1,0:T(8,128)(2,1)S(1)} %pad_maximum_fusion.1.refs_2_), channel_id=1, source_target_pairs={{0,2},{1,3},{2,0},{3,1},{4,6},{5,7},{6,4},{7,5},{8,10},{9,11},{10,... | collective-permute-start | bytes 3538952 | tf_op jit(solution)/shard_map/ppermute | solution.py:347
  166.3 7.9 %collective-permute-start.28 = (bf16[768,768]{1,0:T(8,128)(2,1)S(1)}, bf16[768,768]{1,0:T(8,128)(2,1)}, u32[]{:S(2)}, u32[]{:S(2)}) collective-permute-start(bf16[768,768]{1,0:T(8,128)(2,1)S(1)} %pad_maximum_fusion.2.refs_4_), channel_id=1, source_target_pairs={{0,2},{1,3},{2,0},{3,1},{4,6},{5,7},{6,4},{7,5},{8,10},{9,11},{10,... | collective-permute-start | bytes 3538952 | tf_op jit(solution)/shard_map/ppermute | solution.py:347
  166.4 26.7 %collective-permute-start.9 = (bf16[768,768]{1,0:T(8,128)(2,1)}, bf16[768,768]{1,0:T(8,128)(2,1)}, u32[]{:S(2)}, u32[]{:S(2)}) collective-permute-start(bf16[768,768]{1,0:T(8,128)(2,1)} %constant_dynamic-update-slice_fusion.refs_0_), channel_id=1, source_target_pairs={{0,1},{1,0},{2,10},{3,11},{4,5},{5,4},{6,14},{7,15},{8,9},{9,8},{1... | collective-permute-start | bytes 3538952 | tf_op jit(solution)/shard_map/ppermute | solution.py:347
  168.0 27.1 %collective-permute-start.17 = (bf16[768,768]{1,0:T(8,128)(2,1)S(1)}, bf16[768,768]{1,0:T(8,128)(2,1)}, u32[]{:S(2)}, u32[]{:S(2)}) collective-permute-start(bf16[768,768]{1,0:T(8,128)(2,1)S(1)} %pad_maximum_fusion.1.refs_2_), channel_id=1, source_target_pairs={{0,8},{1,9},{2,6},{3,7},{4,12},{5,13},{6,2},{7,3},{8,0},{9,1},{10,... | collective-permute-start | bytes 3538952 | tf_op jit(solution)/shard_map/ppermute | solution.py:347
  169.6 26.1 %collective-permute-start.25 = (bf16[768,768]{1,0:T(8,128)(2,1)S(1)}, bf16[768,768]{1,0:T(8,128)(2,1)}, u32[]{:S(2)}, u32[]{:S(2)}) collective-permute-start(bf16[768,768]{1,0:T(8,128)(2,1)S(1)} %pad_maximum_fusion.2.refs_4_), channel_id=1, source_target_pairs={{0,4},{1,5},{2,3},{3,2},{4,0},{5,1},{6,7},{7,6},{8,12},{9,13},{10,... | collective-permute-start | bytes 3538952 | tf_op jit(solution)/shard_map/ppermute | solution.py:347
  195.6 5.7 %collective-permute-start.29 = (bf16[768,768]{1,0:T(8,128)(2,1)}, bf16[768,768]{1,0:T(8,128)(2,1)S(1)}, u32[]{:S(2)}, u32[]{:S(2)}) collective-permute-start(bf16[768,768]{1,0:T(8,128)(2,1)} %collective-permute-done.9.refs_0_), channel_id=1, source_target_pairs={{0,2},{1,3},{2,0},{3,1},{4,6},{5,7},{6,4},{7,5},{8,10},{9,11},{10,... | collective-permute-start | bytes 3538952 | tf_op jit(solution)/shard_map/ppermute | solution.py:347
  195.7 5.6 %collective-permute-start.30 = (bf16[768,768]{1,0:T(8,128)(2,1)}, bf16[768,768]{1,0:T(8,128)(2,1)S(1)}, u32[]{:S(2)}, u32[]{:S(2)}) collective-permute-start(bf16[768,768]{1,0:T(8,128)(2,1)} %collective-permute-done.17.refs_1_), channel_id=1, source_target_pairs={{0,2},{1,3},{2,0},{3,1},{4,6},{5,7},{6,4},{7,5},{8,10},{9,11},{10,... | collective-permute-start | bytes 3538952 | tf_op jit(solution)/shard_map/ppermute | solution.py:347
  196.1 5.9 %collective-permute-start.31 = (bf16[768,768]{1,0:T(8,128)(2,1)}, bf16[768,768]{1,0:T(8,128)(2,1)S(1)}, u32[]{:S(2)}, u32[]{:S(2)}) collective-permute-start(bf16[768,768]{1,0:T(8,128)(2,1)} %collective-permute-done.25.refs_2_), channel_id=1, source_target_pairs={{0,2},{1,3},{2,0},{3,1},{4,6},{5,7},{6,4},{7,5},{8,10},{9,11},{10,... | collective-permute-start | bytes 3538952 | tf_op jit(solution)/shard_map/ppermute | solution.py:347
  (17 other events, 166.8 us)

commit v6 on v5

--- a/solution.py
+++ b/solution.py
@@ -207,6 +207,8 @@
         fetch(probs_h.at[pl.ds(2 * p, 2)], probs.at[pl.ds(2 * p, 2)], p_sems.at[p])
         for p in range(heads // 2)
     ]
+    x_t[:, :here] = jnp.transpose(x_own[...])
+    x_t[:, here:] = jnp.transpose(x_oth[...])
     k_t[...] = jnp.transpose(k_all[...])
     masks = half_masks()
     for p in range(heads // 2):
@@ -232,8 +234,6 @@
             jnp.concatenate(grads, 1), jnp.concatenate(queries, 0)
         ).astype(bf16)
     grad_query[...] = jnp.transpose(query_t[...])
-    x_t[:, :here] = jnp.transpose(x_own[...])
-    x_t[:, here:] = jnp.transpose(x_oth[...])
 
     vec_all[...] = vecs[...]
     vec_all[11:12] = jnp.sum(grad_query[...].astype(f32), 0, keepdims=True)
@@ -334,7 +334,7 @@
     ((NEAR, SEQ), (LINE, NEAR), (SEQ, LINE)),
 )
 BLOCKS = 8
-UNPACK_VMEM = 24
+UNPACK_VMEM = 18
 
 
 def flip_of(index, pairs, core):

time: 207 us -> 207 us (level)
  no operation moved by 1% of the time
where the time goes in v6:
time: 207 us; the launch traced here: 206 us
  waiting for transfers between devices  75.9 us (37%)
  Pallas kernels  62.3 us (30%)
  starting transfers between devices  54.8 us (26%)
  local copies, waits for them, and re-layouts  9.91 us (5%)
  other arithmetic  2.22 us (1%)
    ppermute x30, waiting for transfers between devices, swap(): return lax.ppermute(values, AXES, perm)  71.2 us
    ppermute x30, starting transfers between devices, swap(): return lax.ppermute(values, AXES, perm)  50 us
    pallas_call x1, Pallas kernels, body(): call(middle_kernel, [SMEM] + [VMEM] * 17 + [HBM] * 5, [sds((here, width),...  24.5 us
    pallas_call x3, Pallas kernels, unpack(): call(partial(unpack_kernel, parts, len(held) + len(after)), [SMEM] + [VME...  16.6 us
    pallas_call x1, Pallas kernels, body(): call(attention_back_kernel, [SMEM] + [VMEM] * 5 + [HBM] + [VMEM] * 4 + [H...  15.5 us
    unnamed x36, local copies, waits for them, and re-layouts  6.02 us
    ppermute x1, waiting for transfers between devices, body(): x_oth = lax.ppermute(x_own, 'seq', [(0, 1), (1, 0)])  4.7 us
  transfers between devices with their start and end apart: 32, of which 18 were waited for; matrix products, arithmetic and copies ran while one was open for 4% of the time, Pallas kernels for 16%

profile of v6, /device:TPU:0, one launch (start us, length us, event | category | flops | bytes accessed | tf_op | source)
XLA Modules:
  0.0 206.3 jit_solution(1087193254808143851)
XLA Ops:
  0.7 3.0 %collective-permute-start = (bf16[256,768]{1,0:T(8,128)(2,1)}, bf16[256,768]{1,0:T(8,128)(2,1)S(1)}, u32[]{:S(2)}, u32[]{:S(2)}) collective-permute-start(bf16[256,768]{1,0:T(8,128)(2,1)} %bitcast.13), channel_id=1, source_target_pairs={{0,1},{1,0},{2,3},{3,2},{4,5},{5,4},{6,7},{7,6},{8,9},{9,8},{10,11... | collective-permute-start | bytes 1179656 | tf_op jit(solution)/shard_map/ppermute | solution.py:417
  3.7 4.0 %shard_map.339 = (bf16[256,768]{1,0:T(8,128)(2,1)}, bf16[256,768]{1,0:T(8,128)(2,1)}, bf16[256,768]{1,0:T(8,128)(2,1)}) custom-call(bf16[256,768]{1,0:T(8,128)(2,1)} %bitcast.14, bf16[768,768]{1,0:T(8,128)(2,1)} %wq.3, f32[768]{0:T(1024)} %bq.1, bf16[768,768]{1,0:T(8,128)(2,1)} %wk.3, bf16[768,768]{1,0:T(8,128)(2,1)} %wv.3, f32[768]{0:T(1024)} %bv.3), custom_call_target="tpu_custom_call" | custom-call | tf_op jit(solution)/shard_map/pallas_call | solution.py:421
  8.3 4.7 %collective-permute-done.x_oth = bf16[256,768]{1,0:T(8,128)(2,1)S(1)} collective-permute-done((bf16[256,768]{1,0:T(8,128)(2,1)}, bf16[256,768]{1,0:T(8,128)(2,1)S(1)}, u32[]{:S(2)}, u32[]{:S(2)}) %collective-permute-start) | collective-permute-done | bytes 393248 | tf_op jit(solution)/shard_map/ppermute | solution.py:417
  13.8 24.5 %shard_map.340 = (bf16[256,768]{1,0:T(8,128)(2,1)}, f32[1,256]{1,0:T(1,128)}, bf16[12,512,256]{2,1,0:T(8,128)(2,1)}, bf16[512,768]{1,0:T(8,128)(2,1)}, bf16[512,...) custom-call(s32[8]{0:T(128)} %stack.35.scal, ...), custom_call_target="tpu_custom_call" | custom-call | tf_op jit(solution)/shard_map/pallas_call | solution.py:436
  38.8 15.5 %shard_map.341 = (bf16[256,768]{1,0:T(8,128)(2,1)}, bf16[512,768]{1,0:T(8,128)(2,1)}, bf16[512,768]{1,0:T(8,128)(2,1)}, bf16[16,768]{1,0:T(8,128)(2,1)}, bf16[15...) custom-call(s32[8]{0:T(128)} %stack.35.scal, bf16[256,768]{1,0:T(8,128)(2,1)} %bitcast.16, bf16[256,768]{1,0:T(8,128)(2,1)} %copy-done.15, ...), custom_call_target="tpu_custom_call" | custom-call | tf_op jit(solution)/shard_map/pallas_call | solution.py:490
  54.7 1.8 collective-permute-start.3
  60.0 1.8 collective-permute-start.19
  62.2 1.8 shard_map.342
  64.0 1.8 collective-permute-start.1
  65.8 13.3 %collective-permute-done.3 = bf16[768,768]{1,0:T(8,128)(2,1)S(1)} collective-permute-done((bf16[768,768]{1,0:T(8,128)(2,1)S(1)}, bf16[768,768]{1,0:T(8,128)(2,1)S(1)}, u32[]{:S(2)}, u32[]{:S(2)}) %collective-permute-start.3) | collective-permute-done | bytes 1179680 | tf_op jit(solution)/shard_map/ppermute | solution.py:347
  81.0 2.2 %collective-permute-done.11 = bf16[768,768]{1,0:T(8,128)(2,1)S(1)} collective-permute-done((bf16[768,768]{1,0:T(8,128)(2,1)S(1)}, bf16[768,768]{1,0:T(8,128)(2,1)S(1)}, u32[]{:S(2)}, u32[]{:S(2)}) %collective-permute-start.11) | collective-permute-done | bytes 1179680 | tf_op jit(solution)/shard_map/ppermute | solution.py:347
  87.2 4.4 %collective-permute-done.4 = bf16[384,768]{1,0:T(8,128)(2,1)S(1)} collective-permute-done((bf16[384,768]{1,0:T(8,128)(2,1)S(1)}, bf16[384,768]{1,0:T(8,128)(2,1)S(1)}, u32[]{:S(2)}, u32[]{:S(2)}) %collective-permute-start.4) | collective-permute-done | bytes 589856 | tf_op jit(solution)/shard_map/ppermute | solution.py:347
  93.4 6.8 %collective-permute-done.12 = bf16[384,768]{1,0:T(8,128)(2,1)S(1)} collective-permute-done((bf16[384,768]{1,0:T(8,128)(2,1)S(1)}, bf16[384,768]{1,0:T(8,128)(2,1)S(1)}, u32[]{:S(2)}, u32[]{:S(2)}) %collective-permute-start.12) | collective-permute-done | bytes 589856 | tf_op jit(solution)/shard_map/ppermute | solution.py:347
  102.0 2.7 %collective-permute-start.6 = (bf16[192,768]{1,0:T(8,128)(2,1)S(1)}, bf16[192,768]{1,0:T(8,128)(2,1)S(1)}, u32[]{:S(2)}, u32[]{:S(2)}) collective-permute-start(bf16[192,768]{1,0:T(8,128)(2,1)S(1)} %fusion), channel_id=1, source_target_pairs={{0,16},{1,17},{2,18},{3,19},{4,20},{5,21},{6,22},{7,23},{8,24},{9,... | collective-permute-start | bytes 884744 | tf_op jit(solution)/shard_map/ppermute | solution.py:347
  104.7 8.1 %collective-permute-done.6 = bf16[192,768]{1,0:T(8,128)(2,1)S(1)} collective-permute-done((bf16[192,768]{1,0:T(8,128)(2,1)S(1)}, bf16[192,768]{1,0:T(8,128)(2,1)S(1)}, u32[]{:S(2)}, u32[]{:S(2)}) %collective-permute-start.6) | collective-permute-done | bytes 294944 | tf_op jit(solution)/shard_map/ppermute | solution.py:347
  115.3 3.4 %collective-permute-start.14 = (bf16[192,768]{1,0:T(8,128)(2,1)S(1)}, bf16[192,768]{1,0:T(8,128)(2,1)S(1)}, u32[]{:S(2)}, u32[]{:S(2)}) collective-permute-start(bf16[192,768]{1,0:T(8,128)(2,1)S(1)} %add_add_fusion), channel_id=1, source_target_pairs={{0,16},{1,17},{2,18},{3,19},{4,20},{5,21},{6,22},{7,23},{8,24},{9,... | collective-permute-start | bytes 884744 | tf_op jit(solution)/shard_map/ppermute | solution.py:347
  118.8 4.1 %collective-permute-done.7 = bf16[192,768]{1,0:T(8,128)(2,1)S(1)} collective-permute-done((bf16[192,768]{1,0:T(8,128)(2,1)S(1)}, bf16[192,768]{1,0:T(8,128)(2,1)S(1)}, u32[]{:S(2)}, u32[]{:S(2)}) %collective-permute-start.7) | collective-permute-done | bytes 294944 | tf_op jit(solution)/shard_map/ppermute | solution.py:347
  123.1 2.1 %collective-permute-start.22 = (bf16[208,768]{1,0:T(8,128)(2,1)S(1)}, bf16[208,768]{1,0:T(8,128)(2,1)S(1)}, u32[]{:S(2)}, u32[]{:S(2)}) collective-permute-start(bf16[208,768]{1,0:T(8,128)(2,1)S(1)} %pad_maximum_fusion.8), channel_id=1, source_target_pairs={{0,16},{1,17},{2,18},{3,19},{4,20},{5,21},{6,22},{7,23},{8,24},{9,... | collective-permute-start | bytes 958472 | tf_op jit(solution)/shard_map/ppermute | solution.py:347
  125.2 2.1 %collective-permute-done.14 = bf16[192,768]{1,0:T(8,128)(2,1)S(1)} collective-permute-done((bf16[192,768]{1,0:T(8,128)(2,1)S(1)}, bf16[192,768]{1,0:T(8,128)(2,1)S(1)}, u32[]{:S(2)}, u32[]{:S(2)}) %collective-permute-start.14) | collective-permute-done | bytes 294944 | tf_op jit(solution)/shard_map/ppermute | solution.py:347
  130.6 5.4 %collective-permute-done.8 = bf16[384,768]{1,0:T(8,128)(2,1)S(1)} collective-permute-done((bf16[384,768]{1,0:T(8,128)(2,1)S(1)}, bf16[384,768]{1,0:T(8,128)(2,1)S(1)}, u32[]{:S(2)}, u32[]{:S(2)}) %collective-permute-start.8) | collective-permute-done | bytes 589856 | tf_op jit(solution)/shard_map/ppermute | solution.py:347
  136.9 7.8 %collective-permute-start.26 = (bf16[768,768]{1,0:T(8,128)(2,1)}, bf16[768,768]{1,0:T(8,128)(2,1)S(1)}, u32[]{:S(2)}, u32[]{:S(2)}) collective-permute-start(bf16[768,768]{1,0:T(8,128)(2,1)} %constant_dynamic-update-slice_fusion.refs_0_), channel_id=1, source_target_pairs={{0,2},{1,3},{2,0},{3,1},{4,6},{5,7},{6,4},{7,5},{8,10},{9,11},{10,... | collective-permute-start | bytes 3538952 | tf_op jit(solution)/shard_map/ppermute | solution.py:347
  144.8 1.8 collective-permute-start.23
  147.0 4.6 %collective-permute-done.23 = bf16[192,768]{1,0:T(8,128)(2,1)S(1)} collective-permute-done((bf16[192,768]{1,0:T(8,128)(2,1)S(1)}, bf16[192,768]{1,0:T(8,128)(2,1)S(1)}, u32[]{:S(2)}, u32[]{:S(2)}) %collective-permute-start.23) | collective-permute-done | bytes 294944 | tf_op jit(solution)/shard_map/ppermute | solution.py:347
  151.6 3.8 %collective-permute-start.24 = (bf16[384,768]{1,0:T(8,128)(2,1)S(1)}, bf16[384,768]{1,0:T(8,128)(2,1)S(1)}, u32[]{:S(2)}, u32[]{:S(2)}) collective-permute-start(bf16[384,768]{1,0:T(8,128)(2,1)S(1)} %pad_maximum_fusion.6), channel_id=1, source_target_pairs={{0,8},{1,9},{2,6},{3,7},{4,12},{5,13},{6,2},{7,3},{8,0},{9,1},{10,... | collective-permute-start | bytes 1769480 | tf_op jit(solution)/shard_map/ppermute | solution.py:347
  155.4 2.5 %collective-permute-done.16 = bf16[384,768]{1,0:T(8,128)(2,1)S(1)} collective-permute-done((bf16[384,768]{1,0:T(8,128)(2,1)S(1)}, bf16[384,768]{1,0:T(8,128)(2,1)S(1)}, u32[]{:S(2)}, u32[]{:S(2)}) %collective-permute-start.16) | collective-permute-done | bytes 589856 | tf_op jit(solution)/shard_map/ppermute | solution.py:347
  158.0 4.8 %collective-permute-start.27 = (bf16[768,768]{1,0:T(8,128)(2,1)S(1)}, bf16[768,768]{1,0:T(8,128)(2,1)}, u32[]{:S(2)}, u32[]{:S(2)}) collective-permute-start(bf16[768,768]{1,0:T(8,128)(2,1)S(1)} %pad_maximum_fusion.1.refs_2_), channel_id=1, source_target_pairs={{0,2},{1,3},{2,0},{3,1},{4,6},{5,7},{6,4},{7,5},{8,10},{9,11},{10,... | collective-permute-start | bytes 3538952 | tf_op jit(solution)/shard_map/ppermute | solution.py:347
  162.8 3.3 %collective-permute-done.24 = bf16[384,768]{1,0:T(8,128)(2,1)S(1)} collective-permute-done((bf16[384,768]{1,0:T(8,128)(2,1)S(1)}, bf16[384,768]{1,0:T(8,128)(2,1)S(1)}, u32[]{:S(2)}, u32[]{:S(2)}) %collective-permute-start.24) | collective-permute-done | bytes 589856 | tf_op jit(solution)/shard_map/ppermute | solution.py:347
  175.4 7.3 %shard_map.343 = (f32[3072,768]{1,0:T(8,128)}, f32[768,3072]{1,0:T(8,128)}, f32[768,768]{1,0:T(8,128)}, f32[768,768]{1,0:T(8,128)}, f32[768,768]{1,0:T(8,128)}, ...) custom-call(s32[8]{0:T(128)S(1)} %copy-done.11, bf16[768,768]{1,0:T(8,128)(2,1)} %constant_dynamic-update-slice_fusion.refs_0_, ...), custom_call_target="tpu_custom_call" | custom-call | tf_op jit(solution)/shard_map/pallas_call | solution.py:478
  182.7 10.3 %collective-permute-done.9.refs_0_ = bf16[768,768]{1,0:T(8,128)(2,1)} collective-permute-done((bf16[768,768]{1,0:T(8,128)(2,1)}, bf16[768,768]{1,0:T(8,128)(2,1)}, u32[]{:S(2)}, u32[]{:S(2)}) %collective-permute-start.9) | collective-permute-done | bytes 1179680 | tf_op jit(solution)/shard_map/ppermute | solution.py:347
  193.0 2.0 collective-permute-done.17.refs_1_
  196.1 5.1 %shard_map.344 = (f32[3072,768]{1,0:T(8,128)}, f32[768,3072]{1,0:T(8,128)}, f32[768,768]{1,0:T(8,128)}, f32[768,768]{1,0:T(8,128)}, f32[768,768]{1,0:T(8,128)}, ...) custom-call(s32[8]{0:T(128)S(1)} %copy-done.11, ...), custom_call_target="tpu_custom_call", output_to_operand_aliasing={{0}: (4, {}), {1}: (5, {}), {2}: (6, {}), {3}: (7, {}), {4}... | custom-call | tf_op jit(solution)/shard_map/pallas_call | solution.py:478
  201.9 4.2 %shard_map.345 = (f32[3072,768]{1,0:T(8,128)}, f32[768,3072]{1,0:T(8,128)}, f32[768,768]{1,0:T(8,128)}, f32[768,768]{1,0:T(8,128)}, f32[768,768]{1,0:T(8,128)}, /*index=5*/f32[768,768]{1,0:T(8,128)}, f32[8,128]{1,0:T(8,128)}) custom-call(s32[8]{0:T(128)S(1)} %copy-done.11, ...), custom_call_target="tpu_custom_call", output_to_operand_aliasing={{0}: (4, {}), {1}: (5, {}), {2}: (6, {}), {3}: (7, {}), {4}... | custom-call | tf_op jit(solution)/shard_map/pallas_call | solution.py:478
  (111 shorter events, 34.4 us)
Async XLA Ops:
  0.7 12.4 %collective-permute-start = (bf16[256,768]{1,0:T(8,128)(2,1)}, bf16[256,768]{1,0:T(8,128)(2,1)S(1)}, u32[]{:S(2)}, u32[]{:S(2)}) collective-permute-start(bf16[256,768]{1,0:T(8,128)(2,1)} %bitcast.13), channel_id=1, source_target_pairs={{0,1},{1,0},{2,3},{3,2},{4,5},{5,4},{6,7},{7,6},{8,9},{9,8},{10,11... | collective-permute-start | bytes 1179656 | tf_op jit(solution)/shard_map/ppermute | solution.py:417
  38.2 16.2 %collective-permute-start.2 = (bf16[1536,768]{1,0:T(8,128)(2,1)}, bf16[1536,768]{1,0:T(8,128)(2,1)S(1)}, u32[]{:S(2)}, u32[]{:S(2)}) collective-permute-start(bf16[1536,768]{1,0:T(8,128)(2,1)} %get-tuple-element.111), channel_id=1, source_target_pairs={{0,2},{1,3},{2,0},{3,1},{4,6},{5,7},{6,4},{7,5},{8,10},{9,11},{10,... | collective-permute-start | bytes 7077896 | tf_op jit(solution)/shard_map/ppermute | solution.py:347
  38.3 18.2 %collective-permute-start.10 = (bf16[1536,768]{1,0:T(8,128)(2,1)}, bf16[1536,768]{1,0:T(8,128)(2,1)S(1)}, u32[]{:S(2)}, u32[]{:S(2)}) collective-permute-start(bf16[1536,768]{1,0:T(8,128)(2,1)} %get-tuple-element.103.after), channel_id=1, source_target_pairs={{0,2},{1,3},{2,0},{3,1},{4,6},{5,7},{6,4},{7,5},{8,10},{9,11},{10,... | collective-permute-start | bytes 7077896 | tf_op jit(solution)/shard_map/ppermute | solution.py:347
  54.3 4.8 %collective-permute-start.18 = (bf16[1552,768]{1,0:T(8,128)(2,1)}, bf16[1552,768]{1,0:T(8,128)(2,1)S(1)}, u32[]{:S(2)}, u32[]{:S(2)}) collective-permute-start(bf16[1552,768]{1,0:T(8,128)(2,1)} %get-tuple-element.118), channel_id=1, source_target_pairs={{0,2},{1,3},{2,0},{3,1},{4,6},{5,7},{6,4},{7,5},{8,10},{9,11},{10,... | collective-permute-start | bytes 7151624 | tf_op jit(solution)/shard_map/ppermute | solution.py:347
  54.7 24.4 %collective-permute-start.3 = (bf16[768,768]{1,0:T(8,128)(2,1)S(1)}, bf16[768,768]{1,0:T(8,128)(2,1)S(1)}, u32[]{:S(2)}, u32[]{:S(2)}) collective-permute-start(bf16[768,768]{1,0:T(8,128)(2,1)S(1)} %get-tuple-element.175), channel_id=1, source_target_pairs={{0,1},{1,0},{2,10},{3,11},{4,5},{5,4},{6,14},{7,15},{8,9},{9,8},{1... | collective-permute-start | bytes 3538952 | tf_op jit(solution)/shard_map/ppermute | solution.py:347
  56.8 26.3 %collective-permute-start.11 = (bf16[768,768]{1,0:T(8,128)(2,1)S(1)}, bf16[768,768]{1,0:T(8,128)(2,1)S(1)}, u32[]{:S(2)}, u32[]{:S(2)}) collective-permute-start(bf16[768,768]{1,0:T(8,128)(2,1)S(1)} %get-tuple-element.173), channel_id=1, source_target_pairs={{0,8},{1,9},{2,6},{3,7},{4,12},{5,13},{6,2},{7,3},{8,0},{9,1},{10,... | collective-permute-start | bytes 3538952 | tf_op jit(solution)/shard_map/ppermute | solution.py:347
  60.0 25.2 %collective-permute-start.19 = (bf16[784,768]{1,0:T(8,128)(2,1)S(1)}, bf16[784,768]{1,0:T(8,128)(2,1)S(1)}, u32[]{:S(2)}, u32[]{:S(2)}) collective-permute-start(bf16[784,768]{1,0:T(8,128)(2,1)S(1)} %pad_maximum_fusion), channel_id=1, source_target_pairs={{0,4},{1,5},{2,3},{3,2},{4,0},{5,1},{6,7},{7,6},{8,12},{9,13},{10,... | collective-permute-start | bytes 3612680 | tf_op jit(solution)/shard_map/ppermute | solution.py:347
  64.0 29.3 %collective-permute-start.1 = (bf16[256,768]{1,0:T(8,128)(2,1)S(1)}, bf16[256,768]{1,0:T(8,128)(2,1)S(1)}, u32[]{:S(2)}, u32[]{:S(2)}) collective-permute-start(bf16[256,768]{1,0:T(8,128)(2,1)S(1)} %get-tuple-element.142.refs_10_), channel_id=1, source_target_pairs={{0,1},{1,0},{2,3},{3,2},{4,5},{5,4},{6,7},{7,6},{8,9},{9,8},{10,11... | collective-permute-start | bytes 1179656 | tf_op jit(solution)/shard_map/ppermute | solution.py:525
  79.2 12.4 %collective-permute-start.4 = (bf16[384,768]{1,0:T(8,128)(2,1)S(1)}, bf16[384,768]{1,0:T(8,128)(2,1)S(1)}, u32[]{:S(2)}, u32[]{:S(2)}) collective-permute-start(bf16[384,768]{1,0:T(8,128)(2,1)S(1)} %get-tuple-element.181), channel_id=1, source_target_pairs={{0,4},{1,5},{2,3},{3,2},{4,0},{5,1},{6,7},{7,6},{8,12},{9,13},{10,... | collective-permute-start | bytes 1769480 | tf_op jit(solution)/shard_map/ppermute | solution.py:347
  83.3 16.9 %collective-permute-start.12 = (bf16[384,768]{1,0:T(8,128)(2,1)S(1)}, bf16[384,768]{1,0:T(8,128)(2,1)S(1)}, u32[]{:S(2)}, u32[]{:S(2)}) collective-permute-start(bf16[384,768]{1,0:T(8,128)(2,1)S(1)} %get-tuple-element.178), channel_id=1, source_target_pairs={{0,1},{1,0},{2,10},{3,11},{4,5},{5,4},{6,14},{7,15},{8,9},{9,8},{1... | collective-permute-start | bytes 1769480 | tf_op jit(solution)/shard_map/ppermute | solution.py:347
  85.5 19.2 %collective-permute-start.20 = (bf16[400,768]{1,0:T(8,128)(2,1)S(1)}, bf16[400,768]{1,0:T(8,128)(2,1)S(1)}, u32[]{:S(2)}, u32[]{:S(2)}) collective-permute-start(bf16[400,768]{1,0:T(8,128)(2,1)S(1)} %pad_maximum_fusion.3), channel_id=1, source_target_pairs={{0,8},{1,9},{2,6},{3,7},{4,12},{5,13},{6,2},{7,3},{8,0},{9,1},{10,... | collective-permute-start | bytes 1843208 | tf_op jit(solution)/shard_map/ppermute | solution.py:347
  91.6 10.4 %collective-permute-start.5 = (bf16[192,768]{1,0:T(8,128)(2,1)S(1)}, bf16[192,768]{1,0:T(8,128)(2,1)S(1)}, u32[]{:S(2)}, u32[]{:S(2)}) collective-permute-start(bf16[192,768]{1,0:T(8,128)(2,1)S(1)} %slice_add_fusion.15), channel_id=1, source_target_pairs={{0,8},{1,9},{2,6},{3,7},{4,12},{5,13},{6,2},{7,3},{8,0},{9,1},{10,... | collective-permute-start | bytes 884744 | tf_op jit(solution)/shard_map/ppermute | solution.py:347
  100.2 15.1 %collective-permute-start.13 = (bf16[192,768]{1,0:T(8,128)(2,1)S(1)}, bf16[192,768]{1,0:T(8,128)(2,1)S(1)}, u32[]{:S(2)}, u32[]{:S(2)}) collective-permute-start(bf16[192,768]{1,0:T(8,128)(2,1)S(1)} %slice_add_fusion.17), channel_id=1, source_target_pairs={{0,4},{1,5},{2,3},{3,2},{4,0},{5,1},{6,7},{7,6},{8,12},{9,13},{10,... | collective-permute-start | bytes 884744 | tf_op jit(solution)/shard_map/ppermute | solution.py:347
  102.0 10.8 %collective-permute-start.6 = (bf16[192,768]{1,0:T(8,128)(2,1)S(1)}, bf16[192,768]{1,0:T(8,128)(2,1)S(1)}, u32[]{:S(2)}, u32[]{:S(2)}) collective-permute-start(bf16[192,768]{1,0:T(8,128)(2,1)S(1)} %fusion), channel_id=1, source_target_pairs={{0,16},{1,17},{2,18},{3,19},{4,20},{5,21},{6,22},{7,23},{8,24},{9,... | collective-permute-start | bytes 884744 | tf_op jit(solution)/shard_map/ppermute | solution.py:347
  112.9 9.9 %collective-permute-start.7 = (bf16[192,768]{1,0:T(8,128)(2,1)S(1)}, bf16[192,768]{1,0:T(8,128)(2,1)S(1)}, u32[]{:S(2)}, u32[]{:S(2)}) collective-permute-start(bf16[192,768]{1,0:T(8,128)(2,1)S(1)} %add.129), channel_id=1, source_target_pairs={{0,8},{1,9},{2,6},{3,7},{4,12},{5,13},{6,2},{7,3},{8,0},{9,1},{10,... | collective-permute-start | bytes 884744 | tf_op jit(solution)/shard_map/ppermute | solution.py:347
  113.7 9.3 %collective-permute-start.21 = (bf16[208,768]{1,0:T(8,128)(2,1)S(1)}, bf16[208,768]{1,0:T(8,128)(2,1)S(1)}, u32[]{:S(2)}, u32[]{:S(2)}) collective-permute-start(bf16[208,768]{1,0:T(8,128)(2,1)S(1)} %pad_maximum_fusion.7), channel_id=1, source_target_pairs={{0,1},{1,0},{2,10},{3,11},{4,5},{5,4},{6,14},{7,15},{8,9},{9,8},{1... | collective-permute-start | bytes 958472 | tf_op jit(solution)/shard_map/ppermute | solution.py:347
  115.3 12.0 %collective-permute-start.14 = (bf16[192,768]{1,0:T(8,128)(2,1)S(1)}, bf16[192,768]{1,0:T(8,128)(2,1)S(1)}, u32[]{:S(2)}, u32[]{:S(2)}) collective-permute-start(bf16[192,768]{1,0:T(8,128)(2,1)S(1)} %add_add_fusion), channel_id=1, source_target_pairs={{0,16},{1,17},{2,18},{3,19},{4,20},{5,21},{6,22},{7,23},{8,24},{9,... | collective-permute-start | bytes 884744 | tf_op jit(solution)/shard_map/ppermute | solution.py:347
  122.9 13.1 %collective-permute-start.8 = (bf16[384,768]{1,0:T(8,128)(2,1)S(1)}, bf16[384,768]{1,0:T(8,128)(2,1)S(1)}, u32[]{:S(2)}, u32[]{:S(2)}) collective-permute-start(bf16[384,768]{1,0:T(8,128)(2,1)S(1)} %pad_maximum_fusion.4), channel_id=1, source_target_pairs={{0,4},{1,5},{2,3},{3,2},{4,0},{5,1},{6,7},{7,6},{8,12},{9,13},{10,... | collective-permute-start | bytes 1769480 | tf_op jit(solution)/shard_map/ppermute | solution.py:347
  123.1 21.6 %collective-permute-start.22 = (bf16[208,768]{1,0:T(8,128)(2,1)S(1)}, bf16[208,768]{1,0:T(8,128)(2,1)S(1)}, u32[]{:S(2)}, u32[]{:S(2)}) collective-permute-start(bf16[208,768]{1,0:T(8,128)(2,1)S(1)} %pad_maximum_fusion.8), channel_id=1, source_target_pairs={{0,16},{1,17},{2,18},{3,19},{4,20},{5,21},{6,22},{7,23},{8,24},{9,... | collective-permute-start | bytes 958472 | tf_op jit(solution)/shard_map/ppermute | solution.py:347
  127.4 19.2 %collective-permute-start.15 = (bf16[192,768]{1,0:T(8,128)(2,1)S(1)}, bf16[192,768]{1,0:T(8,128)(2,1)S(1)}, u32[]{:S(2)}, u32[]{:S(2)}) collective-permute-start(bf16[192,768]{1,0:T(8,128)(2,1)S(1)} %add.137), channel_id=1, source_target_pairs={{0,4},{1,5},{2,3},{3,2},{4,0},{5,1},{6,7},{7,6},{8,12},{9,13},{10,... | collective-permute-start | bytes 884744 | tf_op jit(solution)/shard_map/ppermute | solution.py:347
  136.9 31.5 %collective-permute-start.26 = (bf16[768,768]{1,0:T(8,128)(2,1)}, bf16[768,768]{1,0:T(8,128)(2,1)S(1)}, u32[]{:S(2)}, u32[]{:S(2)}) collective-permute-start(bf16[768,768]{1,0:T(8,128)(2,1)} %constant_dynamic-update-slice_fusion.refs_0_), channel_id=1, source_target_pairs={{0,2},{1,3},{2,0},{3,1},{4,6},{5,7},{6,4},{7,5},{8,10},{9,11},{10,... | collective-permute-start | bytes 3538952 | tf_op jit(solution)/shard_map/ppermute | solution.py:347
  144.8 6.8 %collective-permute-start.23 = (bf16[192,768]{1,0:T(8,128)(2,1)S(1)}, bf16[192,768]{1,0:T(8,128)(2,1)S(1)}, u32[]{:S(2)}, u32[]{:S(2)}) collective-permute-start(bf16[192,768]{1,0:T(8,128)(2,1)S(1)} %slice.247), channel_id=1, source_target_pairs={{0,1},{1,0},{2,10},{3,11},{4,5},{5,4},{6,14},{7,15},{8,9},{9,8},{1... | collective-permute-start | bytes 884744 | tf_op jit(solution)/shard_map/ppermute | solution.py:347
  146.7 11.3 %collective-permute-start.16 = (bf16[384,768]{1,0:T(8,128)(2,1)S(1)}, bf16[384,768]{1,0:T(8,128)(2,1)S(1)}, u32[]{:S(2)}, u32[]{:S(2)}) collective-permute-start(bf16[384,768]{1,0:T(8,128)(2,1)S(1)} %pad_maximum_fusion.5), channel_id=1, source_target_pairs={{0,1},{1,0},{2,10},{3,11},{4,5},{5,4},{6,14},{7,15},{8,9},{9,8},{1... | collective-permute-start | bytes 1769480 | tf_op jit(solution)/shard_map/ppermute | solution.py:347
  151.6 14.5 %collective-permute-start.24 = (bf16[384,768]{1,0:T(8,128)(2,1)S(1)}, bf16[384,768]{1,0:T(8,128)(2,1)S(1)}, u32[]{:S(2)}, u32[]{:S(2)}) collective-permute-start(bf16[384,768]{1,0:T(8,128)(2,1)S(1)} %pad_maximum_fusion.6), channel_id=1, source_target_pairs={{0,8},{1,9},{2,6},{3,7},{4,12},{5,13},{6,2},{7,3},{8,0},{9,1},{10,... | collective-permute-start | bytes 1769480 | tf_op jit(solution)/shard_map/ppermute | solution.py:347
  158.0 16.1 %collective-permute-start.27 = (bf16[768,768]{1,0:T(8,128)(2,1)S(1)}, bf16[768,768]{1,0:T(8,128)(2,1)}, u32[]{:S(2)}, u32[]{:S(2)}) collective-permute-start(bf16[768,768]{1,0:T(8,128)(2,1)S(1)} %pad_maximum_fusion.1.refs_2_), channel_id=1, source_target_pairs={{0,2},{1,3},{2,0},{3,1},{4,6},{5,7},{6,4},{7,5},{8,10},{9,11},{10,... | collective-permute-start | bytes 3538952 | tf_op jit(solution)/shard_map/ppermute | solution.py:347
  166.2 7.9 %collective-permute-start.28 = (bf16[768,768]{1,0:T(8,128)(2,1)S(1)}, bf16[768,768]{1,0:T(8,128)(2,1)}, u32[]{:S(2)}, u32[]{:S(2)}) collective-permute-start(bf16[768,768]{1,0:T(8,128)(2,1)S(1)} %pad_maximum_fusion.2.refs_4_), channel_id=1, source_target_pairs={{0,2},{1,3},{2,0},{3,1},{4,6},{5,7},{6,4},{7,5},{8,10},{9,11},{10,... | collective-permute-start | bytes 3538952 | tf_op jit(solution)/shard_map/ppermute | solution.py:347
  166.3 26.7 %collective-permute-start.9 = (bf16[768,768]{1,0:T(8,128)(2,1)}, bf16[768,768]{1,0:T(8,128)(2,1)}, u32[]{:S(2)}, u32[]{:S(2)}) collective-permute-start(bf16[768,768]{1,0:T(8,128)(2,1)} %constant_dynamic-update-slice_fusion.refs_0_), channel_id=1, source_target_pairs={{0,1},{1,0},{2,10},{3,11},{4,5},{5,4},{6,14},{7,15},{8,9},{9,8},{1... | collective-permute-start | bytes 3538952 | tf_op jit(solution)/shard_map/ppermute | solution.py:347
  167.8 27.1 %collective-permute-start.17 = (bf16[768,768]{1,0:T(8,128)(2,1)S(1)}, bf16[768,768]{1,0:T(8,128)(2,1)}, u32[]{:S(2)}, u32[]{:S(2)}) collective-permute-start(bf16[768,768]{1,0:T(8,128)(2,1)S(1)} %pad_maximum_fusion.1.refs_2_), channel_id=1, source_target_pairs={{0,8},{1,9},{2,6},{3,7},{4,12},{5,13},{6,2},{7,3},{8,0},{9,1},{10,... | collective-permute-start | bytes 3538952 | tf_op jit(solution)/shard_map/ppermute | solution.py:347
  169.4 26.1 %collective-permute-start.25 = (bf16[768,768]{1,0:T(8,128)(2,1)S(1)}, bf16[768,768]{1,0:T(8,128)(2,1)}, u32[]{:S(2)}, u32[]{:S(2)}) collective-permute-start(bf16[768,768]{1,0:T(8,128)(2,1)S(1)} %pad_maximum_fusion.2.refs_4_), channel_id=1, source_target_pairs={{0,4},{1,5},{2,3},{3,2},{4,0},{5,1},{6,7},{7,6},{8,12},{9,13},{10,... | collective-permute-start | bytes 3538952 | tf_op jit(solution)/shard_map/ppermute | solution.py:347
  195.5 5.7 %collective-permute-start.29 = (bf16[768,768]{1,0:T(8,128)(2,1)}, bf16[768,768]{1,0:T(8,128)(2,1)S(1)}, u32[]{:S(2)}, u32[]{:S(2)}) collective-permute-start(bf16[768,768]{1,0:T(8,128)(2,1)} %collective-permute-done.9.refs_0_), channel_id=1, source_target_pairs={{0,2},{1,3},{2,0},{3,1},{4,6},{5,7},{6,4},{7,5},{8,10},{9,11},{10,... | collective-permute-start | bytes 3538952 | tf_op jit(solution)/shard_map/ppermute | solution.py:347
  195.6 5.6 %collective-permute-start.30 = (bf16[768,768]{1,0:T(8,128)(2,1)}, bf16[768,768]{1,0:T(8,128)(2,1)S(1)}, u32[]{:S(2)}, u32[]{:S(2)}) collective-permute-start(bf16[768,768]{1,0:T(8,128)(2,1)} %collective-permute-done.17.refs_1_), channel_id=1, source_target_pairs={{0,2},{1,3},{2,0},{3,1},{4,6},{5,7},{6,4},{7,5},{8,10},{9,11},{10,... | collective-permute-start | bytes 3538952 | tf_op jit(solution)/shard_map/ppermute | solution.py:347
  196.0 5.9 %collective-permute-start.31 = (bf16[768,768]{1,0:T(8,128)(2,1)}, bf16[768,768]{1,0:T(8,128)(2,1)S(1)}, u32[]{:S(2)}, u32[]{:S(2)}) collective-permute-start(bf16[768,768]{1,0:T(8,128)(2,1)} %collective-permute-done.25.refs_2_), channel_id=1, source_target_pairs={{0,2},{1,3},{2,0},{3,1},{4,6},{5,7},{6,4},{7,5},{8,10},{9,11},{10,... | collective-permute-start | bytes 3538952 | tf_op jit(solution)/shard_map/ppermute | solution.py:347
  (17 other events, 166.7 us)
